TPU v7x, 512 devices: a whole 4x8x8 slice. The times are simulated.
512 devices in a mesh: rows: 512 (over x, z, y, core).
Axes of the slice: x: 4, y: 8, z: 8, core: 2. Of those that a mesh axis runs over, the one named last changes fastest.
Arguments:
- features: float32 [262144, 256], P('rows'), may hold values from -6 to 6
- adjacency: float32 [1024, 6, 256, 256], P('rows'), may hold values from -0.25 to 0.25
- block_index: int32 [1024, 6], P('rows'), may hold values from 0 to 1023, as said below
- block_counts: int32 [1024], P('rows'), may hold values from 1 to 6, as said below
- labels: int32 [262144], P('rows'), may hold values from 0 to 127
- weight_in: float32 [256, 512], replicated, may hold values from -0.375 to 0.375
- weight_out: float32 [512, 128], replicated, may hold values from -0.25 to 0.25
Outputs:
- logits: float32 [262144, 128], P('rows')
- mean_loss: float32 [], replicated
- hidden_grad: float32 [262144, 512], P('rows')
- grad_in: float32 [256, 512], replicated
- grad_out: float32 [512, 128], replicated
Inputs may be any that keep to these rules, and one draw needn't show every extreme that they name: `block_index`: row block b lies on device b // 2; every slot's column block lies at most 2 row blocks away from b, inside the graph. `block_counts`: some row block uses all 6 slots.
All inputs are finite; a program needn't handle non-finite values.
Results may differ from a plain program's by a relative error of at most 0.00011.
Values sent between devices are 32-bit elements; how exact they have to be, the bound alone decides.
No kernel may reach another device: no remote copies, remote signals or barrier semaphores. Data moves between devices by JAX's collectives and lax.ppermute only.
A program may use at most 64 MiB of HBM per device.

v0:
```python
import jax
import jax.numpy as jnp
from jax import lax
from jax.sharding import PartitionSpec as P

REACH = 2


HIGH = lax.Precision.HIGHEST


def extended(block, sides, width):
    for axis, dim in sides:
        count = lax.axis_size(axis)
        forward = [(i, i + 1) for i in range(count - 1)]
        backward = [(target, source) for source, target in forward]
        low = lax.ppermute(
            lax.slice_in_dim(block, block.shape[dim] - width, None, axis=dim), axis, forward
        )
        high = lax.ppermute(lax.slice_in_dim(block, 0, width, axis=dim), axis, backward)
        block = jnp.concatenate([low, block, high], axis=dim)
    return block


def shifted(value, axis, steps):
    count = lax.axis_size(axis)
    first, last = (max(0, -steps), min(count, count - steps))
    return lax.ppermute(value, axis, [(source, source + steps) for source in range(first, last)])


def activate(values):
    return jax.nn.gelu(values, approximate=False)


def propagate(values, masked, relative):
    blocks_here = masked.shape[0]
    block_rows = masked.shape[2]
    width = values.shape[1]
    grouped = values.reshape(blocks_here, block_rows, width)
    nearby = extended(grouped, (("rows", 0),), REACH)
    picked = nearby[relative]
    result = jnp.einsum("bkij,bkjw->biw", masked, picked, precision=HIGH)
    return result.reshape(-1, width)


def transposed(grads, masked, relative):
    blocks_here, slot_total, block_rows = (masked.shape[0], masked.shape[1], masked.shape[2])
    width = grads.shape[1]
    terms = jnp.einsum(
        "bkij,biw->bkjw", masked, grads.reshape(blocks_here, block_rows, width), precision=HIGH
    )
    buckets_total = blocks_here + 2 * REACH
    selector = (
        relative.reshape(-1)[:, None] == jnp.arange(buckets_total, dtype=jnp.int32)[None, :]
    ).astype(jnp.float32)
    buckets = jnp.einsum(
        "ns,njw->sjw",
        selector,
        terms.reshape(blocks_here * slot_total, block_rows, width),
        precision=HIGH,
    )
    gathered = buckets[REACH : REACH + blocks_here]
    for heading in (1, -1):
        if heading == 1:
            outgoing = buckets[REACH + blocks_here :]
        else:
            outgoing = buckets[:REACH]
        arrived = shifted(outgoing, "rows", heading)
        if heading == 1:
            padded = arrived
        else:
            padded = arrived
        gathered = gathered + padded
    return gathered.reshape(-1, width)


def per_device(features, adjacency, block_index, block_counts, labels, weight_in, weight_out):
    blocks_here = adjacency.shape[0]
    slot_total = adjacency.shape[1]
    device_pos = lax.axis_index("rows")
    relative = block_index - (device_pos * blocks_here - REACH)
    usable = jnp.arange(slot_total, dtype=jnp.int32)[None, :] < block_counts[:, None]
    masked = jnp.where(usable[:, :, None, None], adjacency, jnp.zeros_like(adjacency))
    spread_in = propagate(features, masked, relative)
    pre_hidden = jnp.dot(spread_in, weight_in, precision=HIGH)
    hidden = activate(pre_hidden)
    spread_hidden = propagate(hidden, masked, relative)
    logits = jnp.dot(spread_hidden, weight_out, precision=HIGH)
    totals = jnp.log(jnp.sum(jnp.exp(logits), axis=1))
    onehot = (labels[:, None] == jnp.arange(logits.shape[1], dtype=jnp.int32)[None, :]).astype(
        jnp.float32
    )
    row_loss = totals - jnp.sum(onehot * logits, axis=1)
    loss_part = jnp.sum(row_loss)
    logit_grad = jnp.exp(logits - totals[:, None]) - onehot
    returned = transposed(logit_grad, masked, relative)
    grad_out = jnp.dot(spread_hidden.T, logit_grad, precision=HIGH)
    hidden_grad = jnp.dot(returned, weight_out.T, precision=HIGH)
    _, back = jax.vjp(activate, pre_hidden)
    pre_grad = back(hidden_grad)[0]
    grad_in = jnp.dot(spread_in.T, pre_grad, precision=HIGH)
    loss_total, grad_in, grad_out = lax.psum((loss_part, grad_in, grad_out), "rows")
    mean_loss = loss_total / (features.shape[0] * lax.axis_size("rows"))
    return (logits, mean_loss, hidden_grad, grad_in, grad_out)


def solution(mesh):
    in_specs = (
        P("rows", None),
        P("rows", None, None, None),
        P("rows", None),
        P("rows"),
        P("rows"),
        P(),
        P(),
    )
    out_specs = (P("rows", None), P(), P("rows", None), P(), P())
    return jax.shard_map(
        per_device, mesh=mesh, in_specs=in_specs, out_specs=out_specs, check_vma=False
    )
```

profile of v0, /device:TPU:1, one launch (start us, length us, event | category | flops | bytes accessed | tf_op | source)
XLA Modules:
  0.0 400.5 jit_solution(16890459852708432927)
XLA Ops:
  7.2 0.0 copy-start
  7.2 0.0 all-reduce.3.cloned.1.call-start
  7.2 8.9 %collective-permute-start.1 = (f32[2,256,256]{2,1,0:T(8,128)}, f32[2,256,256]{2,1,0:T(8,128)S(1)}, u32[]{:S(2)}, u32[]{:S(2)}) collective-permute-start(f32[2,256,256]{2,1,0:T(8,128)} %bitcast.46), channel_id=1, source_target_pairs={{1,0},{2,1},{3,2},{4,3},{5,4},{6,5},{7,6},{8,7},{9,8},{10,9},{11,1... | collective-permute-start | bytes 1572872 | tf_op jit(solution)/shard_map/ppermute | solution.py:20
  16.2 1.9 collective-permute-start
  18.1 0.7 compare_select_fusion
  18.8 0.1 reshape.66
  18.9 0.7 iota_compare_fusion.2
  19.6 0.0 collective-permute-done.1
  19.6 4.9 %collective-permute-done = f32[2,256,256]{2,1,0:T(8,128)S(1)} collective-permute-done((f32[2,256,256]{2,1,0:T(8,128)}, f32[2,256,256]{2,1,0:T(8,128)S(1)}, u32[]{:S(2)}, u32[]{:S(2)}) %collective-permute-start) | collective-permute-done | bytes 524320 | tf_op jit(solution)/shard_map/ppermute | solution.py:17
  24.5 1.2 pad_maximum_fusion.1
  25.7 2.4 gather_fusion
  28.1 6.0 %fusion.4 = f32[2,256,256,1]{2,1,3,0:T(8,128)S(1)} fusion(f32[2,6,256,256]{3,2,1,0:T(8,128)} %bitcast.35, f32[2,6,256,256]{3,2,1,0:T(8,128)} %param.8, pred[2,6]{1,0:T(4,128)(4,1)S(1)} %iota_compare_fusion.2), kind=kOutput, calls=%fused_computation.7 | convolution fusion | flops 2416705536 | bytes 6815756 | tf_op jit(solution)/shard_map/bkij,bkjw->biw/dot_general | solution.py:42
  34.0 0.0 copy-done
  34.1 6.7 %multiply_multiply_fusion.5 = (f32[512,512]{1,0:T(8,128)S(1)}, f32[512,512]{1,0:T(8,128)}, f32[512,512]{1,0:T(8,128)}) fusion(f32[512,256]{1,0:T(8,128)S(1)} %bitcast.44, f32[256,512]{1,0:T(8,128)S(1)} %copy-done), kind=kOutput, calls=%fused_computation.44 | convolution fusion | flops 822083584 | bytes 4194304 | tf_op jit(solution)/shard_map/dot_general | solution.py:85
  40.8 1.9 collective-permute-start.3
  42.7 4.3 %collective-permute-start.2 = (f32[2,256,512]{2,1,0:T(8,128)S(1)}, f32[2,256,512]{2,1,0:T(8,128)}, u32[]{:S(2)}, u32[]{:S(2)}) collective-permute-start(f32[2,256,512]{2,1,0:T(8,128)S(1)} %bitcast.42), channel_id=1, source_target_pairs={{0,1},{1,2},{2,3},{3,4},{4,5},{5,6},{6,7},{7,8},{8,9},{9,10},{10,1... | collective-permute-start | bytes 3145736 | tf_op jit(solution)/shard_map/ppermute | solution.py:17
  47.0 0.1 eq.31
  47.1 10.5 %collective-permute-done.3 = f32[2,256,512]{2,1,0:T(8,128)S(1)} collective-permute-done((f32[2,256,512]{2,1,0:T(8,128)S(1)}, f32[2,256,512]{2,1,0:T(8,128)S(1)}, u32[]{:S(2)}, u32[]{:S(2)}) %collective-permute-start.3) | collective-permute-done | bytes 1048608 | tf_op jit(solution)/shard_map/ppermute | solution.py:20
  57.5 1.2 collective-permute-done.2
  58.7 3.3 pad_maximum_fusion
  62.1 5.5 %gather_fusion.1 = f32[12,256,512]{2,1,0:T(8,128)} fusion(f32[6,256,512]{2,1,0:T(8,128)} %pad_maximum_fusion, s32[1024]{0:T(1024)S(1)} %pad_clamp_fusion), kind=kCustom, calls=%fused_computation.1 | custom fusion | bytes 12582960 | tf_op jit(solution)/shard_map/gather | solution.py:41
  67.6 0.0 copy-start.4
  67.6 0.0 copy-start.5
  67.6 0.0 copy-start.1
  67.6 9.6 %fusion.2 = f32[2,256,512,1]{2,1,3,0:T(8,128)S(1)} fusion(f32[2,6,256,512]{3,2,1,0:T(8,128)} %bitcast.34, f32[2,6,256,256]{3,2,1,0:T(8,128)} %param.8, pred[2,6]{1,0:T(4,128)(4,1)S(1)} %iota_compare_fusion.2), kind=kOutput, calls=%fused_computation.5 | convolution fusion | flops 4832624640 | bytes 10485772 | tf_op jit(solution)/shard_map/bkij,bkjw->biw/dot_general | solution.py:42
  77.2 0.0 copy-done.4
  77.2 0.0 copy-done.5
  77.2 1.1 exponential_reduce_fusion
  78.3 0.0 copy-start.3
  78.3 0.6 fusion.46
  78.9 0.2 convert_subtract_fusion
  79.1 0.0 copy-done.1
  79.1 5.2 %fusion = f32[2,6,256,128]{3,2,1,0:T(8,128)S(1)} fusion(f32[2,256,128,1]{2,1,3,0:T(8,128)S(1)} %bitcast.39, f32[2,6,256,256]{3,2,1,0:T(8,128)S(1)} %copy-done.1, pred[2,6]{1,0:T(4,128)(4,1)S(1)} %iota_compare_fusion.2), kind=kOutput, calls=%fused_computation.3 | convolution fusion | flops 1208745984 | bytes 4980748 | tf_op jit(solution)/shard_map/bkij,biw->bkjw/dot_general | solution.py:49
  84.4 1.7 fusion.6
  86.0 0.0 copy-done.3
  86.1 0.0 copy-start.6
  86.1 0.0 copy-start.7
  86.1 0.2 fusion.45
  86.3 4.6 %collective-permute-start.4 = (f32[2,256,128]{2,0,1:T(2,128)S(1)}, f32[2,256,128]{2,0,1:T(2,128)S(1)}, u32[]{:S(2)}, u32[]{:S(2)}) collective-permute-start(f32[2,256,128]{2,0,1:T(2,128)S(1)} %get-tuple-element.13), channel_id=1, source_target_pairs={{0,1},{1,2},{2,3},{3,4},{4,5},{5,6},{6,7},{7,8},{8,9},{9,10},{10,1... | collective-permute-start | bytes 786440 | tf_op jit(solution)/shard_map/ppermute | solution.py:28
  90.9 2.1 collective-permute-start.5
  93.1 2.5 fusion.48
  95.6 0.0 collective-permute-done.4
  95.6 3.0 collective-permute-done.5
  98.6 0.2 fusion.34
  98.9 1.0 fusion.47
  99.9 0.0 copy-start.2
  99.9 0.0 copy-done.6
  99.9 0.0 copy-done.7
  99.9 2.3 fusion.15
  102.2 0.0 all-reduce.3.cloned.1.call-update
  102.2 117.9 %psum.21 = f32[]{:T(128)} all-reduce(f32[]{:T(128)} %get-tuple-element.16), channel_id=1, replica_groups=mesh['rows'=512] {'rows'}, use_global_device_ids=true, to_apply=%region_3.4 | all-reduce | flops 1 | bytes 8 | tf_op jit(solution)/shard_map/psum | solution.py:102
  220.7 168.3 %all-reduce.3.cloned.1.call-done = (f32[256,512]{1,0:T(8,128)}, f32[512,128]{1,0:T(8,128)}) async-done(((f32[256,512]{1,0:T(8,128)}, f32[512,128]{1,0:T(8,128)}), (f32[256,512]{1,0:T(8,128)}, f32[512,128]{1,0:T(8,128)})) %all-reduce.3.cloned.1.call-update) | async-done | bytes 786448 | tf_op jit(solution)/shard_map/psum | solution.py:102
  389.0 1.9 copy.25
  390.9 0.0 copy-done.2
  390.9 1.7 copy.26
  (2 shorter events, 0.0 us)
Async XLA Ops:
  7.2 26.9 %copy-start = (f32[256,512]{1,0:T(8,128)S(1)}, f32[256,512]{1,0:T(8,128)}, u32[]{:S(2)}) copy-start(f32[256,512]{1,0:T(8,128)} %param.12) | copy-start | bytes 1572868
  7.2 381.8 %all-reduce.3.cloned.1.call-start = ((), (), s32[]{:S(2)}) async-start(), calls=%async_computation | async-start | bytes 1572864 | tf_op jit(solution)/shard_map/psum | solution.py:102
  7.2 12.4 %collective-permute-start.1 = (f32[2,256,256]{2,1,0:T(8,128)}, f32[2,256,256]{2,1,0:T(8,128)S(1)}, u32[]{:S(2)}, u32[]{:S(2)}) collective-permute-start(f32[2,256,256]{2,1,0:T(8,128)} %bitcast.46), channel_id=1, source_target_pairs={{1,0},{2,1},{3,2},{4,3},{5,4},{6,5},{7,6},{8,7},{9,8},{10,9},{11,1... | collective-permute-start | bytes 1572872 | tf_op jit(solution)/shard_map/ppermute | solution.py:20
  16.2 8.3 %collective-permute-start = (f32[2,256,256]{2,1,0:T(8,128)}, f32[2,256,256]{2,1,0:T(8,128)S(1)}, u32[]{:S(2)}, u32[]{:S(2)}) collective-permute-start(f32[2,256,256]{2,1,0:T(8,128)} %bitcast.47), channel_id=1, source_target_pairs={{0,1},{1,2},{2,3},{3,4},{4,5},{5,6},{6,7},{7,8},{8,9},{9,10},{10,1... | collective-permute-start | bytes 1572872 | tf_op jit(solution)/shard_map/ppermute | solution.py:17
  40.8 16.7 %collective-permute-start.3 = (f32[2,256,512]{2,1,0:T(8,128)S(1)}, f32[2,256,512]{2,1,0:T(8,128)S(1)}, u32[]{:S(2)}, u32[]{:S(2)}) collective-permute-start(f32[2,256,512]{2,1,0:T(8,128)S(1)} %bitcast.41), channel_id=1, source_target_pairs={{1,0},{2,1},{3,2},{4,3},{5,4},{6,5},{7,6},{8,7},{9,8},{10,9},{11,1... | collective-permute-start | bytes 3145736 | tf_op jit(solution)/shard_map/ppermute | solution.py:20
  42.7 16.0 %collective-permute-start.2 = (f32[2,256,512]{2,1,0:T(8,128)S(1)}, f32[2,256,512]{2,1,0:T(8,128)}, u32[]{:S(2)}, u32[]{:S(2)}) collective-permute-start(f32[2,256,512]{2,1,0:T(8,128)S(1)} %bitcast.42), channel_id=1, source_target_pairs={{0,1},{1,2},{2,3},{3,4},{4,5},{5,6},{6,7},{7,8},{8,9},{9,10},{10,1... | collective-permute-start | bytes 3145736 | tf_op jit(solution)/shard_map/ppermute | solution.py:17
  67.6 9.6 %copy-start.4 = (f32[512,128]{1,0:T(8,128)S(1)}, f32[512,128]{1,0:T(8,128)}, u32[]{:S(2)}) copy-start(f32[512,128]{1,0:T(8,128)} %param.13) | copy-start | bytes 786436
  67.6 9.6 %copy-start.5 = (s32[512]{0:T(512)S(1)}, s32[512]{0:T(512)}, u32[]{:S(2)}) copy-start(s32[512]{0:T(512)} %param.11) | copy-start | bytes 6148
  67.6 11.6 %copy-start.1 = (f32[2,6,256,256]{3,2,1,0:T(8,128)S(1)}, f32[2,6,256,256]{3,2,1,0:T(8,128)}, u32[]{:S(2)}) copy-start(f32[2,6,256,256]{3,2,1,0:T(8,128)} %param.8) | copy-start | bytes 9437188
  78.3 7.7 %copy-start.3 = (f32[512,128]{1,0:T(8,128)}, f32[512,128]{1,0:T(8,128)S(1)}, u32[]{:S(2)}) copy-start(f32[512,128]{1,0:T(8,128)S(1)} %get-tuple-element.19) | copy-start | bytes 786436
  86.1 13.8 %copy-start.6 = (f32[512,512]{1,0:T(8,128)S(1)}, f32[512,512]{1,0:T(8,128)}, u32[]{:S(2)}) copy-start(f32[512,512]{1,0:T(8,128)} %get-tuple-element.10) | copy-start | bytes 3145732
  86.1 13.8 %copy-start.7 = (f32[512,512]{1,0:T(8,128)S(1)}, f32[512,512]{1,0:T(8,128)}, u32[]{:S(2)}) copy-start(f32[512,512]{1,0:T(8,128)} %get-tuple-element.17) | copy-start | bytes 3145732
  86.3 9.3 %collective-permute-start.4 = (f32[2,256,128]{2,0,1:T(2,128)S(1)}, f32[2,256,128]{2,0,1:T(2,128)S(1)}, u32[]{:S(2)}, u32[]{:S(2)}) collective-permute-start(f32[2,256,128]{2,0,1:T(2,128)S(1)} %get-tuple-element.13), channel_id=1, source_target_pairs={{0,1},{1,2},{2,3},{3,4},{4,5},{5,6},{6,7},{7,8},{8,9},{9,10},{10,1... | collective-permute-start | bytes 786440 | tf_op jit(solution)/shard_map/ppermute | solution.py:28
  90.9 7.7 %collective-permute-start.5 = (f32[2,256,128]{2,0,1:T(2,128)S(1)}, f32[2,256,128]{2,0,1:T(2,128)S(1)}, u32[]{:S(2)}, u32[]{:S(2)}) collective-permute-start(f32[2,256,128]{2,0,1:T(2,128)S(1)} %get-tuple-element.14), channel_id=1, source_target_pairs={{1,0},{2,1},{3,2},{4,3},{5,4},{6,5},{7,6},{8,7},{9,8},{10,9},{11,1... | collective-permute-start | bytes 786440 | tf_op jit(solution)/shard_map/ppermute | solution.py:28
  99.9 291.0 %copy-start.2 = (f32[512,512]{1,0:T(8,128)}, f32[512,512]{1,0:T(8,128)S(1)}, u32[]{:S(2)}) copy-start(f32[512,512]{1,0:T(8,128)S(1)} %fusion.47) | copy-start | bytes 3145732
Sparse Core Ops, SparseCore 0:
  102.3 286.6 all-reduce.2
where the time goes:
time: 401 us
  waiting for transfers between devices  188 us (47%)
  blocking collectives  118 us (29%)
  matrix products  36 us (9%)
  starting transfers between devices  23.8 us (6%)
  between operations  16 us (4%)
  local copies, waits for them, and re-layouts  11.9 us (3%)
  other arithmetic  6.99 us (2%)
    psum x1, waiting for transfers between devices, per_device(): lax.psum((loss_part, grad_in, grad_out), 'rows')  168 us
    psum x1, blocking collectives, per_device(): lax.psum((loss_part, grad_in, grad_out), 'rows')  118 us
    dot_general x2, matrix products, propagate(): result = jnp.einsum('bkij,bkjw->biw', masked, picked, precision=HIGH)  15.6 us
    ppermute x2, starting transfers between devices, extended(): lax.ppermute(lax.slice_in_dim(block, 0, width, axis=dim), axis, backward)  10.8 us
    ppermute x2, waiting for transfers between devices, extended(): lax.ppermute(lax.slice_in_dim(block, 0, width, axis=dim), axis, backward)  10.5 us
  transfers between devices with their start and end apart: 7, of which 5 were waited for; matrix products, arithmetic and copies ran while one was open for 1% of the time, Pallas kernels for 0%

commit v1 on v0

v1 whole, which is shorter than its diff:
```python
import jax
import jax.numpy as jnp
from jax import lax
from jax.sharding import Mesh, PartitionSpec as P

HIGH = lax.Precision.HIGH
ALL = ("x", "z", "y", "c")
BIG = ("x", "y")
MID = ("z",)


def activate(values):
    return jax.nn.gelu(values, approximate=False)


def dot(a, b, dims):
    return lax.dot_general(a, b, (dims, ((), ())), precision=HIGH)


def mate(value, devices):
    return lax.ppermute(value, ALL, [(i, i ^ 1) for i in range(devices)])


def beside(value, devices):
    pairs = [(i, i + 1) for i in range(1, devices - 1, 2)]
    return lax.ppermute(value, ALL, pairs + [(b, a) for a, b in pairs])


def exchange(value, axes):
    return lax.all_to_all(value, axes, 0, 0, tiled=True)


def spread(value, count):
    return jnp.broadcast_to(value[None], (count,) + value.shape)


def per_device(features, adjacency, block_index, block_counts, labels, weight_in, weight_out):
    devices = lax.axis_size(ALL)
    core = lax.axis_index("c")
    here, slots, rows = adjacency.shape[:3]
    nodes = here * rows
    classes = weight_out.shape[1]
    near = block_index - lax.axis_index(ALL) * here
    local = (near >= 0) & (near < here)
    right = near >= here
    outside = jnp.where(right, near - here, near + here)
    bucket = jnp.where(local, here + near, outside + jnp.where(right == (core == 0), 0, 2 * here))
    usable = jnp.arange(slots, dtype=jnp.int32)[None, :] < block_counts[:, None]
    feat_e = beside(features, devices)
    feat_i = mate(features, devices)
    pieces = []
    for s in range(3 * here):
        take = usable & (bucket == s)
        pieces.append(jnp.sum(jnp.where(take[:, :, None, None], adjacency, 0.0), axis=1))
    band = jnp.concatenate([p.reshape(nodes, rows) for p in pieces], axis=1)
    spread_in = dot(band, jnp.concatenate([feat_i, features, feat_e], axis=0), ((1,), (0,)))
    pre_hidden = dot(spread_in, weight_in, ((1,), (0,)))
    hidden, back = jax.vjp(activate, pre_hidden)
    scores = dot(hidden, weight_out, ((1,), (0,)))
    scores_e = beside(scores, devices)
    scores_i = mate(scores, devices)
    logits = dot(band, jnp.concatenate([scores_i, scores, scores_e], axis=0), ((1,), (0,)))
    totals = jnp.log(jnp.sum(jnp.exp(logits), axis=1))
    onehot = (labels[:, None] == jnp.arange(classes, dtype=jnp.int32)[None, :]).astype(jnp.float32)
    loss = jnp.sum(totals - jnp.sum(onehot * logits, axis=1))
    logit_grad = jnp.exp(logits - totals[:, None]) - onehot
    returns = dot(band, logit_grad, ((0,), (0,)))
    ret_e = beside(returns[2 * nodes :], devices)
    ret_i = mate(returns[:nodes], devices)
    returned = returns[nodes : 2 * nodes] + ret_e + ret_i
    hidden_grad = dot(returned, weight_out, ((1,), (1,)))
    pre_grad = back(hidden_grad)[0]
    grad_in = dot(spread_in, pre_grad, ((0,), (0,)))
    grad_out = dot(hidden, returned, ((0,), (0,)))
    width = 128
    tiles = grad_in.shape[1] // width
    flat = jnp.concatenate(
        [grad_in[:, t * width : (t + 1) * width] for t in range(tiles)] + [grad_out], axis=0
    )
    half = flat.shape[0] // 2
    keep = jnp.where(core == 0, flat[:half], flat[half:])
    give = jnp.where(core == 0, flat[half:], flat[:half])
    big, mid = lax.axis_size(BIG), lax.axis_size(MID)
    tail = jnp.full((8, width), loss)
    parts = jnp.concatenate([give, tail], axis=0)
    parts = mate(parts, devices)
    shard = half // big
    mine = (keep + parts[:half]).reshape(big, shard, width)
    loss_row = jnp.broadcast_to(tail[:1] + parts[half : half + 1], (big, 1, width))
    summed = jnp.sum(exchange(jnp.concatenate([mine, loss_row], axis=1), BIG), axis=0)
    summed = jnp.sum(exchange(spread(summed, mid), MID), axis=0)
    mean_loss = summed[shard, 0] / (nodes * devices)
    own = exchange(spread(summed[:shard], big), BIG).reshape(half, width)
    other = mate(own, devices)
    low = jnp.where(core == 0, own, other)
    high = jnp.where(core == 0, other, own)
    whole = jnp.concatenate([low, high], axis=0)
    deep = grad_in.shape[0]
    grad_in = jnp.concatenate([whole[t * deep : (t + 1) * deep] for t in range(tiles)], axis=1)
    return (logits, mean_loss, hidden_grad, grad_in, whole[tiles * deep :])


def solution(mesh):
    grid = Mesh(mesh.devices.reshape(4, 8, 8, 2), ALL)
    split = P(ALL)
    return jax.shard_map(
        per_device,
        mesh=grid,
        in_specs=(split, split, split, split, split, P(), P()),
        out_specs=(split, P(), split, P(), P()),
        check_vma=False,
    )
```

time: 401 us -> 134 us (0.33)
  waiting for transfers between devices: 188 us -> 13.9 us
  blocking collectives: 118 us -> 64.3 us
  matrix products: 36 us -> 14 us
  between operations: 16 us -> 2.8 us
  local copies, waits for them, and re-layouts: 11.9 us -> 3.36 us
    psum x1 -> x0, waiting for transfers between devices: 168 us -> none  [per_device(): lax.psum((loss_part, grad_in, grad_out), 'rows')]
    psum x1 -> x0, blocking collectives: 118 us -> none  [per_device(): lax.psum((loss_part, grad_in, grad_out), 'rows')]
    all_to_all x0 -> x3, blocking collectives: none -> 64.3 us  [exchange(): return lax.all_to_all(value, axes, 0, 0, tiled=True)]
    dot_general x9 -> x8, matrix products: 36 us -> 14 us  [dot(): return lax.dot_general(a, b, (dims, ((), ())), precision=HIGH)]
    gather x2 -> x0, local copies, waits for them, and re-layouts: 7.89 us -> none  [propagate(): picked = nearby[relative]]
    ppermute x6 -> x8, waiting for transfers between devices: 19.6 us -> 13.9 us  [the longest x3 12.2 us: beside(): return lax.ppermute(value, ALL, pairs + [(b, a) for a, b in pairs])]
    reduce_sum x0 -> x4, other arithmetic: none -> 4.63 us  [the longest x1 3.96 us: per_device(): jnp.sum(jnp.where(take[:, :, None, None], adjacency, 0.0), axis=1)]
    ppermute x6 -> x8, starting transfers between devices: 23.8 us -> 27.8 us  [the longest x5 22 us: mate(): return lax.ppermute(value, ALL, [(i, i ^ 1) for i in range(devices)])]
  transfers between devices with their start and end apart: 7 -> 8, of which waited for: 5 -> 4; matrix products, arithmetic and copies ran while one was open for 1% -> 5% of each run, Pallas kernels for 0% -> 0%
where the time goes in v1:
time: 134 us
  blocking collectives  64.3 us (48%)
  starting transfers between devices  27.8 us (21%)
  matrix products  14 us (10%)
  waiting for transfers between devices  13.9 us (10%)
  other arithmetic  7.82 us (6%)
  local copies, waits for them, and re-layouts  3.36 us (3%)
  between operations  2.8 us (2%)
    all_to_all x3, blocking collectives, exchange(): return lax.all_to_all(value, axes, 0, 0, tiled=True)  64.3 us
    ppermute x5, starting transfers between devices, mate(): return lax.ppermute(value, ALL, [(i, i ^ 1) for i in range(devices)])  22 us
    dot_general x8, matrix products, dot(): return lax.dot_general(a, b, (dims, ((), ())), precision=HIGH)  14 us
    ppermute x3, waiting for transfers between devices, beside(): return lax.ppermute(value, ALL, pairs + [(b, a) for a, b in pairs])  12.2 us
    ppermute x3, starting transfers between devices, beside(): return lax.ppermute(value, ALL, pairs + [(b, a) for a, b in pairs])  5.76 us
    reduce_sum x1, other arithmetic, per_device(): jnp.sum(jnp.where(take[:, :, None, None], adjacency, 0.0), axis=1)  3.96 us
  transfers between devices with their start and end apart: 8, of which 4 were waited for; matrix products, arithmetic and copies ran while one was open for 5% of the time, Pallas kernels for 0%

profile of v1, /device:TPU:1, one launch (start us, length us, event | category | flops | bytes accessed | tf_op | source)
XLA Modules:
  0.0 134.0 jit_solution(5528660534284696129)
XLA Ops:
  0.6 0.0 copy-start
  0.6 8.9 %collective-permute-start = (f32[512,256]{1,0:T(8,128)}, f32[512,256]{1,0:T(8,128)S(1)}, u32[]{:S(2)}, u32[]{:S(2)}) collective-permute-start(f32[512,256]{1,0:T(8,128)} %param.7), channel_id=1, source_target_pairs={{0,1},{1,0},{2,3},{3,2},{4,5},{5,4},{6,7},{7,6},{8,9},{9,8},{10,11... | collective-permute-start | bytes 1572872 | tf_op jit(solution)/shard_map/ppermute | solution.py:21
  9.6 1.9 %collective-permute-start.1 = (f32[512,256]{1,0:T(8,128)}, f32[512,256]{1,0:T(8,128)S(1)}, u32[]{:S(2)}, u32[]{:S(2)}) collective-permute-start(f32[512,256]{1,0:T(8,128)} %param.7), channel_id=1, source_target_pairs={{1,2},{3,4},{5,6},{7,8},{9,10},{11,12},{13,14},{15,16},{17,18},{19... | collective-permute-start | bytes 1572872 | tf_op jit(solution)/shard_map/ppermute | solution.py:26
  11.5 0.8 compare_and_fusion.1
  12.3 0.7 compare_and_fusion.5
  13.0 4.0 %select_reduce_fusion = (f32[2,256,256]{2,1,0:T(8,128)S(1)}, f32[2,256,256]{2,1,0:T(8,128)S(1)}, f32[2,256,256]{2,1,0:T(8,128)S(1)}, f32[2,256,256]{2,1,0:T(8,12...) fusion(f32[2,6,256,256]{3,2,1,0:T(8,128)} %param.8, pred[2,6]{1,0:T(4,128)(4,1)S(1)} %get-tuple-element.44, ...), kind=kLoop, calls=%fused_computation | loop fusion | flops 8650752 | bytes 6291528 | tf_op jit(solution)/shard_map/reduce_sum | solution.py:54
  17.0 0.0 copy-start.3
  17.0 0.1 constant_dynamic-update-slice_fusion.5
  17.1 0.1 constant_dynamic-update-slice_fusion.4
  17.1 0.1 constant_dynamic-update-slice_fusion.3
  17.2 0.1 constant_dynamic-update-slice_fusion.2
  17.3 0.1 constant_dynamic-update-slice_fusion.1
  17.4 0.1 constant_dynamic-update-slice_fusion
  17.5 0.0 collective-permute-done
  17.5 2.8 %collective-permute-done.1 = f32[512,256]{1,0:T(8,128)S(1)} collective-permute-done((f32[512,256]{1,0:T(8,128)}, f32[512,256]{1,0:T(8,128)S(1)}, u32[]{:S(2)}, u32[]{:S(2)}) %collective-permute-start.1) | collective-permute-done | bytes 524320 | tf_op jit(solution)/shard_map/ppermute | solution.py:26
  20.3 0.0 copy-done.3
  20.3 1.5 %fusion = f32[512,256]{1,0:T(8,128)S(1)} fusion(f32[512,1536]{1,0:T(8,128)S(1)} %constant_dynamic-update-slice_fusion, f32[512,256]{1,0:T(8,128)S(1)} %collective-permute-done.1, f32[512,256]{1,0:T(8,128)S(1)} %copy-done.3, f32[512,256]{1,0:T(8,128)S(1)} %collective-permute-done), kind=kOutput, calls=%fused_computation.6 | convolution fusion | flops 1208745984 | bytes 5242880 | tf_op jit(solution)/shard_map/dot_general | solution.py:17
  21.8 0.0 copy-done
  21.8 0.0 copy-start.2
  21.8 0.0 copy-start.4
  21.8 4.9 %fusion.6 = (f32[512,512]{1,0:T(8,128)S(1)}, f32[512,512]{1,0:T(8,128)S(1)}) fusion(f32[512,256]{1,0:T(8,128)S(1)} %fusion, f32[256,512]{1,0:T(8,128)S(1)} %copy-done), kind=kOutput, calls=%fused_computation.13 | convolution fusion | flops 418906112 | bytes 3145728 | tf_op jit(solution)/shard_map/dot_general | solution.py:17
  26.7 0.0 copy-done.2
  26.7 0.6 fusion.33
  27.3 1.9 %collective-permute-start.2 = (f32[512,128]{1,0:T(8,128)S(1)}, f32[512,128]{1,0:T(8,128)S(1)}, u32[]{:S(2)}, u32[]{:S(2)}) collective-permute-start(f32[512,128]{1,0:T(8,128)S(1)} %fusion.33), channel_id=1, source_target_pairs={{0,1},{1,0},{2,3},{3,2},{4,5},{5,4},{6,7},{7,6},{8,9},{9,8},{10,11... | collective-permute-start | bytes 786440 | tf_op jit(solution)/shard_map/ppermute | solution.py:21
  29.2 1.9 %collective-permute-start.3 = (f32[512,128]{1,0:T(8,128)S(1)}, f32[512,128]{1,0:T(8,128)S(1)}, u32[]{:S(2)}, u32[]{:S(2)}) collective-permute-start(f32[512,128]{1,0:T(8,128)S(1)} %fusion.33), channel_id=1, source_target_pairs={{1,2},{3,4},{5,6},{7,8},{9,10},{11,12},{13,14},{15,16},{17,18},{19... | collective-permute-start | bytes 786440 | tf_op jit(solution)/shard_map/ppermute | solution.py:26
  31.1 0.0 collective-permute-done.2
  31.2 5.8 %collective-permute-done.3 = f32[512,128]{1,0:T(8,128)S(1)} collective-permute-done((f32[512,128]{1,0:T(8,128)S(1)}, f32[512,128]{1,0:T(8,128)S(1)}, u32[]{:S(2)}, u32[]{:S(2)}) %collective-permute-start.3) | collective-permute-done | bytes 262176 | tf_op jit(solution)/shard_map/ppermute | solution.py:26
  36.9 0.0 copy-done.4
  36.9 1.8 %select_reduce_fusion.6 = (f32[512]{0:T(512)S(1)}, f32[512]{0:T(512)S(1)}, f32[512,128]{0,1:T(8,128)S(1)}) fusion(s32[512]{0:T(512)S(1)} %copy-done.4, f32[512,1536]{1,0:T(8,128)S(1)} %constant_dynamic-update-slice_fusion, f32[512,128]{1,0:T(8,128)S(1)} %collective-permute-done.3, f32[512,128]{1,0:T(8,128)S(1)} %fusion.33, ...), kind=kOutput, calls=%fused_computation.58 | convolution fusion | flops 604634112 | bytes 4200448 | tf_op jit(solution)/shard_map/dot_general | solution.py:17
  38.7 0.6 subtract_reduce_fusion
  39.3 2.7 %fusion.36 = f32[1536,128]{1,0:T(8,128)S(1)} fusion(f32[512,1536]{1,0:T(8,128)S(1)} %constant_dynamic-update-slice_fusion, f32[512,128]{0,1:T(8,128)S(1)} %get-tuple-element.50, s32[512]{0:T(512)S(1)} %copy-done.4, f32[512]{0:T(512)S(1)} %get-tuple-element.42), kind=kOutput, calls=%fused_computation.59 | convolution fusion | flops 604241920 | bytes 4198400 | tf_op jit(solution)/shard_map/dot_general | solution.py:17
  42.0 1.9 %collective-permute-start.4 = (f32[512,128]{1,0:T(8,128)S(1)}, f32[512,128]{1,0:T(8,128)S(1)}, u32[]{:S(2)}, u32[]{:S(2)}) collective-permute-start(f32[512,128]{1,0:T(8,128)S(1)} %get-tuple-element.32), channel_id=1, source_target_pairs={{1,2},{3,4},{5,6},{7,8},{9,10},{11,12},{13,14},{15,16},{17,18},{19... | collective-permute-start | bytes 786440 | tf_op jit(solution)/shard_map/ppermute | solution.py:26
  44.0 2.1 %collective-permute-start.5 = (f32[512,128]{1,0:T(8,128)S(1)}, f32[512,128]{1,0:T(8,128)S(1)}, u32[]{:S(2)}, u32[]{:S(2)}) collective-permute-start(f32[512,128]{1,0:T(8,128)S(1)} %get-tuple-element.33), channel_id=1, source_target_pairs={{0,1},{1,0},{2,3},{3,2},{4,5},{5,4},{6,7},{7,6},{8,9},{9,8},{10,11... | collective-permute-start | bytes 786440 | tf_op jit(solution)/shard_map/ppermute | solution.py:21
  46.1 3.7 %collective-permute-done.4 = f32[512,128]{1,0:T(8,128)S(1)} collective-permute-done((f32[512,128]{1,0:T(8,128)S(1)}, f32[512,128]{1,0:T(8,128)S(1)}, u32[]{:S(2)}, u32[]{:S(2)}) %collective-permute-start.4) | collective-permute-done | bytes 262176 | tf_op jit(solution)/shard_map/ppermute | solution.py:26
  49.7 0.0 collective-permute-done.5
  49.7 0.6 fusion.53
  50.3 0.0 copy-start.1
  50.3 1.0 fusion.7
  51.4 1.0 fusion.32
  52.4 0.0 copy-done.1
  52.5 0.7 concatenate.30
  53.2 1.9 %collective-permute-start.6 = (f32[776,128]{1,0:T(8,128)S(1)}, f32[776,128]{1,0:T(8,128)S(1)}, u32[]{:S(2)}, u32[]{:S(2)}) collective-permute-start(f32[776,128]{1,0:T(8,128)S(1)} %concatenate.30), channel_id=1, source_target_pairs={{0,1},{1,0},{2,3},{3,2},{4,5},{5,4},{6,7},{7,6},{8,9},{9,8},{10,11... | collective-permute-start | bytes 1191944 | tf_op jit(solution)/shard_map/ppermute | solution.py:21
  55.1 1.7 %collective-permute-done.6 = f32[776,128]{1,0:T(8,128)S(1)} collective-permute-done((f32[776,128]{1,0:T(8,128)S(1)}, f32[776,128]{1,0:T(8,128)S(1)}, u32[]{:S(2)}, u32[]{:S(2)}) %collective-permute-start.6) | collective-permute-done | bytes 397344 | tf_op jit(solution)/shard_map/ppermute | solution.py:21
  56.8 0.1 slice_add_fusion
  56.9 0.7 fusion.44
  57.6 31.4 %all_to_all.15 = f32[32,25,128]{2,1,0:T(8,128)S(1)} all-to-all(f32[32,25,128]{2,1,0:T(8,128)S(1)} %pad_maximum_fusion), channel_id=1, replica_groups=mesh['x'=4,'z'=8,'y'=8,'c'=2] {'x','y'}, dimensions={0} | all-to-all | bytes 819200 | tf_op jit(solution)/shard_map/all_to_all | solution.py:30
  89.0 15.7 %all_to_all.16 = f32[8,25,128]{2,1,0:T(8,128)S(1)} all-to-all(f32[8,25,128]{2,1,0:T(8,128)S(1)} %broadcast_in_dim.84), channel_id=1, replica_groups=mesh['x'=4,'z'=8,'y'=8,'c'=2] {'z'}, dimensions={0} | all-to-all | bytes 204800 | tf_op jit(solution)/shard_map/all_to_all | solution.py:30
  104.8 17.3 %all_to_all.17 = f32[32,24,128]{2,1,0:T(8,128)S(1)} all-to-all(f32[32,24,128]{2,1,0:T(8,128)S(1)} %broadcast_in_dim.85), channel_id=1, replica_groups=mesh['x'=4,'z'=8,'y'=8,'c'=2] {'x','y'}, dimensions={0} | all-to-all | bytes 786432 | tf_op jit(solution)/shard_map/all_to_all | solution.py:30
  122.0 7.2 %collective-permute-start.7 = (f32[768,128]{1,0:T(8,128)S(1)}, f32[768,128]{1,0:T(8,128)S(1)}, u32[]{:S(2)}, u32[]{:S(2)}) collective-permute-start(f32[768,128]{1,0:T(8,128)S(1)} %bitcast.28), channel_id=1, source_target_pairs={{0,1},{1,0},{2,3},{3,2},{4,5},{5,4},{6,7},{7,6},{8,9},{9,8},{10,11... | collective-permute-start | bytes 1179656 | tf_op jit(solution)/shard_map/ppermute | solution.py:21
  129.2 0.8 copy.15
  130.0 0.5 slice.83
  131.2 0.0 collective-permute-done.7
  131.2 0.1 broadcast_select_fusion.1
  131.3 0.7 slice.89
  132.0 0.8 pad_maximum_fusion.1
  (12 shorter events, 0.3 us)
Async XLA Ops:
  0.6 21.1 %copy-start = (f32[256,512]{1,0:T(8,128)S(1)}, f32[256,512]{1,0:T(8,128)}, u32[]{:S(2)}) copy-start(f32[256,512]{1,0:T(8,128)} %param.12) | copy-start | bytes 1572868
  0.6 16.8 %collective-permute-start = (f32[512,256]{1,0:T(8,128)}, f32[512,256]{1,0:T(8,128)S(1)}, u32[]{:S(2)}, u32[]{:S(2)}) collective-permute-start(f32[512,256]{1,0:T(8,128)} %param.7), channel_id=1, source_target_pairs={{0,1},{1,0},{2,3},{3,2},{4,5},{5,4},{6,7},{7,6},{8,9},{9,8},{10,11... | collective-permute-start | bytes 1572872 | tf_op jit(solution)/shard_map/ppermute | solution.py:21
  9.6 10.7 %collective-permute-start.1 = (f32[512,256]{1,0:T(8,128)}, f32[512,256]{1,0:T(8,128)S(1)}, u32[]{:S(2)}, u32[]{:S(2)}) collective-permute-start(f32[512,256]{1,0:T(8,128)} %param.7), channel_id=1, source_target_pairs={{1,2},{3,4},{5,6},{7,8},{9,10},{11,12},{13,14},{15,16},{17,18},{19... | collective-permute-start | bytes 1572872 | tf_op jit(solution)/shard_map/ppermute | solution.py:26
  17.0 3.3 %copy-start.3 = (f32[512,256]{1,0:T(8,128)S(1)}, f32[512,256]{1,0:T(8,128)}, u32[]{:S(2)}) copy-start(f32[512,256]{1,0:T(8,128)} %param.7) | copy-start | bytes 1572868
  21.8 4.9 %copy-start.2 = (f32[512,128]{1,0:T(8,128)S(1)}, f32[512,128]{1,0:T(8,128)}, u32[]{:S(2)}) copy-start(f32[512,128]{1,0:T(8,128)} %param.13) | copy-start | bytes 786436
  21.8 15.1 %copy-start.4 = (s32[512]{0:T(512)S(1)}, s32[512]{0:T(512)}, u32[]{:S(2)}) copy-start(s32[512]{0:T(512)} %param.11) | copy-start | bytes 6148
  27.3 3.9 %collective-permute-start.2 = (f32[512,128]{1,0:T(8,128)S(1)}, f32[512,128]{1,0:T(8,128)S(1)}, u32[]{:S(2)}, u32[]{:S(2)}) collective-permute-start(f32[512,128]{1,0:T(8,128)S(1)} %fusion.33), channel_id=1, source_target_pairs={{0,1},{1,0},{2,3},{3,2},{4,5},{5,4},{6,7},{7,6},{8,9},{9,8},{10,11... | collective-permute-start | bytes 786440 | tf_op jit(solution)/shard_map/ppermute | solution.py:21
  29.2 7.7 %collective-permute-start.3 = (f32[512,128]{1,0:T(8,128)S(1)}, f32[512,128]{1,0:T(8,128)S(1)}, u32[]{:S(2)}, u32[]{:S(2)}) collective-permute-start(f32[512,128]{1,0:T(8,128)S(1)} %fusion.33), channel_id=1, source_target_pairs={{1,2},{3,4},{5,6},{7,8},{9,10},{11,12},{13,14},{15,16},{17,18},{19... | collective-permute-start | bytes 786440 | tf_op jit(solution)/shard_map/ppermute | solution.py:26
  42.0 7.7 %collective-permute-start.4 = (f32[512,128]{1,0:T(8,128)S(1)}, f32[512,128]{1,0:T(8,128)S(1)}, u32[]{:S(2)}, u32[]{:S(2)}) collective-permute-start(f32[512,128]{1,0:T(8,128)S(1)} %get-tuple-element.32), channel_id=1, source_target_pairs={{1,2},{3,4},{5,6},{7,8},{9,10},{11,12},{13,14},{15,16},{17,18},{19... | collective-permute-start | bytes 786440 | tf_op jit(solution)/shard_map/ppermute | solution.py:26
  44.0 5.8 %collective-permute-start.5 = (f32[512,128]{1,0:T(8,128)S(1)}, f32[512,128]{1,0:T(8,128)S(1)}, u32[]{:S(2)}, u32[]{:S(2)}) collective-permute-start(f32[512,128]{1,0:T(8,128)S(1)} %get-tuple-element.33), channel_id=1, source_target_pairs={{0,1},{1,0},{2,3},{3,2},{4,5},{5,4},{6,7},{7,6},{8,9},{9,8},{10,11... | collective-permute-start | bytes 786440 | tf_op jit(solution)/shard_map/ppermute | solution.py:21
  50.3 2.1 %copy-start.1 = (f32[512,512]{1,0:T(8,128)}, f32[512,512]{1,0:T(8,128)S(1)}, u32[]{:S(2)}) copy-start(f32[512,512]{1,0:T(8,128)S(1)} %fusion.53) | copy-start | bytes 3145732
  53.2 3.6 %collective-permute-start.6 = (f32[776,128]{1,0:T(8,128)S(1)}, f32[776,128]{1,0:T(8,128)S(1)}, u32[]{:S(2)}, u32[]{:S(2)}) collective-permute-start(f32[776,128]{1,0:T(8,128)S(1)} %concatenate.30), channel_id=1, source_target_pairs={{0,1},{1,0},{2,3},{3,2},{4,5},{5,4},{6,7},{7,6},{8,9},{9,8},{10,11... | collective-permute-start | bytes 1191944 | tf_op jit(solution)/shard_map/ppermute | solution.py:21
  122.0 9.2 %collective-permute-start.7 = (f32[768,128]{1,0:T(8,128)S(1)}, f32[768,128]{1,0:T(8,128)S(1)}, u32[]{:S(2)}, u32[]{:S(2)}) collective-permute-start(f32[768,128]{1,0:T(8,128)S(1)} %bitcast.28), channel_id=1, source_target_pairs={{0,1},{1,0},{2,3},{3,2},{4,5},{5,4},{6,7},{7,6},{8,9},{9,8},{10,11... | collective-permute-start | bytes 1179656 | tf_op jit(solution)/shard_map/ppermute | solution.py:21

commit v2 on v1

v2 whole, which is shorter than its diff:
```python
import jax
import jax.numpy as jnp
from jax import lax
from jax.experimental import pallas as pl
from jax.experimental.pallas import tpu as pltpu
from jax.sharding import Mesh, PartitionSpec as P

ALL = ("x", "z", "y", "c")
BIG = ("x", "y")
MID = ("z",)
LANES = 128
F32 = jnp.float32
BF16 = jnp.bfloat16
VMEM_LIMIT = 24 * 1024 * 1024
SQRT_HALF = 0.7071067811865476
INV_SQRT_2PI = 0.3989422804014327


def mate(value, devices):
    return lax.ppermute(value, ALL, [(i, i ^ 1) for i in range(devices)])


def beside(value, devices):
    pairs = [(i, i + 1) for i in range(1, devices - 1, 2)]
    return lax.ppermute(value, ALL, pairs + [(b, a) for a, b in pairs])


def exchange(value, axes):
    return lax.all_to_all(value, axes, 0, 0, tiled=True)


def spread(value, count):
    return jnp.broadcast_to(value[None], (count,) + value.shape)


def halves(value):
    high = value.astype(BF16)
    return high, (value - high.astype(F32)).astype(BF16)


def mm(a, b, dims=((1,), (0,))):
    return lax.dot_general(a, b, (dims, ((), ())), preferred_element_type=F32)


def fold(wide):
    half = wide.shape[1] // 2
    return wide[:, :half] + wide[:, half:]


def erfc(value):
    size = jnp.abs(value)
    t = 1.0 / (1.0 + 0.5 * size)
    poly = jnp.full_like(t, 0.17087277)
    for term in (-0.82215223, 1.48851587, -1.13520398, 0.27886807, -0.18628806, 0.09678418,
                 0.37409196, 1.00002368, -1.26551223):
        poly = poly * t + term
    tail = t * jnp.exp(poly - size * size)
    return jnp.where(value < 0, 2.0 - tail, tail)


def prepare(sel, adjacency, features, w_in, w_out, labels,
            loc_h, loc_l, halo_h, halo_l, s_loc, win_h, win_l, wout_hl, wout_hh, wout_ll, onehot, band):
    here, slots, rows, _ = adjacency.shape
    for b in range(here):
        band[...] = jnp.zeros_like(band)
        for k in range(slots):
            place = sel[b, k]

            @pl.when(place >= 0)
            def _():
                band[place] += adjacency[b, k]

        at = pl.ds(b * rows, rows)
        for s in range(3 * here):
            high, low = halves(band[s])
            if here <= s < 2 * here:
                cols = pl.ds((s - here) * rows, rows)
                loc_h[at, cols] = high
                loc_l[at, cols] = low
            else:
                cols = pl.ds((s if s < here else s - here) * rows, rows)
                halo_h[at, cols] = high
                halo_l[at, cols] = low
    feat_h, feat_l = halves(features[...])
    s_loc[...] = mm(loc_h[...], feat_h) + mm(loc_h[...], feat_l) + mm(loc_l[...], feat_h)
    high, low = halves(w_in[...])
    win_h[...] = high
    win_l[...] = low
    high, low = halves(w_out[...])
    classes = high.shape[1]
    for ref, left, right in ((wout_hl, high, low), (wout_hh, high, high), (wout_ll, low, low)):
        ref[:, :classes] = left
        ref[:, classes:] = right
    columns = lax.broadcasted_iota(jnp.int32, (classes, labels.shape[1]), 0)
    onehot[...] = jnp.where(columns == labels[...], 1.0, 0.0).T


def spread_forward(halo_h, halo_l, s_loc, feat_i, feat_e, win_h, win_l, wout_hl, spread_in, scores):
    half = feat_i.shape[0]
    fi_h, fi_l = halves(feat_i[...])
    fe_h, fe_l = halves(feat_e[...])
    hi, he = halo_h[:, :half], halo_h[:, half:]
    li, le = halo_l[:, :half], halo_l[:, half:]
    near = mm(hi, fi_h) + mm(hi, fi_l) + mm(li, fi_h)
    far = mm(he, fe_h) + mm(he, fe_l) + mm(le, fe_h)
    s = s_loc[...] + near + far
    spread_in[...] = s
    s_h, s_l = halves(s)
    pre = mm(s_h, win_h[...]) + mm(s_h, win_l[...]) + mm(s_l, win_h[...])
    hid_h, hid_l = halves(0.5 * pre * erfc(-SQRT_HALF * pre))
    scores[...] = fold(mm(hid_h, wout_hl[...]) + mm(hid_l, wout_hl[...]))


def beside_forward(loc_h, loc_l, spread_in, scores, win_h, win_l, slope, hid_th, hid_tl, in_th, in_tl, logits_loc):
    s = spread_in[...]
    s_h, s_l = halves(s)
    pre = mm(s_h, win_h[...]) + mm(s_h, win_l[...]) + mm(s_l, win_h[...])
    gate = 0.5 * erfc(-SQRT_HALF * pre)
    slope[...] = gate + pre * (INV_SQRT_2PI * jnp.exp(-0.5 * pre * pre))
    high, low = halves((pre * gate).T)
    hid_th[...] = high
    hid_tl[...] = low
    high, low = halves(s.T)
    in_th[...] = high
    in_tl[...] = low
    pair = jnp.concatenate(halves(scores[...]), axis=1)
    logits_loc[...] = fold(mm(loc_h[...], pair) + mm(loc_l[...], pair))


def classify(halo_h, halo_l, logits_loc, sco_i, sco_e, onehot, logits, grads_t, loss, out_i, out_e):
    half = sco_i.shape[0]
    classes = logits.shape[1]
    pair_i = jnp.concatenate(halves(sco_i[...]), axis=1)
    pair_e = jnp.concatenate(halves(sco_e[...]), axis=1)
    wide = mm(halo_h[:, :half], pair_i) + mm(halo_l[:, :half], pair_i)
    wide = wide + mm(halo_h[:, half:], pair_e) + mm(halo_l[:, half:], pair_e)
    values = logits_loc[...] + fold(wide)
    logits[...] = values
    totals = jnp.log(jnp.sum(jnp.exp(values), axis=1, keepdims=True))
    hot = onehot[...]
    row_loss = totals - jnp.sum(hot * values, axis=1, keepdims=True)
    loss[...] = jnp.broadcast_to(jnp.sum(row_loss, axis=0, keepdims=True), loss.shape)
    high, low = halves((jnp.exp(values - totals) - hot).T)
    grads = jnp.concatenate([high, low], axis=0)
    grads_t[...] = grads
    for out, cols in ((out_i, pl.ds(0, half)), (out_e, pl.ds(half, half))):
        tall = mm(grads, halo_h[:, cols]) + mm(grads, halo_l[:, cols])
        out[...] = tall[:classes] + tall[classes:]


def beside_classify(grads_t, loc_h, loc_l, out):
    tall = mm(grads_t[...], loc_h[...]) + mm(grads_t[...], loc_l[...])
    half = tall.shape[0] // 2
    out[...] = tall[:half] + tall[half:]


def backward(core, ret_loc, ret_i, ret_e, wout_hh, wout_ll, slope, in_th, in_tl, hid_th, hid_tl, loss,
             hidden_grad, keep, give):
    returned = (ret_loc[...] + ret_i[...] + ret_e[...]).T
    pair = jnp.concatenate(halves(returned), axis=1)
    across = ((1,), (1,))
    grad = mm(pair, wout_hh[...], across) + mm(pair, wout_ll[...], across)
    hidden_grad[...] = grad
    pre_h, pre_l = halves(grad * slope[...])
    grad_in = mm(in_th[...], pre_h) + mm(in_th[...], pre_l) + mm(in_tl[...], pre_h)
    grad_out = fold(mm(hid_th[...], pair) + mm(hid_tl[...], pair))
    deep = grad_in.shape[0]
    rows = keep.shape[0]
    give[rows:, :] = loss[...]
    pieces = [grad_in[:, t : t + LANES] for t in range(0, grad_in.shape[1], LANES)] + [grad_out]
    for first, second in ((keep, give), (give, keep)):

        @pl.when(core[0] == (0 if first is keep else 1))
        def _():
            at = 0
            for piece in pieces:
                ref, start = (first, at) if at < rows else (second, at - rows)
                ref[pl.ds(start, piece.shape[0]), :] = piece
                at += piece.shape[0]


def assemble(core, own, other, grad_in, grad_out):
    deep = grad_in.shape[0]
    rows = own.shape[0]
    for first, second in ((own, other), (other, own)):

        @pl.when(core[0] == (0 if first is own else 1))
        def _():
            tiles = grad_in.shape[1] // LANES
            for t in range(tiles):
                at = t * deep
                ref, start = (first, at) if at < rows else (second, at - rows)
                grad_in[:, pl.ds(t * LANES, LANES)] = ref[pl.ds(start, deep), :]
            grad_out[...] = second[pl.ds(tiles * deep - rows, grad_out.shape[0]), :]


def call(body, outs, args, scalars=0, flops=0, scratch=()):
    smem = pl.BlockSpec(memory_space=pltpu.SMEM)
    vmem = pl.BlockSpec(memory_space=pltpu.VMEM)
    moved = sum(a.size * a.dtype.itemsize for a in args)
    return pl.pallas_call(
        body,
        out_shape=[jax.ShapeDtypeStruct(shape, kind) for shape, kind in outs],
        in_specs=[smem] * scalars + [vmem] * (len(args) - scalars),
        out_specs=[vmem] * len(outs),
        scratch_shapes=scratch,
        cost_estimate=pl.CostEstimate(flops=flops, bytes_accessed=moved, transcendentals=0),
        compiler_params=pltpu.CompilerParams(vmem_limit_bytes=VMEM_LIMIT),
        name=body.__name__,
    )(*args)


def per_device(features, adjacency, block_index, block_counts, labels, weight_in, weight_out):
    devices = lax.axis_size(ALL)
    core = lax.axis_index("c")
    cores = jnp.full((1,), core, jnp.int32)
    here, slots, rows = adjacency.shape[:3]
    nodes = here * rows
    deep, hid = weight_in.shape
    classes = weight_out.shape[1]
    near = block_index - lax.axis_index(ALL) * here
    local = (near >= 0) & (near < here)
    right = near >= here
    outside = jnp.where(right, near - here, near + here)
    bucket = jnp.where(local, here + near, outside + jnp.where(right == (core == 0), 0, 2 * here))
    usable = jnp.arange(slots, dtype=jnp.int32)[None, :] < block_counts[:, None]
    sel = jnp.where(usable, bucket, -1)

    feat_e = beside(features, devices)
    feat_i = mate(features, devices)
    loc = ((nodes, nodes), BF16)
    halo = ((nodes, 2 * nodes), BF16)
    w_pair = ((hid, 2 * classes), BF16)
    loc_h, loc_l, halo_h, halo_l, s_loc, win_h, win_l, wout_hl, wout_hh, wout_ll, onehot = call(
        prepare,
        [loc, loc, halo, halo, ((nodes, deep), F32), ((deep, hid), BF16), ((deep, hid), BF16),
         w_pair, w_pair, w_pair, ((nodes, classes), F32)],
        [sel, adjacency, features, weight_in, weight_out, labels.reshape(1, nodes)],
        scalars=1,
        flops=6 * nodes * nodes * deep,
        scratch=[pltpu.VMEM((3 * here, rows, rows), F32)],
    )
    spread_in, scores = call(
        spread_forward,
        [((nodes, deep), F32), ((nodes, classes), F32)],
        [halo_h, halo_l, s_loc, feat_i, feat_e, win_h, win_l, wout_hl],
        flops=20 * nodes * nodes * deep,
    )
    sco_e = beside(scores, devices)
    sco_i = mate(scores, devices)
    slope, hid_th, hid_tl, in_th, in_tl, logits_loc = call(
        beside_forward,
        [((nodes, hid), F32), ((hid, nodes), BF16), ((hid, nodes), BF16), ((deep, nodes), BF16), ((deep, nodes), BF16),
         ((nodes, classes), F32)],
        [loc_h, loc_l, spread_in, scores, win_h, win_l],
        flops=12 * nodes * nodes * deep,
    )
    logits, grads_t, loss, out_i, out_e = call(
        classify,
        [((nodes, classes), F32), ((2 * classes, nodes), BF16), ((8, LANES), F32), ((classes, nodes), F32),
         ((classes, nodes), F32)],
        [halo_h, halo_l, logits_loc, sco_i, sco_e, onehot],
        flops=16 * nodes * nodes * classes,
    )
    ret_e = beside(out_e, devices)
    ret_i = mate(out_i, devices)
    (ret_loc,) = call(
        beside_classify, [((classes, nodes), F32)], [grads_t, loc_h, loc_l], flops=8 * nodes * nodes * classes
    )
    half = (deep * hid + hid * classes) // LANES // 2
    hidden_grad, keep, give = call(
        backward,
        [((nodes, hid), F32), ((half, LANES), F32), ((half + 8, LANES), F32)],
        [cores, ret_loc, ret_i, ret_e, wout_hh, wout_ll, slope, in_th, in_tl, hid_th, hid_tl, loss],
        scalars=1,
        flops=12 * nodes * nodes * deep,
    )
    parts = mate(give, devices)
    big, mid = lax.axis_size(BIG), lax.axis_size(MID)
    shard = half // big
    mine = (keep + parts[:half]).reshape(big, shard, LANES)
    loss_row = jnp.broadcast_to(loss[:1] + parts[half : half + 1], (big, 1, LANES))
    summed = jnp.sum(exchange(jnp.concatenate([mine, loss_row], axis=1), BIG), axis=0)
    summed = jnp.sum(exchange(spread(summed, mid), MID), axis=0)
    mean_loss = summed[shard, 0] / (nodes * devices)
    own = exchange(spread(summed[:shard], big), BIG).reshape(half, LANES)
    other = mate(own, devices)
    grad_in, grad_out = call(
        assemble, [((deep, hid), F32), ((hid, classes), F32)], [cores, own, other], scalars=1
    )
    return (logits, mean_loss, hidden_grad, grad_in, grad_out)


def solution(mesh):
    grid = Mesh(mesh.devices.reshape(4, 8, 8, 2), ALL)
    split = P(ALL)
    return jax.shard_map(
        per_device,
        mesh=grid,
        in_specs=(split, split, split, split, split, P(), P()),
        out_specs=(split, P(), split, P(), P()),
        check_vma=False,
    )
```

time: 134 us -> 128 us (0.955)
  Pallas kernels: 0 us -> 15.1 us
  matrix products: 14 us -> 0 us
  other arithmetic: 7.82 us -> 0.92 us
  waiting for transfers between devices: 13.9 us -> 7.38 us
  starting transfers between devices: 27.8 us -> 31.5 us
  local copies, waits for them, and re-layouts: 3.36 us -> 6.17 us
    pallas_call x0 -> x7, Pallas kernels: none -> 15.1 us  [call(): pl.pallas_call(body, out_shape=[jax.ShapeDtypeStruct(shape, kind) for sha...]
    dot_general x8 -> x0, matrix products: 14 us -> none  [dot(): return lax.dot_general(a, b, (dims, ((), ())), precision=HIGH)]
    ppermute x3, waiting for transfers between devices: 12.2 us -> 5.51 us  [beside(): return lax.ppermute(value, ALL, pairs + [(b, a) for a, b in pairs])]
    reduce_sum x2 -> x0, other arithmetic: 4.57 us -> none  [the longest x1 3.96 us: per_device(): jnp.sum(jnp.where(take[:, :, None, None], adjacency, 0.0), axis=1)]
    unnamed x16 -> x10, local copies, waits for them, and re-layouts: 1.22 us -> 5.6 us
    ppermute x3, starting transfers between devices: 5.76 us -> 9.79 us  [beside(): return lax.ppermute(value, ALL, pairs + [(b, a) for a, b in pairs])]
    and x2 -> x0, other arithmetic: 1.5 us -> none  [per_device(): take = usable & (bucket == s)]
  transfers between devices with their start and end apart: 8 -> 8, of which waited for: 4 -> 4; matrix products, arithmetic and copies ran while one was open for 5% -> 1% of each run, Pallas kernels for 0% -> 4%
where the time goes in v2:
time: 128 us; the launch traced here: 127 us
  blocking collectives  63.7 us (50%)
  starting transfers between devices  31.5 us (25%)
  Pallas kernels  15.1 us (12%)
  waiting for transfers between devices  7.38 us (6%)
  local copies, waits for them, and re-layouts  6.17 us (5%)
  between operations  2.62 us (2%)
    all_to_all x3, blocking collectives, exchange(): return lax.all_to_all(value, axes, 0, 0, tiled=True)  63.7 us
    ppermute x5, starting transfers between devices, mate(): return lax.ppermute(value, ALL, [(i, i ^ 1) for i in range(devices)])  21.7 us
    pallas_call x7, Pallas kernels, call(): pl.pallas_call(body, out_shape=[jax.ShapeDtypeStruct(shape, kind) for sha...  15.1 us
    ppermute x3, starting transfers between devices, beside(): return lax.ppermute(value, ALL, pairs + [(b, a) for a, b in pairs])  9.79 us
    unnamed x10, local copies, waits for them, and re-layouts  5.6 us
    ppermute x3, waiting for transfers between devices, beside(): return lax.ppermute(value, ALL, pairs + [(b, a) for a, b in pairs])  5.51 us
  transfers between devices with their start and end apart: 8, of which 4 were waited for; matrix products, arithmetic and copies ran while one was open for 1% of the time, Pallas kernels for 4%

profile of v2, /device:TPU:1, one launch (start us, length us, event | category | flops | bytes accessed | tf_op | source)
XLA Modules:
  0.0 127.4 jit_solution(3329642290010479263)
XLA Ops:
  0.6 8.8 %collective-permute-start = (f32[512,256]{1,0:T(8,128)}, f32[512,256]{1,0:T(8,128)S(1)}, u32[]{:S(2)}, u32[]{:S(2)}) collective-permute-start(f32[512,256]{1,0:T(8,128)} %features.1), channel_id=1, source_target_pairs={{0,1},{1,0},{2,3},{3,2},{4,5},{5,4},{6,7},{7,6},{8,9},{9,8},{10,11... | collective-permute-start | bytes 1572872 | tf_op jit(solution)/shard_map/ppermute | solution.py:20
  9.4 1.9 %collective-permute-start.1 = (f32[512,256]{1,0:T(8,128)}, f32[512,256]{1,0:T(8,128)S(1)}, u32[]{:S(2)}, u32[]{:S(2)}) collective-permute-start(f32[512,256]{1,0:T(8,128)} %features.1), channel_id=1, source_target_pairs={{1,2},{3,4},{5,6},{7,8},{9,10},{11,12},{13,14},{15,16},{17,18},{19... | collective-permute-start | bytes 1572872 | tf_op jit(solution)/shard_map/ppermute | solution.py:25
  11.4 0.8 compare_select_fusion.1.sel
  12.1 0.0 copy-start
  12.1 1.9 %copy-done = f32[2,6,256,256]{3,2,1,0:T(8,128)S(1)} copy-done((f32[2,6,256,256]{3,2,1,0:T(8,128)S(1)}, f32[2,6,256,256]{3,2,1,0:T(8,128)}, u32[]{:S(2)}) %copy-start) | copy-done | bytes 3145752
  14.0 0.0 copy-start.1
  14.0 1.0 copy-done.1
  15.1 0.0 copy-start.2
  15.1 1.0 copy-done.2
  16.1 0.0 copy-start.3
  16.1 0.9 copy-done.3
  17.1 0.0 copy-start.4
  17.1 0.7 copy-done.4
  17.7 2.4 %prepare.1 = (bf16[512,512]{1,0:T(8,128)(2,1)S(1)}, bf16[512,512]{1,0:T(8,128)(2,1)S(1)}, bf16[512,1024]{1,0:T(8,128)(2,1)S(1)}, bf16[512,1024]{1,0:T(8,128)(2,1...) custom-call(s32[2,6]{1,0:T(2,128)S(1)} %compare_select_fusion.1.sel,, ...), custom_call_target="tpu_custom_call" | custom-call | flops 402653184 | bytes 4458544 | tf_op jit(solution)/shard_map/prepare/pallas_call | solution.py:201
  20.2 0.0 collective-permute-done.feat_i
  20.2 0.0 collective-permute-done.1.feat_e
  20.2 4.0 %spread_forward.1 = (f32[512,256]{1,0:T(8,128)S(1)}, f32[512,128]{1,0:T(8,128)S(1)}) custom-call(bf16[512,1024]{1,0:T(8,128)(2,1)S(1)} %get-tuple-element.34.halo_h, bf16[512,1024]{1,0:T(8,128)(2,1)S(1)} %get-tuple-element.35.halo_l, f32[512,256]{1,0:T(8,128)S(1)} %get-tuple-element.38.s_loc, f32[512,256]{1,0:T(8,128)S(1)} %collective-permute-done.feat_i, ...), custom_call_target="tpu_custom_call" | custom-call | flops 1342177280 | bytes 4456448 | tf_op jit(solution)/shard_map/spread_forward/pallas_call | solution.py:201
  24.2 1.9 %collective-permute-start.2 = (f32[512,128]{1,0:T(8,128)S(1)}, f32[512,128]{1,0:T(8,128)S(1)}, u32[]{:S(2)}, u32[]{:S(2)}) collective-permute-start(f32[512,128]{1,0:T(8,128)S(1)} %get-tuple-element.43.scores), channel_id=1, source_target_pairs={{0,1},{1,0},{2,3},{3,2},{4,5},{5,4},{6,7},{7,6},{8,9},{9,8},{10,11... | collective-permute-start | bytes 786440 | tf_op jit(solution)/shard_map/ppermute | solution.py:20
  26.1 3.7 %collective-permute-start.3 = (f32[512,128]{1,0:T(8,128)S(1)}, f32[512,128]{1,0:T(8,128)S(1)}, u32[]{:S(2)}, u32[]{:S(2)}) collective-permute-start(f32[512,128]{1,0:T(8,128)S(1)} %get-tuple-element.43.scores), channel_id=1, source_target_pairs={{1,2},{3,4},{5,6},{7,8},{9,10},{11,12},{13,14},{15,16},{17,18},{19... | collective-permute-start | bytes 786440 | tf_op jit(solution)/shard_map/ppermute | solution.py:25
  29.8 2.1 %beside_forward.1 = (f32[512,512]{1,0:T(8,128)S(1)}, bf16[512,512]{1,0:T(8,128)(2,1)S(1)}, bf16[512,512]{1,0:T(8,128)(2,1)S(1)}, bf16[256,512]{1,0:T(8,128)(2,1)...) custom-call(bf16[512,512]{1,0:T(8,128)(2,1)S(1)} %get-tuple-element.36.loc_h, ...), custom_call_target="tpu_custom_call" | custom-call | flops 805306368 | bytes 2359296 | tf_op jit(solution)/shard_map/beside_forward/pallas_call | solution.py:201
  31.9 0.0 collective-permute-done.2.sco_i
  32.0 1.9 %collective-permute-done.3.sco_e = f32[512,128]{1,0:T(8,128)S(1)} collective-permute-done((f32[512,128]{1,0:T(8,128)S(1)}, f32[512,128]{1,0:T(8,128)S(1)}, u32[]{:S(2)}, u32[]{:S(2)}) %collective-permute-start.3) | collective-permute-done | bytes 262176 | tf_op jit(solution)/shard_map/ppermute | solution.py:25
  33.9 2.6 %classify.1 = (f32[512,128]{1,0:T(8,128)}, bf16[256,512]{1,0:T(8,128)(2,1)S(1)}, f32[8,128]{1,0:T(8,128)S(1)}, f32[128,512]{1,0:T(8,128)S(1)}, f32[128,512]{1,0:T(8,128)S(1)}) custom-call(bf16[512,1024]{1,0:T(8,128)(2,1)S(1)} %get-tuple-element.34.halo_h, bf16[512,1024]{1,0:T(8,128)(2,1)S(1)} %get-tuple-element.35.halo_l, ...), custom_call_target="tpu_custom_call" | custom-call | flops 536870912 | bytes 3145728 | tf_op jit(solution)/shard_map/classify/pallas_call | solution.py:201
  36.5 1.9 %collective-permute-start.4 = (f32[128,512]{1,0:T(8,128)S(1)}, f32[128,512]{1,0:T(8,128)S(1)}, u32[]{:S(2)}, u32[]{:S(2)}) collective-permute-start(f32[128,512]{1,0:T(8,128)S(1)} %get-tuple-element.48), channel_id=1, source_target_pairs={{0,1},{1,0},{2,3},{3,2},{4,5},{5,4},{6,7},{7,6},{8,9},{9,8},{10,11... | collective-permute-start | bytes 786440 | tf_op jit(solution)/shard_map/ppermute | solution.py:20
  38.4 4.1 %collective-permute-start.5 = (f32[128,512]{1,0:T(8,128)S(1)}, f32[128,512]{1,0:T(8,128)S(1)}, u32[]{:S(2)}, u32[]{:S(2)}) collective-permute-start(f32[128,512]{1,0:T(8,128)S(1)} %get-tuple-element.49), channel_id=1, source_target_pairs={{1,2},{3,4},{5,6},{7,8},{9,10},{11,12},{13,14},{15,16},{17,18},{19... | collective-permute-start | bytes 786440 | tf_op jit(solution)/shard_map/ppermute | solution.py:25
  42.5 0.4 beside_classify.1.ret_loc
  43.0 0.0 collective-permute-done.4.ret_i
  43.0 3.6 %collective-permute-done.5.ret_e = f32[128,512]{1,0:T(8,128)S(1)} collective-permute-done((f32[128,512]{1,0:T(8,128)S(1)}, f32[128,512]{1,0:T(8,128)S(1)}, u32[]{:S(2)}, u32[]{:S(2)}) %collective-permute-start.5) | collective-permute-done | bytes 262176 | tf_op jit(solution)/shard_map/ppermute | solution.py:25
  46.6 2.6 %backward.1 = (f32[512,512]{1,0:T(8,128)}, f32[768,128]{1,0:T(8,128)S(1)}, f32[776,128]{1,0:T(8,128)S(1)}) custom-call(s32[1]{0:T(128)} %bitcast.1.core, f32[128,512]{1,0:T(8,128)S(1)} %beside_classify.1.ret_loc, f32[128,512]{1,0:T(8,128)S(1)} %collective-permute-done.4.ret_i, f32[128,512]{1,0:T(8,128)S(1)} %collective-permute-done.5.ret_e, ...), custom_call_target="tpu_custom_call" | custom-call | flops 805306368 | bytes 3936260 | tf_op jit(solution)/shard_map/backward/pallas_call | solution.py:201
  49.2 1.9 %collective-permute-start.6 = (f32[776,128]{1,0:T(8,128)S(1)}, f32[776,128]{1,0:T(8,128)S(1)}, u32[]{:S(2)}, u32[]{:S(2)}) collective-permute-start(f32[776,128]{1,0:T(8,128)S(1)} %get-tuple-element.59), channel_id=1, source_target_pairs={{0,1},{1,0},{2,3},{3,2},{4,5},{5,4},{6,7},{7,6},{8,9},{9,8},{10,11... | collective-permute-start | bytes 1191944 | tf_op jit(solution)/shard_map/ppermute | solution.py:20
  51.1 1.7 %collective-permute-done.6 = f32[776,128]{1,0:T(8,128)S(1)} collective-permute-done((f32[776,128]{1,0:T(8,128)S(1)}, f32[776,128]{1,0:T(8,128)S(1)}, u32[]{:S(2)}, u32[]{:S(2)}) %collective-permute-start.6) | collective-permute-done | bytes 397344 | tf_op jit(solution)/shard_map/ppermute | solution.py:20
  52.8 0.1 slice_add_fusion
  53.0 32.4 %all_to_all.15 = f32[32,25,128]{2,1,0:T(8,128)S(1)} all-to-all(f32[32,25,128]{2,1,0:T(8,128)S(1)} %pad_maximum_fusion), channel_id=1, replica_groups=mesh['x'=4,'z'=8,'y'=8,'c'=2] {'x','y'}, dimensions={0} | all-to-all | bytes 819200 | tf_op jit(solution)/shard_map/all_to_all | solution.py:29
  85.4 14.1 %all_to_all.16 = f32[8,25,128]{2,1,0:T(8,128)S(1)} all-to-all(f32[8,25,128]{2,1,0:T(8,128)S(1)} %broadcast_in_dim.34), channel_id=1, replica_groups=mesh['x'=4,'z'=8,'y'=8,'c'=2] {'z'}, dimensions={0} | all-to-all | bytes 204800 | tf_op jit(solution)/shard_map/all_to_all | solution.py:29
  99.5 17.3 %all_to_all.17 = f32[32,24,128]{2,1,0:T(8,128)S(1)} all-to-all(f32[32,24,128]{2,1,0:T(8,128)S(1)} %broadcast_in_dim.35), channel_id=1, replica_groups=mesh['x'=4,'z'=8,'y'=8,'c'=2] {'x','y'}, dimensions={0} | all-to-all | bytes 786432 | tf_op jit(solution)/shard_map/all_to_all | solution.py:29
  116.8 7.2 %collective-permute-start.7 = (f32[768,128]{1,0:T(8,128)S(1)}, f32[768,128]{1,0:T(8,128)S(1)}, u32[]{:S(2)}, u32[]{:S(2)}) collective-permute-start(f32[768,128]{1,0:T(8,128)S(1)} %bitcast.7), channel_id=1, source_target_pairs={{0,1},{1,0},{2,3},{3,2},{4,5},{5,4},{6,7},{7,6},{8,9},{9,8},{10,11... | collective-permute-start | bytes 1179656 | tf_op jit(solution)/shard_map/ppermute | solution.py:20
  123.9 0.5 slice.22
  125.1 0.2 collective-permute-done.7.other
  125.3 1.0 assemble.1
  (8 shorter events, 0.2 us)
Async XLA Ops:
  0.6 19.5 %collective-permute-start = (f32[512,256]{1,0:T(8,128)}, f32[512,256]{1,0:T(8,128)S(1)}, u32[]{:S(2)}, u32[]{:S(2)}) collective-permute-start(f32[512,256]{1,0:T(8,128)} %features.1), channel_id=1, source_target_pairs={{0,1},{1,0},{2,3},{3,2},{4,5},{5,4},{6,7},{7,6},{8,9},{9,8},{10,11... | collective-permute-start | bytes 1572872 | tf_op jit(solution)/shard_map/ppermute | solution.py:20
  9.4 10.7 %collective-permute-start.1 = (f32[512,256]{1,0:T(8,128)}, f32[512,256]{1,0:T(8,128)S(1)}, u32[]{:S(2)}, u32[]{:S(2)}) collective-permute-start(f32[512,256]{1,0:T(8,128)} %features.1), channel_id=1, source_target_pairs={{1,2},{3,4},{5,6},{7,8},{9,10},{11,12},{13,14},{15,16},{17,18},{19... | collective-permute-start | bytes 1572872 | tf_op jit(solution)/shard_map/ppermute | solution.py:25
  12.1 1.9 %copy-start = (f32[2,6,256,256]{3,2,1,0:T(8,128)S(1)}, f32[2,6,256,256]{3,2,1,0:T(8,128)}, u32[]{:S(2)}) copy-start(f32[2,6,256,256]{3,2,1,0:T(8,128)} %adjacency.1) | copy-start | bytes 9437188
  14.0 1.0 copy-start.1
  15.1 1.0 copy-start.2
  16.1 0.9 copy-start.3
  17.1 0.7 copy-start.4
  24.2 7.8 %collective-permute-start.2 = (f32[512,128]{1,0:T(8,128)S(1)}, f32[512,128]{1,0:T(8,128)S(1)}, u32[]{:S(2)}, u32[]{:S(2)}) collective-permute-start(f32[512,128]{1,0:T(8,128)S(1)} %get-tuple-element.43.scores), channel_id=1, source_target_pairs={{0,1},{1,0},{2,3},{3,2},{4,5},{5,4},{6,7},{7,6},{8,9},{9,8},{10,11... | collective-permute-start | bytes 786440 | tf_op jit(solution)/shard_map/ppermute | solution.py:20
  26.1 7.8 %collective-permute-start.3 = (f32[512,128]{1,0:T(8,128)S(1)}, f32[512,128]{1,0:T(8,128)S(1)}, u32[]{:S(2)}, u32[]{:S(2)}) collective-permute-start(f32[512,128]{1,0:T(8,128)S(1)} %get-tuple-element.43.scores), channel_id=1, source_target_pairs={{1,2},{3,4},{5,6},{7,8},{9,10},{11,12},{13,14},{15,16},{17,18},{19... | collective-permute-start | bytes 786440 | tf_op jit(solution)/shard_map/ppermute | solution.py:25
  36.5 6.5 %collective-permute-start.4 = (f32[128,512]{1,0:T(8,128)S(1)}, f32[128,512]{1,0:T(8,128)S(1)}, u32[]{:S(2)}, u32[]{:S(2)}) collective-permute-start(f32[128,512]{1,0:T(8,128)S(1)} %get-tuple-element.48), channel_id=1, source_target_pairs={{0,1},{1,0},{2,3},{3,2},{4,5},{5,4},{6,7},{7,6},{8,9},{9,8},{10,11... | collective-permute-start | bytes 786440 | tf_op jit(solution)/shard_map/ppermute | solution.py:20
  38.4 8.2 %collective-permute-start.5 = (f32[128,512]{1,0:T(8,128)S(1)}, f32[128,512]{1,0:T(8,128)S(1)}, u32[]{:S(2)}, u32[]{:S(2)}) collective-permute-start(f32[128,512]{1,0:T(8,128)S(1)} %get-tuple-element.49), channel_id=1, source_target_pairs={{1,2},{3,4},{5,6},{7,8},{9,10},{11,12},{13,14},{15,16},{17,18},{19... | collective-permute-start | bytes 786440 | tf_op jit(solution)/shard_map/ppermute | solution.py:25
  49.2 3.6 %collective-permute-start.6 = (f32[776,128]{1,0:T(8,128)S(1)}, f32[776,128]{1,0:T(8,128)S(1)}, u32[]{:S(2)}, u32[]{:S(2)}) collective-permute-start(f32[776,128]{1,0:T(8,128)S(1)} %get-tuple-element.59), channel_id=1, source_target_pairs={{0,1},{1,0},{2,3},{3,2},{4,5},{5,4},{6,7},{7,6},{8,9},{9,8},{10,11... | collective-permute-start | bytes 1191944 | tf_op jit(solution)/shard_map/ppermute | solution.py:20
  116.8 8.5 %collective-permute-start.7 = (f32[768,128]{1,0:T(8,128)S(1)}, f32[768,128]{1,0:T(8,128)S(1)}, u32[]{:S(2)}, u32[]{:S(2)}) collective-permute-start(f32[768,128]{1,0:T(8,128)S(1)} %bitcast.7), channel_id=1, source_target_pairs={{0,1},{1,0},{2,3},{3,2},{4,5},{5,4},{6,7},{7,6},{8,9},{9,8},{10,11... | collective-permute-start | bytes 1179656 | tf_op jit(solution)/shard_map/ppermute | solution.py:20

commit v3 on v2

v3 whole, which is shorter than its diff:
```python
import functools

import jax
import jax.numpy as jnp
from jax import lax
from jax.experimental import pallas as pl
from jax.experimental.pallas import tpu as pltpu
from jax.sharding import Mesh, PartitionSpec as P

ALL = ("x", "z", "y", "c")
BIG = ("x", "y")
MID = ("z",)
LANES = 128
F32 = jnp.float32
BF16 = jnp.bfloat16
VMEM_LIMIT = 24 * 1024 * 1024
CHUNK = 256
SQRT_HALF = 0.7071067811865476
INV_SQRT_2PI = 0.3989422804014327


def mate(value, devices):
    return lax.ppermute(value, ALL, [(i, i ^ 1) for i in range(devices)])


def beside(value, devices):
    pairs = [(i, i + 1) for i in range(1, devices - 1, 2)]
    return lax.ppermute(value, ALL, pairs + [(b, a) for a, b in pairs])


def exchange(value, axes):
    return lax.all_to_all(value, axes, 0, 0, tiled=True)


def spread(value, count):
    return jnp.broadcast_to(value[None], (count,) + value.shape)


def position():
    place = 0
    for axis in ALL:
        place = place * lax.axis_size(axis) + lax.axis_index(axis)
    return place


def halves(value):
    high = value.astype(BF16)
    return high, (value - high.astype(F32)).astype(BF16)


def mm(a, b, dims=((1,), (0,))):
    return lax.dot_general(a, b, (dims, ((), ())), preferred_element_type=F32)


def fold(wide):
    half = wide.shape[1] // 2
    return wide[:, :half] + wide[:, half:]


def erfc(value):
    size = jnp.abs(value)
    t = 1.0 / (1.0 + 0.5 * size)
    poly = jnp.full_like(t, 0.17087277)
    for term in (-0.82215223, 1.48851587, -1.13520398, 0.27886807, -0.18628806, 0.09678418,
                 0.37409196, 1.00002368, -1.26551223):
        poly = poly * t + term
    tail = t * jnp.exp(poly - size * size)
    return jnp.where(value < 0, 2.0 - tail, tail)


def prepare(block_index, block_counts, adjacency, features, w_in, w_out, labels,
            loc_h, loc_l, halo_h, halo_l, s_loc, win_h, win_l, wout_hl, wout_hh, wout_ll, onehot, feat_out,
            slots_in, feat_in, win_in, wout_in, labels_in, band, sems):
    here, slots, rows, _ = adjacency.shape
    moves = [(features, feat_in), (w_in, win_in), (w_out, wout_in), (labels, labels_in)]
    moves += [(adjacency.at[b, k], slots_in.at[b, k]) for b in range(here) for k in range(slots)]
    moves = [pltpu.make_async_copy(source, target, sems.at[i]) for i, (source, target) in enumerate(moves)]
    for move in moves:
        move.start()
    core = lax.axis_index("c")
    first = position() * here
    band[...] = jnp.zeros_like(band)
    for move in moves[:4]:
        move.wait()
    high, low = halves(win_in[...])
    win_h[...] = high
    win_l[...] = low
    high, low = halves(wout_in[...])
    classes = high.shape[1]
    for ref, left, right in ((wout_hl, high, low), (wout_hh, high, high), (wout_ll, low, low)):
        ref[:, :classes] = left
        ref[:, classes:] = right
    columns = lax.broadcasted_iota(jnp.int32, (classes, labels_in.shape[1]), 0)
    onehot[...] = jnp.where(columns == labels_in[...], 1.0, 0.0).T
    feat_out[...] = feat_in[...]
    feat_h, feat_l = halves(feat_in[...])
    for b in range(here):
        for k in range(slots):
            moves[4 + b * slots + k].wait()
            near = block_index[b, k] - first
            right = near >= here
            outside = jnp.where(right, near - here, near + here)
            outside += jnp.where(right == (core == 0), 0, 2 * here)
            place = jnp.where((near >= 0) & (near < here), here + near, outside)

            @pl.when(k < block_counts[b])
            def _():
                band[b, place] += slots_in[b, k]

        at = pl.ds(b * rows, rows)
        for s in range(3 * here):
            high, low = halves(band[b, s])
            if here <= s < 2 * here:
                cols = pl.ds((s - here) * rows, rows)
                loc_h[at, cols] = high
                loc_l[at, cols] = low
            else:
                cols = pl.ds((s if s < here else s - here) * rows, rows)
                halo_h[at, cols] = high
                halo_l[at, cols] = low
        s_loc[at, :] = mm(loc_h[at, :], feat_h) + mm(loc_h[at, :], feat_l) + mm(loc_l[at, :], feat_h)


def add_features(halo_h, halo_l, s_loc, feat_e, out):
    half = feat_e.shape[0]
    high, low = halves(feat_e[...])
    he, le = halo_h[:, half:], halo_l[:, half:]
    out[...] = s_loc[...] + mm(he, high) + mm(he, low) + mm(le, high)


def spread_forward(halo_h, halo_l, s_loc, feat_i, win_h, win_l, wout_hl, spread_in, scores):
    half = feat_i.shape[0]
    high, low = halves(feat_i[...])
    for start in range(0, half, CHUNK):
        at = pl.ds(start, CHUNK)
        hi, li = halo_h[at, :half], halo_l[at, :half]
        s = s_loc[at, :] + mm(hi, high) + mm(hi, low) + mm(li, high)
        spread_in[at, :] = s
        s_h, s_l = halves(s)
        pre = mm(s_h, win_h[...]) + mm(s_h, win_l[...]) + mm(s_l, win_h[...])
        hid_h, hid_l = halves(0.5 * pre * erfc(-SQRT_HALF * pre))
        scores[at, :] = fold(mm(hid_h, wout_hl[...]) + mm(hid_l, wout_hl[...]))


def beside_forward(loc_h, loc_l, spread_in, scores, win_h, win_l, slope, hid_th, hid_tl, in_th, in_tl, logits_loc, sco_out):
    sco_out[...] = scores[...]
    s = spread_in[...]
    s_h, s_l = halves(s)
    pre = mm(s_h, win_h[...]) + mm(s_h, win_l[...]) + mm(s_l, win_h[...])
    gate = 0.5 * erfc(-SQRT_HALF * pre)
    slope[...] = gate + pre * (INV_SQRT_2PI * jnp.exp(-0.5 * pre * pre))
    high, low = halves((pre * gate).T)
    hid_th[...] = high
    hid_tl[...] = low
    high, low = halves(s.T)
    in_th[...] = high
    in_tl[...] = low
    pair = jnp.concatenate(halves(scores[...]), axis=1)
    logits_loc[...] = fold(mm(loc_h[...], pair) + mm(loc_l[...], pair))


def add_scores(halo_h, halo_l, logits_loc, sco_e, out):
    half = sco_e.shape[0]
    pair = jnp.concatenate(halves(sco_e[...]), axis=1)
    out[...] = logits_loc[...] + fold(mm(halo_h[:, half:], pair) + mm(halo_l[:, half:], pair))


def classify(halo_h, halo_l, logits_loc, sco_i, onehot, logits, grads_t, loss, out):
    half = sco_i.shape[0]
    classes = logits.shape[1]
    pair = jnp.concatenate(halves(sco_i[...]), axis=1)
    wide = mm(halo_h[:, :half], pair) + mm(halo_l[:, :half], pair)
    values = logits_loc[...] + fold(wide)
    logits[...] = values
    totals = jnp.log(jnp.sum(jnp.exp(values), axis=1, keepdims=True))
    hot = onehot[...]
    row_loss = totals - jnp.sum(hot * values, axis=1, keepdims=True)
    loss[...] = jnp.broadcast_to(jnp.sum(row_loss, axis=0, keepdims=True), loss.shape)
    high, low = halves((jnp.exp(values - totals) - hot).T)
    grads = jnp.concatenate([high, low], axis=0)
    grads_t[...] = grads
    tall = mm(grads, halo_h[:, half:]) + mm(grads, halo_l[:, half:])
    out[...] = tall[:classes] + tall[classes:]


def beside_classify(grads_t, halo_h, halo_l, loc_h, loc_l, out, own):
    grads = grads_t[...]
    classes, half = out.shape
    for ref, high, low in ((out, halo_h[:, :half], halo_l[:, :half]), (own, loc_h[...], loc_l[...])):
        tall = mm(grads, high) + mm(grads, low)
        ref[...] = tall[:classes] + tall[classes:]


def backward(ret_near, ret_i, wout_hh, wout_ll, slope, in_th, in_tl, hid_th, hid_tl, loss,
             hidden_grad, keep, give):
    returned = (ret_near[...] + ret_i[...]).T
    pair = jnp.concatenate(halves(returned), axis=1)
    across = ((1,), (1,))
    grad = mm(pair, wout_hh[...], across) + mm(pair, wout_ll[...], across)
    hidden_grad[...] = grad
    pre_h, pre_l = halves(grad * slope[...])
    grad_in = mm(in_th[...], pre_h) + mm(in_th[...], pre_l) + mm(in_tl[...], pre_h)
    grad_out = fold(mm(hid_th[...], pair) + mm(hid_tl[...], pair))
    grad_out = jnp.where(last_element(grad_out), loss[:1, :], grad_out)
    rows = keep.shape[0]
    pieces = [grad_in[:, t : t + LANES] for t in range(0, grad_in.shape[1], LANES)] + [grad_out]
    core = lax.axis_index("c")
    for first, second in ((keep, give), (give, keep)):

        @pl.when(core == (0 if first is keep else 1))
        def _():
            at = 0
            for piece in pieces:
                ref, start = (first, at) if at < rows else (second, at - rows)
                ref[pl.ds(start, piece.shape[0]), :] = piece
                at += piece.shape[0]


def last_element(value):
    row = lax.broadcasted_iota(jnp.int32, value.shape, 0)
    column = lax.broadcasted_iota(jnp.int32, value.shape, 1)
    return (row == value.shape[0] - 1) & (column == value.shape[1] - 1)


def assemble(nodes_total, own, other, grad_in, grad_out, mean_loss):
    deep = grad_in.shape[0]
    rows = own.shape[0]
    core = lax.axis_index("c")
    for first, second in ((own, other), (other, own)):

        @pl.when(core == (0 if first is own else 1))
        def _():
            tiles = grad_in.shape[1] // LANES
            for t in range(tiles):
                at = t * deep
                ref, start = (first, at) if at < rows else (second, at - rows)
                grad_in[:, pl.ds(t * LANES, LANES)] = ref[pl.ds(start, deep), :]
            grad_out[...] = second[pl.ds(tiles * deep - rows, grad_out.shape[0]), :]

    end = pl.ds(grad_out.shape[0] - 8, 8)
    value = grad_out[end, :]
    there = last_element(value)
    mean_loss[0, 0] = jnp.sum(jnp.where(there, value, 0.0)) / nodes_total
    others = jnp.sum(jnp.where(there, 0.0, value), axis=1, keepdims=True)
    grad_out[end, :] = jnp.where(there, -others, value)


def call(body, outs, args, scalars=0, flops=0, scratch=(), space=pltpu.VMEM, name=""):
    smem = pl.BlockSpec(memory_space=pltpu.SMEM)
    vmem = pl.BlockSpec(memory_space=pltpu.VMEM)
    moved = sum(a.size * a.dtype.itemsize for a in args)
    return pl.pallas_call(
        body,
        out_shape=[jax.ShapeDtypeStruct(shape, kind) for shape, kind in outs],
        in_specs=[smem] * scalars + [pl.BlockSpec(memory_space=space)] * (len(args) - scalars),
        out_specs=[smem if shape == (1, 1) else vmem for shape, _ in outs],
        scratch_shapes=scratch,
        cost_estimate=pl.CostEstimate(flops=flops, bytes_accessed=moved, transcendentals=0),
        compiler_params=pltpu.CompilerParams(vmem_limit_bytes=VMEM_LIMIT),
        name=name or body.__name__,
    )(*args)


def per_device(features, adjacency, block_index, block_counts, labels, weight_in, weight_out):
    devices = lax.axis_size(ALL)
    here, slots, rows = adjacency.shape[:3]
    nodes = here * rows
    deep, hid = weight_in.shape
    classes = weight_out.shape[1]

    feat_e = beside(features, devices)
    loc = ((nodes, nodes), BF16)
    halo = ((nodes, 2 * nodes), BF16)
    w_pair = ((hid, 2 * classes), BF16)
    loc_h, loc_l, halo_h, halo_l, s_loc, win_h, win_l, wout_hl, wout_hh, wout_ll, onehot, feat_out = call(
        prepare,
        [loc, loc, halo, halo, ((nodes, deep), F32), ((deep, hid), BF16), ((deep, hid), BF16),
         w_pair, w_pair, w_pair, ((nodes, classes), F32), ((nodes, deep), F32)],
        [pltpu.with_memory_space_constraint(v, pltpu.HBM)
         for v in (block_index, block_counts, adjacency, features, weight_in, weight_out, labels.reshape(1, nodes))],
        scalars=2,
        flops=6 * nodes * nodes * deep,
        scratch=[
            pltpu.VMEM(adjacency.shape, F32),
            pltpu.VMEM(features.shape, F32),
            pltpu.VMEM(weight_in.shape, F32),
            pltpu.VMEM(weight_out.shape, F32),
            pltpu.VMEM((1, nodes), jnp.int32),
            pltpu.VMEM((here, 3 * here, rows, rows), F32),
            pltpu.SemaphoreType.DMA((4 + here * slots,)),
        ],
        space=pltpu.HBM,
    )
    feat_i = mate(feat_out, devices)
    (s_loc,) = call(
        add_features,
        [((nodes, deep), F32)],
        [halo_h, halo_l, s_loc, feat_e],
        flops=6 * nodes * nodes * deep,
    )
    spread_in, scores = call(
        spread_forward,
        [((nodes, deep), F32), ((nodes, classes), F32)],
        [halo_h, halo_l, s_loc, feat_i, win_h, win_l, wout_hl],
        flops=20 * nodes * nodes * deep,
    )
    sco_e = beside(scores, devices)
    slope, hid_th, hid_tl, in_th, in_tl, logits_loc, sco_out = call(
        beside_forward,
        [((nodes, hid), F32), ((hid, nodes), BF16), ((hid, nodes), BF16), ((deep, nodes), BF16), ((deep, nodes), BF16),
         ((nodes, classes), F32), ((nodes, classes), F32)],
        [loc_h, loc_l, spread_in, scores, win_h, win_l],
        flops=12 * nodes * nodes * deep,
    )
    sco_i = mate(sco_out, devices)
    (logits_loc,) = call(
        add_scores,
        [((nodes, classes), F32)],
        [halo_h, halo_l, logits_loc, sco_e],
        flops=8 * nodes * nodes * classes,
    )
    logits, grads_t, loss, out_e = call(
        classify,
        [((nodes, classes), F32), ((2 * classes, nodes), BF16), ((8, LANES), F32), ((classes, nodes), F32)],
        [halo_h, halo_l, logits_loc, sco_i, onehot],
        flops=12 * nodes * nodes * classes,
    )
    ret_e = beside(out_e, devices)
    out_i, ret_loc = call(
        beside_classify,
        [((classes, nodes), F32), ((classes, nodes), F32)],
        [grads_t, halo_h, halo_l, loc_h, loc_l],
        flops=16 * nodes * nodes * classes,
    )
    ret_i = mate(out_i, devices)
    ret_near = ret_loc + ret_e
    half = (deep * hid + hid * classes) // LANES // 2
    hidden_grad, keep, give = call(
        backward,
        [((nodes, hid), F32), ((half, LANES), F32), ((half, LANES), F32)],
        [ret_near, ret_i, wout_hh, wout_ll, slope, in_th, in_tl, hid_th, hid_tl, loss],
        flops=12 * nodes * nodes * deep,
    )
    big, mid = lax.axis_size(BIG), lax.axis_size(MID)
    mine = (keep + mate(give, devices)).reshape(big, half // big, LANES)
    summed = jnp.sum(exchange(mine, BIG), axis=0)
    summed = jnp.sum(exchange(spread(summed, mid), MID), axis=0)
    own = exchange(spread(summed, big), BIG).reshape(half, LANES)
    other = mate(own, devices)
    grad_in, grad_out, mean_loss = call(
        functools.partial(assemble, nodes * devices),
        [((deep, hid), F32), ((hid, classes), F32), ((1, 1), F32)],
        [own, other],
        name="assemble",
    )
    return (logits, mean_loss.reshape(()), hidden_grad, grad_in, grad_out)


def solution(mesh):
    grid = Mesh(mesh.devices.reshape(4, 8, 8, 2), ALL)
    split = P(ALL)
    return jax.shard_map(
        per_device,
        mesh=grid,
        in_specs=(split, split, split, split, split, P(), P()),
        out_specs=(split, P(), split, P(), P()),
        check_vma=False,
    )
```

time: 128 us -> 117 us (0.914)
  local copies, waits for them, and re-layouts: 6.17 us -> 0.04 us
  starting transfers between devices: 31.5 us -> 27.2 us
  between operations: 2.62 us -> 0.8 us
  Pallas kernels: 15.1 us -> 16.8 us
    unnamed x10 -> x0, local copies, waits for them, and re-layouts: 5.6 us -> none
    ppermute x5, starting transfers between devices: 21.7 us -> 17.7 us  [mate(): return lax.ppermute(value, ALL, [(i, i ^ 1) for i in range(devices)])]
    ppermute x5, waiting for transfers between devices: 1.86 us -> 3.94 us  [mate(): return lax.ppermute(value, ALL, [(i, i ^ 1) for i in range(devices)])]
    ppermute x3, waiting for transfers between devices: 5.51 us -> 3.79 us  [beside(): return lax.ppermute(value, ALL, pairs + [(b, a) for a, b in pairs])]
    pallas_call x7 -> x9, Pallas kernels: 15.1 us -> 16.8 us  [call(): pl.pallas_call(body, out_shape=[jax.ShapeDtypeStruct(shape, kind) for sha...]
  transfers between devices with their start and end apart: 8 -> 8, of which waited for: 4 -> 5; matrix products, arithmetic and copies ran while one was open for 1% -> 0% of each run, Pallas kernels for 4% -> 7%
where the time goes in v3:
time: 117 us; the launch traced here: 116 us
  blocking collectives  63.4 us (54%)
  starting transfers between devices  27.2 us (23%)
  Pallas kernels  16.8 us (14%)
  waiting for transfers between devices  7.73 us (7%)
    all_to_all x3, blocking collectives, exchange(): return lax.all_to_all(value, axes, 0, 0, tiled=True)  63.4 us
    ppermute x5, starting transfers between devices, mate(): return lax.ppermute(value, ALL, [(i, i ^ 1) for i in range(devices)])  17.7 us
    pallas_call x9, Pallas kernels, call(): pl.pallas_call(body, out_shape=[jax.ShapeDtypeStruct(shape, kind) for sha...  16.8 us
    ppermute x3, starting transfers between devices, beside(): return lax.ppermute(value, ALL, pairs + [(b, a) for a, b in pairs])  9.47 us
    ppermute x5, waiting for transfers between devices, mate(): return lax.ppermute(value, ALL, [(i, i ^ 1) for i in range(devices)])  3.94 us
    ppermute x3, waiting for transfers between devices, beside(): return lax.ppermute(value, ALL, pairs + [(b, a) for a, b in pairs])  3.79 us
  transfers between devices with their start and end apart: 8, of which 5 were waited for; matrix products, arithmetic and copies ran while one was open for 0% of the time, Pallas kernels for 7%

profile of v3, /device:TPU:1, one launch (start us, length us, event | category | flops | bytes accessed | tf_op | source)
XLA Modules:
  0.0 116.1 jit_solution(8563364385760270999)
XLA Ops:
  0.6 4.6 %collective-permute-start = (f32[512,256]{1,0:T(8,128)}, f32[512,256]{1,0:T(8,128)S(1)}, u32[]{:S(2)}, u32[]{:S(2)}) collective-permute-start(f32[512,256]{1,0:T(8,128)} %features.1), channel_id=1, source_target_pairs={{1,2},{3,4},{5,6},{7,8},{9,10},{11,12},{13,14},{15,16},{17,18},{19... | collective-permute-start | bytes 1572872 | tf_op jit(solution)/shard_map/ppermute | solution.py:28
  5.2 4.5 %prepare.1 = (bf16[512,512]{1,0:T(8,128)(2,1)S(1)}, bf16[512,512]{1,0:T(8,128)(2,1)S(1)}, bf16[512,1024]{1,0:T(8,128)(2,1)S(1)}, bf16[512,1024]{1,0:T(8,128)(2,1...) custom-call(s32[2,6]{1,0:T(2,128)} %block_index.1, ...), custom_call_target="tpu_custom_call" | custom-call | flops 402653184 | bytes 4458552 | tf_op jit(solution)/shard_map/prepare/pallas_call | solution.py:252
  9.8 4.8 %collective-permute-start.1 = (f32[512,256]{1,0:T(8,128)S(1)}, f32[512,256]{1,0:T(8,128)S(1)}, u32[]{:S(2)}, u32[]{:S(2)}) collective-permute-start(f32[512,256]{1,0:T(8,128)S(1)} %get-tuple-element.43), channel_id=1, source_target_pairs={{0,1},{1,0},{2,3},{3,2},{4,5},{5,4},{6,7},{7,6},{8,9},{9,8},{10,11... | collective-permute-start | bytes 1572872 | tf_op jit(solution)/shard_map/ppermute | solution.py:23
  14.6 0.0 collective-permute-done.feat_e
  14.6 0.6 add_features.1.s_loc
  15.2 0.9 collective-permute-done.1.feat_i
  16.1 3.1 %spread_forward.1 = (f32[512,256]{1,0:T(8,128)S(1)}, f32[512,128]{1,0:T(8,128)S(1)}) custom-call(bf16[512,1024]{1,0:T(8,128)(2,1)S(1)} %get-tuple-element.38.halo_h, bf16[512,1024]{1,0:T(8,128)(2,1)S(1)} %get-tuple-element.39.halo_l, f32[512,256]{1,0:T(8,128)S(1)} %add_features.1.s_loc, f32[512,256]{1,0:T(8,128)S(1)} %collective-permute-done.1.feat_i, ...), custom_call_target="tpu_custom_call" | custom-call | flops 1342177280 | bytes 3932160 | tf_op jit(solution)/shard_map/spread_forward/pallas_call | solution.py:252
  19.3 1.9 %collective-permute-start.2 = (f32[512,128]{1,0:T(8,128)S(1)}, f32[512,128]{1,0:T(8,128)S(1)}, u32[]{:S(2)}, u32[]{:S(2)}) collective-permute-start(f32[512,128]{1,0:T(8,128)S(1)} %get-tuple-element.48.scores), channel_id=1, source_target_pairs={{1,2},{3,4},{5,6},{7,8},{9,10},{11,12},{13,14},{15,16},{17,18},{19... | collective-permute-start | bytes 786440 | tf_op jit(solution)/shard_map/ppermute | solution.py:28
  21.2 2.1 %beside_forward.1 = (f32[512,512]{1,0:T(8,128)S(1)}, bf16[512,512]{1,0:T(8,128)(2,1)S(1)}, bf16[512,512]{1,0:T(8,128)(2,1)S(1)}, bf16[256,512]{1,0:T(8,128)(2,1)...) custom-call(bf16[512,512]{1,0:T(8,128)(2,1)S(1)} %get-tuple-element.40.loc_h, ...), custom_call_target="tpu_custom_call" | custom-call | flops 805306368 | bytes 2359296 | tf_op jit(solution)/shard_map/beside_forward/pallas_call | solution.py:252
  23.3 1.9 %collective-permute-start.3 = (f32[512,128]{1,0:T(8,128)S(1)}, f32[512,128]{1,0:T(8,128)S(1)}, u32[]{:S(2)}, u32[]{:S(2)}) collective-permute-start(f32[512,128]{1,0:T(8,128)S(1)} %get-tuple-element.50), channel_id=1, source_target_pairs={{0,1},{1,0},{2,3},{3,2},{4,5},{5,4},{6,7},{7,6},{8,9},{9,8},{10,11... | collective-permute-start | bytes 786440 | tf_op jit(solution)/shard_map/ppermute | solution.py:23
  25.2 1.7 %collective-permute-done.2.sco_e = f32[512,128]{1,0:T(8,128)S(1)} collective-permute-done((f32[512,128]{1,0:T(8,128)S(1)}, f32[512,128]{1,0:T(8,128)S(1)}, u32[]{:S(2)}, u32[]{:S(2)}) %collective-permute-start.2) | collective-permute-done | bytes 262176 | tf_op jit(solution)/shard_map/ppermute | solution.py:28
  27.0 0.4 add_scores.1.logits_loc
  27.4 0.0 collective-permute-done.3.sco_i
  27.4 1.7 %classify.1 = (f32[512,128]{1,0:T(8,128)}, bf16[256,512]{1,0:T(8,128)(2,1)S(1)}, f32[8,128]{1,0:T(8,128)S(1)}, f32[128,512]{1,0:T(8,128)S(1)}) custom-call(bf16[512,1024]{1,0:T(8,128)(2,1)S(1)} %get-tuple-element.38.halo_h, bf16[512,1024]{1,0:T(8,128)(2,1)S(1)} %get-tuple-element.39.halo_l, f32[512,128]{1,0:T(8,128)S(1)} %add_scores.1.logits_loc, ...), custom_call_target="tpu_custom_call" | custom-call | flops 402653184 | bytes 2883584 | tf_op jit(solution)/shard_map/classify/pallas_call | solution.py:252
  29.1 3.0 %collective-permute-start.4 = (f32[128,512]{1,0:T(8,128)S(1)}, f32[128,512]{1,0:T(8,128)S(1)}, u32[]{:S(2)}, u32[]{:S(2)}) collective-permute-start(f32[128,512]{1,0:T(8,128)S(1)} %get-tuple-element.55), channel_id=1, source_target_pairs={{1,2},{3,4},{5,6},{7,8},{9,10},{11,12},{13,14},{15,16},{17,18},{19... | collective-permute-start | bytes 786440 | tf_op jit(solution)/shard_map/ppermute | solution.py:28
  32.0 0.7 beside_classify.1
  32.8 1.9 %collective-permute-start.5 = (f32[128,512]{1,0:T(8,128)S(1)}, f32[128,512]{1,0:T(8,128)S(1)}, u32[]{:S(2)}, u32[]{:S(2)}) collective-permute-start(f32[128,512]{1,0:T(8,128)S(1)} %get-tuple-element.56), channel_id=1, source_target_pairs={{0,1},{1,0},{2,3},{3,2},{4,5},{5,4},{6,7},{7,6},{8,9},{9,8},{10,11... | collective-permute-start | bytes 786440 | tf_op jit(solution)/shard_map/ppermute | solution.py:23
  34.7 2.1 %collective-permute-done.4 = f32[128,512]{1,0:T(8,128)S(1)} collective-permute-done((f32[128,512]{1,0:T(8,128)S(1)}, f32[128,512]{1,0:T(8,128)S(1)}, u32[]{:S(2)}, u32[]{:S(2)}) %collective-permute-start.4) | collective-permute-done | bytes 262176 | tf_op jit(solution)/shard_map/ppermute | solution.py:28
  36.8 0.0 collective-permute-done.5.ret_i
  36.8 2.7 %backward.1 = (f32[512,512]{1,0:T(8,128)}, f32[768,128]{1,0:T(8,128)S(1)}, f32[768,128]{1,0:T(8,128)S(1)}) custom-call(f32[128,512]{1,0:T(8,128)S(1)} %add.6.ret_near, f32[128,512]{1,0:T(8,128)S(1)} %collective-permute-done.5.ret_i, bf16[512,256]{1,0:T(8,128)(2,1)S(1)} %get-tuple-element.57.wout_hh, bf16[512,256]{1,0:T(8,128)(2,1)S(1)} %get-tuple-element.58.wout_ll, ...), custom_call_target="tpu_custom_call" | custom-call | flops 805306368 | bytes 3674112 | tf_op jit(solution)/shard_map/backward/pallas_call | solution.py:252
  39.5 1.9 %collective-permute-start.6 = (f32[768,128]{1,0:T(8,128)S(1)}, f32[768,128]{1,0:T(8,128)S(1)}, u32[]{:S(2)}, u32[]{:S(2)}) collective-permute-start(f32[768,128]{1,0:T(8,128)S(1)} %get-tuple-element.66), channel_id=1, source_target_pairs={{0,1},{1,0},{2,3},{3,2},{4,5},{5,4},{6,7},{7,6},{8,9},{9,8},{10,11... | collective-permute-start | bytes 1179656 | tf_op jit(solution)/shard_map/ppermute | solution.py:23
  41.4 1.7 %collective-permute-done.6 = f32[768,128]{1,0:T(8,128)S(1)} collective-permute-done((f32[768,128]{1,0:T(8,128)S(1)}, f32[768,128]{1,0:T(8,128)S(1)}, u32[]{:S(2)}, u32[]{:S(2)}) %collective-permute-start.6) | collective-permute-done | bytes 393248 | tf_op jit(solution)/shard_map/ppermute | solution.py:23
  43.1 32.1 %all_to_all.15 = f32[32,24,128]{2,1,0:T(8,128)S(1)} all-to-all(f32[32,24,128]{2,1,0:T(8,128)S(1)} %bitcast.6), channel_id=1, replica_groups=mesh['x'=4,'z'=8,'y'=8,'c'=2] {'x','y'}, dimensions={0} | all-to-all | bytes 786432 | tf_op jit(solution)/shard_map/all_to_all | solution.py:32
  75.2 14.0 %all_to_all.16 = f32[8,24,128]{2,1,0:T(8,128)S(1)} all-to-all(f32[8,24,128]{2,1,0:T(8,128)S(1)} %broadcast_in_dim.4), channel_id=1, replica_groups=mesh['x'=4,'z'=8,'y'=8,'c'=2] {'z'}, dimensions={0} | all-to-all | bytes 196608 | tf_op jit(solution)/shard_map/all_to_all | solution.py:32
  89.3 17.3 %all_to_all.17 = f32[32,24,128]{2,1,0:T(8,128)S(1)} all-to-all(f32[32,24,128]{2,1,0:T(8,128)S(1)} %broadcast_in_dim.5), channel_id=1, replica_groups=mesh['x'=4,'z'=8,'y'=8,'c'=2] {'x','y'}, dimensions={0} | all-to-all | bytes 786432 | tf_op jit(solution)/shard_map/all_to_all | solution.py:32
  106.7 7.2 %collective-permute-start.7 = (f32[768,128]{1,0:T(8,128)S(1)}, f32[768,128]{1,0:T(8,128)S(1)}, u32[]{:S(2)}, u32[]{:S(2)}) collective-permute-start(f32[768,128]{1,0:T(8,128)S(1)} %bitcast.4), channel_id=1, source_target_pairs={{0,1},{1,0},{2,3},{3,2},{4,5},{5,4},{6,7},{7,6},{8,9},{9,8},{10,11... | collective-permute-start | bytes 1179656 | tf_op jit(solution)/shard_map/ppermute | solution.py:23
  113.8 1.3 %collective-permute-done.7.other = f32[768,128]{1,0:T(8,128)S(1)} collective-permute-done((f32[768,128]{1,0:T(8,128)S(1)}, f32[768,128]{1,0:T(8,128)S(1)}, u32[]{:S(2)}, u32[]{:S(2)}) %collective-permute-start.7) | collective-permute-done | bytes 393248 | tf_op jit(solution)/shard_map/ppermute | solution.py:23
  115.1 1.0 assemble.1
  (6 shorter events, 0.2 us)
Async XLA Ops:
  0.6 14.0 %collective-permute-start = (f32[512,256]{1,0:T(8,128)}, f32[512,256]{1,0:T(8,128)S(1)}, u32[]{:S(2)}, u32[]{:S(2)}) collective-permute-start(f32[512,256]{1,0:T(8,128)} %features.1), channel_id=1, source_target_pairs={{1,2},{3,4},{5,6},{7,8},{9,10},{11,12},{13,14},{15,16},{17,18},{19... | collective-permute-start | bytes 1572872 | tf_op jit(solution)/shard_map/ppermute | solution.py:28
  9.8 6.3 %collective-permute-start.1 = (f32[512,256]{1,0:T(8,128)S(1)}, f32[512,256]{1,0:T(8,128)S(1)}, u32[]{:S(2)}, u32[]{:S(2)}) collective-permute-start(f32[512,256]{1,0:T(8,128)S(1)} %get-tuple-element.43), channel_id=1, source_target_pairs={{0,1},{1,0},{2,3},{3,2},{4,5},{5,4},{6,7},{7,6},{8,9},{9,8},{10,11... | collective-permute-start | bytes 1572872 | tf_op jit(solution)/shard_map/ppermute | solution.py:23
  19.3 7.7 %collective-permute-start.2 = (f32[512,128]{1,0:T(8,128)S(1)}, f32[512,128]{1,0:T(8,128)S(1)}, u32[]{:S(2)}, u32[]{:S(2)}) collective-permute-start(f32[512,128]{1,0:T(8,128)S(1)} %get-tuple-element.48.scores), channel_id=1, source_target_pairs={{1,2},{3,4},{5,6},{7,8},{9,10},{11,12},{13,14},{15,16},{17,18},{19... | collective-permute-start | bytes 786440 | tf_op jit(solution)/shard_map/ppermute | solution.py:28
  23.3 4.1 %collective-permute-start.3 = (f32[512,128]{1,0:T(8,128)S(1)}, f32[512,128]{1,0:T(8,128)S(1)}, u32[]{:S(2)}, u32[]{:S(2)}) collective-permute-start(f32[512,128]{1,0:T(8,128)S(1)} %get-tuple-element.50), channel_id=1, source_target_pairs={{0,1},{1,0},{2,3},{3,2},{4,5},{5,4},{6,7},{7,6},{8,9},{9,8},{10,11... | collective-permute-start | bytes 786440 | tf_op jit(solution)/shard_map/ppermute | solution.py:23
  29.1 7.7 %collective-permute-start.4 = (f32[128,512]{1,0:T(8,128)S(1)}, f32[128,512]{1,0:T(8,128)S(1)}, u32[]{:S(2)}, u32[]{:S(2)}) collective-permute-start(f32[128,512]{1,0:T(8,128)S(1)} %get-tuple-element.55), channel_id=1, source_target_pairs={{1,2},{3,4},{5,6},{7,8},{9,10},{11,12},{13,14},{15,16},{17,18},{19... | collective-permute-start | bytes 786440 | tf_op jit(solution)/shard_map/ppermute | solution.py:28
  32.8 4.0 %collective-permute-start.5 = (f32[128,512]{1,0:T(8,128)S(1)}, f32[128,512]{1,0:T(8,128)S(1)}, u32[]{:S(2)}, u32[]{:S(2)}) collective-permute-start(f32[128,512]{1,0:T(8,128)S(1)} %get-tuple-element.56), channel_id=1, source_target_pairs={{0,1},{1,0},{2,3},{3,2},{4,5},{5,4},{6,7},{7,6},{8,9},{9,8},{10,11... | collective-permute-start | bytes 786440 | tf_op jit(solution)/shard_map/ppermute | solution.py:23
  39.5 3.6 %collective-permute-start.6 = (f32[768,128]{1,0:T(8,128)S(1)}, f32[768,128]{1,0:T(8,128)S(1)}, u32[]{:S(2)}, u32[]{:S(2)}) collective-permute-start(f32[768,128]{1,0:T(8,128)S(1)} %get-tuple-element.66), channel_id=1, source_target_pairs={{0,1},{1,0},{2,3},{3,2},{4,5},{5,4},{6,7},{7,6},{8,9},{9,8},{10,11... | collective-permute-start | bytes 1179656 | tf_op jit(solution)/shard_map/ppermute | solution.py:23
  106.7 8.5 %collective-permute-start.7 = (f32[768,128]{1,0:T(8,128)S(1)}, f32[768,128]{1,0:T(8,128)S(1)}, u32[]{:S(2)}, u32[]{:S(2)}) collective-permute-start(f32[768,128]{1,0:T(8,128)S(1)} %bitcast.4), channel_id=1, source_target_pairs={{0,1},{1,0},{2,3},{3,2},{4,5},{5,4},{6,7},{7,6},{8,9},{9,8},{10,11... | collective-permute-start | bytes 1179656 | tf_op jit(solution)/shard_map/ppermute | solution.py:23

commit v4 on v3

--- a/solution.py
+++ b/solution.py
@@ -1,15 +1,17 @@
 import functools
+import math
 
 import jax
 import jax.numpy as jnp
+import numpy as np
 from jax import lax
 from jax.experimental import pallas as pl
 from jax.experimental.pallas import tpu as pltpu
-from jax.sharding import Mesh, PartitionSpec as P
-
-ALL = ("x", "z", "y", "c")
-BIG = ("x", "y")
-MID = ("z",)
+from jax.sharding import PartitionSpec as P
+
+AXIS = "rows"
+GRID = (4, 8, 8, 2)
+X, Z, Y = range(3)
 LANES = 128
 F32 = jnp.float32
 BF16 = jnp.bfloat16
@@ -19,28 +21,31 @@
 INV_SQRT_2PI = 0.3989422804014327
 
 
-def mate(value, devices):
-    return lax.ppermute(value, ALL, [(i, i ^ 1) for i in range(devices)])
-
-
-def beside(value, devices):
-    pairs = [(i, i + 1) for i in range(1, devices - 1, 2)]
-    return lax.ppermute(value, ALL, pairs + [(b, a) for a, b in pairs])
-
-
-def exchange(value, axes):
-    return lax.all_to_all(value, axes, 0, 0, tiled=True)
+def mate(value):
+    return lax.ppermute(value, AXIS, [(i, i ^ 1) for i in range(lax.axis_size(AXIS))])
+
+
+def beside(value):
+    pairs = [(i, i + 1) for i in range(1, lax.axis_size(AXIS) - 1, 2)]
+    return lax.ppermute(value, AXIS, pairs + [(b, a) for a, b in pairs])
+
+
+def groups(*per_core):
+    ids = np.arange(math.prod(GRID)).reshape(GRID)
+    found = []
+    for core, axes in enumerate(per_core):
+        rest = [axis for axis in range(3) if axis not in axes]
+        size = math.prod(GRID[axis] for axis in axes)
+        found += ids[..., core].transpose(rest + list(axes)).reshape(-1, size).tolist()
+    return found
+
+
+def exchange(value, members):
+    return lax.all_to_all(value, AXIS, 0, 0, axis_index_groups=members, tiled=True)
 
 
 def spread(value, count):
     return jnp.broadcast_to(value[None], (count,) + value.shape)
-
-
-def position():
-    place = 0
-    for axis in ALL:
-        place = place * lax.axis_size(axis) + lax.axis_index(axis)
-    return place
 
 
 def halves(value):
@@ -77,8 +82,9 @@
     moves = [pltpu.make_async_copy(source, target, sems.at[i]) for i, (source, target) in enumerate(moves)]
     for move in moves:
         move.start()
-    core = lax.axis_index("c")
-    first = position() * here
+    me = lax.axis_index(AXIS)
+    core = lax.rem(me, 2)
+    first = me * here
     band[...] = jnp.zeros_like(band)
     for move in moves[:4]:
         move.wait()
@@ -165,7 +171,7 @@
     out[...] = logits_loc[...] + fold(mm(halo_h[:, half:], pair) + mm(halo_l[:, half:], pair))
 
 
-def classify(halo_h, halo_l, logits_loc, sco_i, onehot, logits, grads_t, loss, out):
+def classify(halo_h, halo_l, logits_loc, sco_i, onehot, logits, grads_t, out):
     half = sco_i.shape[0]
     classes = logits.shape[1]
     pair = jnp.concatenate(halves(sco_i[...]), axis=1)
@@ -173,47 +179,39 @@
     values = logits_loc[...] + fold(wide)
     logits[...] = values
     totals = jnp.log(jnp.sum(jnp.exp(values), axis=1, keepdims=True))
-    hot = onehot[...]
-    row_loss = totals - jnp.sum(hot * values, axis=1, keepdims=True)
-    loss[...] = jnp.broadcast_to(jnp.sum(row_loss, axis=0, keepdims=True), loss.shape)
-    high, low = halves((jnp.exp(values - totals) - hot).T)
+    high, low = halves((jnp.exp(values - totals) - onehot[...]).T)
     grads = jnp.concatenate([high, low], axis=0)
     grads_t[...] = grads
     tall = mm(grads, halo_h[:, half:]) + mm(grads, halo_l[:, half:])
     out[...] = tall[:classes] + tall[classes:]
 
 
-def beside_classify(grads_t, halo_h, halo_l, loc_h, loc_l, out, own):
+def beside_classify(grads_t, halo_h, halo_l, loc_h, loc_l, values, onehot, out, own, logits, loss):
     grads = grads_t[...]
     classes, half = out.shape
     for ref, high, low in ((out, halo_h[:, :half], halo_l[:, :half]), (own, loc_h[...], loc_l[...])):
         tall = mm(grads, high) + mm(grads, low)
         ref[...] = tall[:classes] + tall[classes:]
-
-
-def backward(ret_near, ret_i, wout_hh, wout_ll, slope, in_th, in_tl, hid_th, hid_tl, loss,
-             hidden_grad, keep, give):
-    returned = (ret_near[...] + ret_i[...]).T
-    pair = jnp.concatenate(halves(returned), axis=1)
-    across = ((1,), (1,))
-    grad = mm(pair, wout_hh[...], across) + mm(pair, wout_ll[...], across)
-    hidden_grad[...] = grad
-    pre_h, pre_l = halves(grad * slope[...])
-    grad_in = mm(in_th[...], pre_h) + mm(in_th[...], pre_l) + mm(in_tl[...], pre_h)
-    grad_out = fold(mm(hid_th[...], pair) + mm(hid_tl[...], pair))
-    grad_out = jnp.where(last_element(grad_out), loss[:1, :], grad_out)
-    rows = keep.shape[0]
-    pieces = [grad_in[:, t : t + LANES] for t in range(0, grad_in.shape[1], LANES)] + [grad_out]
-    core = lax.axis_index("c")
-    for first, second in ((keep, give), (give, keep)):
-
-        @pl.when(core == (0 if first is keep else 1))
-        def _():
-            at = 0
-            for piece in pieces:
-                ref, start = (first, at) if at < rows else (second, at - rows)
-                ref[pl.ds(start, piece.shape[0]), :] = piece
-                at += piece.shape[0]
+    scores = values[...]
+    logits[...] = scores
+    totals = jnp.log(jnp.sum(jnp.exp(scores), axis=1, keepdims=True))
+    row_loss = totals - jnp.sum(onehot[...] * scores, axis=1, keepdims=True)
+    loss[...] = jnp.broadcast_to(jnp.sum(row_loss, axis=0, keepdims=True), loss.shape)
+
+
+def gradient_half(which, in_th, in_tl, hid_th, hid_tl, pre_h, pre_l, pair, loss, out):
+    deep = in_th.shape[0] // 2
+    hid = hid_th.shape[0] // 2
+    at = pl.ds(pl.multiple_of(which * deep, deep), deep)
+    high, low = in_th[at, :], in_tl[at, :]
+    tall = mm(jnp.concatenate([high, low], axis=0), pre_h)
+    grad_in = tall[:deep] + tall[deep:] + mm(high, pre_l)
+    for t in range(grad_in.shape[1] // LANES):
+        out[pl.ds(t * deep, deep), :] = grad_in[:, t * LANES : (t + 1) * LANES]
+    at = pl.ds(pl.multiple_of(which * hid, hid), hid)
+    grad_out = fold(mm(hid_th[at, :], pair) + mm(hid_tl[at, :], pair))
+    grad_out = jnp.where(last_element(grad_out) & (which == 1), loss[:1, :], grad_out)
+    out[pl.ds(out.shape[0] - hid, hid), :] = grad_out
 
 
 def last_element(value):
@@ -222,38 +220,66 @@
     return (row == value.shape[0] - 1) & (column == value.shape[1] - 1)
 
 
-def assemble(nodes_total, own, other, grad_in, grad_out, mean_loss):
-    deep = grad_in.shape[0]
-    rows = own.shape[0]
-    core = lax.axis_index("c")
-    for first, second in ((own, other), (other, own)):
-
-        @pl.when(core == (0 if first is own else 1))
-        def _():
-            tiles = grad_in.shape[1] // LANES
-            for t in range(tiles):
-                at = t * deep
-                ref, start = (first, at) if at < rows else (second, at - rows)
-                grad_in[:, pl.ds(t * LANES, LANES)] = ref[pl.ds(start, deep), :]
-            grad_out[...] = second[pl.ds(tiles * deep - rows, grad_out.shape[0]), :]
-
-    end = pl.ds(grad_out.shape[0] - 8, 8)
-    value = grad_out[end, :]
-    there = last_element(value)
-    mean_loss[0, 0] = jnp.sum(jnp.where(there, value, 0.0)) / nodes_total
-    others = jnp.sum(jnp.where(there, 0.0, value), axis=1, keepdims=True)
-    grad_out[end, :] = jnp.where(there, -others, value)
-
-
-def call(body, outs, args, scalars=0, flops=0, scratch=(), space=pltpu.VMEM, name=""):
+def backward(ret_near, ret_i, wout_hh, wout_ll, slope, in_th, in_tl, hid_th, hid_tl, loss,
+             grad, pre_h, pre_l, pair, give):
+    returned = (ret_near[...] + ret_i[...]).T
+    both = jnp.concatenate(halves(returned), axis=1)
+    pair[...] = both
+    across = ((1,), (1,))
+    hidden_grad = mm(both, wout_hh[...], across) + mm(both, wout_ll[...], across)
+    grad[...] = hidden_grad
+    high, low = halves(hidden_grad * slope[...])
+    pre_h[...] = high
+    pre_l[...] = low
+    other = 1 - lax.rem(lax.axis_index(AXIS), 2)
+    gradient_half(other, in_th, in_tl, hid_th, hid_tl, high, low, both, loss, give)
+
+
+def beside_backward(grad, pre_h, pre_l, pair, in_th, in_tl, hid_th, hid_tl, loss, hidden_grad, keep):
+    hidden_grad[...] = grad[...]
+    core = lax.rem(lax.axis_index(AXIS), 2)
+    gradient_half(core, in_th, in_tl, hid_th, hid_tl, pre_h[...], pre_l[...], pair[...], loss, keep)
+
+
+def assemble(nodes_total, own, other, grad_in, grad_out, mean_loss, ends, sems):
+    deep = grad_in.shape[0] // 2
+    hid = grad_out.shape[0] // 2
+    tiles = grad_in.shape[1] // LANES
+    core = lax.rem(lax.axis_index(AXIS), 2)
+    moves = []
+
+    def move(source, target):
+        moves.append(pltpu.make_async_copy(source, target, sems.at[len(moves)]))
+        moves[-1].start()
+
+    for k, (half, which) in enumerate(((own, core), (other, 1 - core))):
+        rows = pl.ds(pl.multiple_of(which * deep, deep), deep)
+        for t in range(tiles):
+            move(half.at[pl.ds(t * deep, deep), :], grad_in.at[rows, pl.ds(t * LANES, LANES)])
+        start = pl.multiple_of(which * hid, hid)
+        move(half.at[pl.ds(tiles * deep, hid - 8), :], grad_out.at[pl.ds(start, hid - 8), :])
+        value = half[pl.ds(tiles * deep + hid - 8, 8), :]
+        there = last_element(value) & (which == 1)
+        loss = jnp.sum(jnp.where(there, value, 0.0))
+        others = jnp.sum(jnp.where(there, 0.0, value), axis=1, keepdims=True)
+        ends[k] = jnp.where(there, -others, value)
+        move(ends.at[k], grad_out.at[pl.ds(start + hid - 8, 8), :])
+        if k == 0:
+            total = loss
+    mean_loss[0, 0] = (total + loss) / nodes_total
+    for copy in moves:
+        copy.wait()
+
+
+def call(body, outs, args, scalars=0, flops=0, scratch=(), space=pltpu.VMEM, out_space=pltpu.VMEM, name=""):
     smem = pl.BlockSpec(memory_space=pltpu.SMEM)
-    vmem = pl.BlockSpec(memory_space=pltpu.VMEM)
+    out_spec = pl.BlockSpec(memory_space=out_space)
     moved = sum(a.size * a.dtype.itemsize for a in args)
     return pl.pallas_call(
         body,
         out_shape=[jax.ShapeDtypeStruct(shape, kind) for shape, kind in outs],
         in_specs=[smem] * scalars + [pl.BlockSpec(memory_space=space)] * (len(args) - scalars),
-        out_specs=[smem if shape == (1, 1) else vmem for shape, _ in outs],
+        out_specs=[smem if shape == (1, 1) else out_spec for shape, _ in outs],
         scratch_shapes=scratch,
         cost_estimate=pl.CostEstimate(flops=flops, bytes_accessed=moved, transcendentals=0),
         compiler_params=pltpu.CompilerParams(vmem_limit_bytes=VMEM_LIMIT),
@@ -262,13 +288,12 @@
 
 
 def per_device(features, adjacency, block_index, block_counts, labels, weight_in, weight_out):
-    devices = lax.axis_size(ALL)
     here, slots, rows = adjacency.shape[:3]
     nodes = here * rows
     deep, hid = weight_in.shape
     classes = weight_out.shape[1]
 
-    feat_e = beside(features, devices)
+    feat_e = beside(features)
     loc = ((nodes, nodes), BF16)
     halo = ((nodes, 2 * nodes), BF16)
     w_pair = ((hid, 2 * classes), BF16)
@@ -291,7 +316,7 @@
         ],
         space=pltpu.HBM,
     )
-    feat_i = mate(feat_out, devices)
+    feat_i = mate(feat_out)
     (s_loc,) = call(
         add_features,
         [((nodes, deep), F32)],
@@ -304,7 +329,7 @@
         [halo_h, halo_l, s_loc, feat_i, win_h, win_l, wout_hl],
         flops=20 * nodes * nodes * deep,
     )
-    sco_e = beside(scores, devices)
+    sco_e = beside(scores)
     slope, hid_th, hid_tl, in_th, in_tl, logits_loc, sco_out = call(
         beside_forward,
         [((nodes, hid), F32), ((hid, nodes), BF16), ((hid, nodes), BF16), ((deep, nodes), BF16), ((deep, nodes), BF16),
@@ -312,56 +337,67 @@
         [loc_h, loc_l, spread_in, scores, win_h, win_l],
         flops=12 * nodes * nodes * deep,
     )
-    sco_i = mate(sco_out, devices)
+    sco_i = mate(sco_out)
     (logits_loc,) = call(
         add_scores,
         [((nodes, classes), F32)],
         [halo_h, halo_l, logits_loc, sco_e],
         flops=8 * nodes * nodes * classes,
     )
-    logits, grads_t, loss, out_e = call(
+    values, grads_t, out_e = call(
         classify,
-        [((nodes, classes), F32), ((2 * classes, nodes), BF16), ((8, LANES), F32), ((classes, nodes), F32)],
+        [((nodes, classes), F32), ((2 * classes, nodes), BF16), ((classes, nodes), F32)],
         [halo_h, halo_l, logits_loc, sco_i, onehot],
         flops=12 * nodes * nodes * classes,
     )
-    ret_e = beside(out_e, devices)
-    out_i, ret_loc = call(
+    ret_e = beside(out_e)
+    out_i, ret_loc, logits, loss = call(
         beside_classify,
-        [((classes, nodes), F32), ((classes, nodes), F32)],
-        [grads_t, halo_h, halo_l, loc_h, loc_l],
+        [((classes, nodes), F32), ((classes, nodes), F32), ((nodes, classes), F32), ((8, LANES), F32)],
+        [grads_t, halo_h, halo_l, loc_h, loc_l, values, onehot],
         flops=16 * nodes * nodes * classes,
     )
-    ret_i = mate(out_i, devices)
+    ret_i = mate(out_i)
     ret_near = ret_loc + ret_e
     half = (deep * hid + hid * classes) // LANES // 2
-    hidden_grad, keep, give = call(
+    sides = [in_th, in_tl, hid_th, hid_tl, loss]
+    grad, pre_h, pre_l, pair, give = call(
         backward,
-        [((nodes, hid), F32), ((half, LANES), F32), ((half, LANES), F32)],
-        [ret_near, ret_i, wout_hh, wout_ll, slope, in_th, in_tl, hid_th, hid_tl, loss],
+        [((nodes, hid), F32), ((nodes, hid), BF16), ((nodes, hid), BF16), ((nodes, 2 * classes), BF16),
+         ((half, LANES), F32)],
+        [ret_near, ret_i, wout_hh, wout_ll, slope, *sides],
         flops=12 * nodes * nodes * deep,
     )
-    big, mid = lax.axis_size(BIG), lax.axis_size(MID)
-    mine = (keep + mate(give, devices)).reshape(big, half // big, LANES)
-    summed = jnp.sum(exchange(mine, BIG), axis=0)
-    summed = jnp.sum(exchange(spread(summed, mid), MID), axis=0)
-    own = exchange(spread(summed, big), BIG).reshape(half, LANES)
-    other = mate(own, devices)
+    got = mate(give)
+    hidden_grad, keep = call(
+        beside_backward,
+        [((nodes, hid), F32), ((half, LANES), F32)],
+        [grad, pre_h, pre_l, pair, *sides],
+        flops=6 * nodes * nodes * deep,
+    )
+    big, mid = groups((X, Y), (X, Z)), groups((Z,), (Y,))
+    wide, narrow = len(big[0]), len(mid[0])
+    mine = (keep + got).reshape(wide, half // wide, LANES)
+    summed = jnp.sum(exchange(mine, big), axis=0)
+    summed = jnp.sum(exchange(spread(summed, narrow), mid), axis=0)
+    own = exchange(spread(summed, wide), big).reshape(half, LANES)
+    other = mate(own)
     grad_in, grad_out, mean_loss = call(
-        functools.partial(assemble, nodes * devices),
+        functools.partial(assemble, nodes * lax.axis_size(AXIS)),
         [((deep, hid), F32), ((hid, classes), F32), ((1, 1), F32)],
         [own, other],
+        scratch=[pltpu.VMEM((2, 8, LANES), F32), pltpu.SemaphoreType.DMA((2 * (hid // LANES + 2),))],
+        out_space=pltpu.HBM,
         name="assemble",
     )
     return (logits, mean_loss.reshape(()), hidden_grad, grad_in, grad_out)
 
 
 def solution(mesh):
-    grid = Mesh(mesh.devices.reshape(4, 8, 8, 2), ALL)
-    split = P(ALL)
+    split = P(AXIS)
     return jax.shard_map(
         per_device,
-        mesh=grid,
+        mesh=mesh,
         in_specs=(split, split, split, split, split, P(), P()),
         out_specs=(split, P(), split, P(), P()),
         check_vma=False,

time: 117 us -> 111 us (0.949)
  blocking collectives: 63.4 us -> 59.7 us
  waiting for transfers between devices: 7.73 us -> 5.8 us
    all_to_all x3, blocking collectives: 63.4 us -> 59.7 us  [exchange(): lax.all_to_all(value, AXIS, 0, 0, axis_index_groups=members, tiled=True)]
    ppermute x8, waiting for transfers between devices: 7.73 us -> 5.8 us  [the longest x3 3.33 us: beside(): return lax.ppermute(value, AXIS, pairs + [(b, a) for a, b in pairs])]
    pallas_call x9 -> x10, Pallas kernels: 16.8 us -> 17.3 us  [call(): pl.pallas_call(body, out_shape=[jax.ShapeDtypeStruct(shape, kind) for sha...]
  transfers between devices with their start and end apart: 8 -> 8, of which waited for: 5 -> 5; matrix products, arithmetic and copies ran while one was open for 0% -> 0% of each run, Pallas kernels for 7% -> 9%
where the time goes in v4:
time: 111 us; the launch traced here: 110 us
  blocking collectives  59.7 us (54%)
  starting transfers between devices  26.1 us (24%)
  Pallas kernels  17.3 us (16%)
  waiting for transfers between devices  5.8 us (5%)
    all_to_all x3, blocking collectives, exchange(): lax.all_to_all(value, AXIS, 0, 0, axis_index_groups=members, tiled=True)  59.7 us
    pallas_call x10, Pallas kernels, call(): pl.pallas_call(body, out_shape=[jax.ShapeDtypeStruct(shape, kind) for sha...  17.3 us
    ppermute x5, starting transfers between devices, mate(): lax.ppermute(value, AXIS, [(i, i ^ 1) for i in range(lax.axis_size(AXIS))])  16.7 us
    ppermute x3, starting transfers between devices, beside(): return lax.ppermute(value, AXIS, pairs + [(b, a) for a, b in pairs])  9.47 us
    ppermute x3, waiting for transfers between devices, beside(): return lax.ppermute(value, AXIS, pairs + [(b, a) for a, b in pairs])  3.33 us
    ppermute x5, waiting for transfers between devices, mate(): lax.ppermute(value, AXIS, [(i, i ^ 1) for i in range(lax.axis_size(AXIS))])  2.47 us
  transfers between devices with their start and end apart: 8, of which 5 were waited for; matrix products, arithmetic and copies ran while one was open for 0% of the time, Pallas kernels for 9%

profile of v4, /device:TPU:1, one launch (start us, length us, event | category | flops | bytes accessed | tf_op | source)
XLA Modules:
  0.0 110.0 jit_solution(6132749612134793575)
XLA Ops:
  0.6 4.6 %collective-permute-start = (f32[512,256]{1,0:T(8,128)}, f32[512,256]{1,0:T(8,128)S(1)}, u32[]{:S(2)}, u32[]{:S(2)}) collective-permute-start(f32[512,256]{1,0:T(8,128)} %features.1), channel_id=1, source_target_pairs={{1,2},{3,4},{5,6},{7,8},{9,10},{11,12},{13,14},{15,16},{17,18},{19... | collective-permute-start | bytes 1572872 | tf_op jit(solution)/shard_map/ppermute | solution.py:30
  5.2 4.5 %prepare.1 = (bf16[512,512]{1,0:T(8,128)(2,1)S(1)}, bf16[512,512]{1,0:T(8,128)(2,1)S(1)}, bf16[512,1024]{1,0:T(8,128)(2,1)S(1)}, bf16[512,1024]{1,0:T(8,128)(2,1...) custom-call(s32[2,6]{1,0:T(2,128)} %block_index.1, ...), custom_call_target="tpu_custom_call" | custom-call | flops 402653184 | bytes 4458552 | tf_op jit(solution)/shard_map/prepare/pallas_call | solution.py:278
  9.7 4.9 %collective-permute-start.1 = (f32[512,256]{1,0:T(8,128)S(1)}, f32[512,256]{1,0:T(8,128)S(1)}, u32[]{:S(2)}, u32[]{:S(2)}) collective-permute-start(f32[512,256]{1,0:T(8,128)S(1)} %get-tuple-element.48), channel_id=1, source_target_pairs={{0,1},{1,0},{2,3},{3,2},{4,5},{5,4},{6,7},{7,6},{8,9},{9,8},{10,11... | collective-permute-start | bytes 1572872 | tf_op jit(solution)/shard_map/ppermute | solution.py:25
  14.6 0.0 collective-permute-done.feat_e
  14.6 0.6 add_features.1.s_loc
  15.2 0.9 collective-permute-done.1.feat_i
  16.1 3.2 %spread_forward.1 = (f32[512,256]{1,0:T(8,128)S(1)}, f32[512,128]{1,0:T(8,128)S(1)}) custom-call(bf16[512,1024]{1,0:T(8,128)(2,1)S(1)} %get-tuple-element.43.halo_h, bf16[512,1024]{1,0:T(8,128)(2,1)S(1)} %get-tuple-element.44.halo_l, f32[512,256]{1,0:T(8,128)S(1)} %add_features.1.s_loc, f32[512,256]{1,0:T(8,128)S(1)} %collective-permute-done.1.feat_i, ...), custom_call_target="tpu_custom_call" | custom-call | flops 1342177280 | bytes 3932160 | tf_op jit(solution)/shard_map/spread_forward/pallas_call | solution.py:278
  19.3 1.9 %collective-permute-start.2 = (f32[512,128]{1,0:T(8,128)S(1)}, f32[512,128]{1,0:T(8,128)S(1)}, u32[]{:S(2)}, u32[]{:S(2)}) collective-permute-start(f32[512,128]{1,0:T(8,128)S(1)} %get-tuple-element.53.scores), channel_id=1, source_target_pairs={{1,2},{3,4},{5,6},{7,8},{9,10},{11,12},{13,14},{15,16},{17,18},{19... | collective-permute-start | bytes 786440 | tf_op jit(solution)/shard_map/ppermute | solution.py:30
  21.2 2.1 %beside_forward.1 = (f32[512,512]{1,0:T(8,128)S(1)}, bf16[512,512]{1,0:T(8,128)(2,1)S(1)}, bf16[512,512]{1,0:T(8,128)(2,1)S(1)}, bf16[256,512]{1,0:T(8,128)(2,1)...) custom-call(bf16[512,512]{1,0:T(8,128)(2,1)S(1)} %get-tuple-element.45.loc_h, ...), custom_call_target="tpu_custom_call" | custom-call | flops 805306368 | bytes 2359296 | tf_op jit(solution)/shard_map/beside_forward/pallas_call | solution.py:278
  23.3 1.9 %collective-permute-start.3 = (f32[512,128]{1,0:T(8,128)S(1)}, f32[512,128]{1,0:T(8,128)S(1)}, u32[]{:S(2)}, u32[]{:S(2)}) collective-permute-start(f32[512,128]{1,0:T(8,128)S(1)} %get-tuple-element.55), channel_id=1, source_target_pairs={{0,1},{1,0},{2,3},{3,2},{4,5},{5,4},{6,7},{7,6},{8,9},{9,8},{10,11... | collective-permute-start | bytes 786440 | tf_op jit(solution)/shard_map/ppermute | solution.py:25
  25.2 1.7 %collective-permute-done.2.sco_e = f32[512,128]{1,0:T(8,128)S(1)} collective-permute-done((f32[512,128]{1,0:T(8,128)S(1)}, f32[512,128]{1,0:T(8,128)S(1)}, u32[]{:S(2)}, u32[]{:S(2)}) %collective-permute-start.2) | collective-permute-done | bytes 262176 | tf_op jit(solution)/shard_map/ppermute | solution.py:30
  27.0 0.4 add_scores.1.logits_loc
  27.4 0.0 collective-permute-done.3.sco_i
  27.4 1.5 %classify.1 = (f32[512,128]{1,0:T(8,128)S(1)}, bf16[256,512]{1,0:T(8,128)(2,1)S(1)}, f32[128,512]{1,0:T(8,128)S(1)}) custom-call(bf16[512,1024]{1,0:T(8,128)(2,1)S(1)} %get-tuple-element.43.halo_h, bf16[512,1024]{1,0:T(8,128)(2,1)S(1)} %get-tuple-element.44.halo_l, f32[512,128]{1,0:T(8,128)S(1)} %add_scores.1.logits_loc, ...), custom_call_target="tpu_custom_call" | custom-call | flops 402653184 | bytes 2883584 | tf_op jit(solution)/shard_map/classify/pallas_call | solution.py:278
  28.9 3.0 %collective-permute-start.4 = (f32[128,512]{1,0:T(8,128)S(1)}, f32[128,512]{1,0:T(8,128)S(1)}, u32[]{:S(2)}, u32[]{:S(2)}) collective-permute-start(f32[128,512]{1,0:T(8,128)S(1)} %get-tuple-element.61), channel_id=1, source_target_pairs={{1,2},{3,4},{5,6},{7,8},{9,10},{11,12},{13,14},{15,16},{17,18},{19... | collective-permute-start | bytes 786440 | tf_op jit(solution)/shard_map/ppermute | solution.py:30
  31.9 1.2 %beside_classify.1 = (f32[128,512]{1,0:T(8,128)S(1)}, f32[128,512]{1,0:T(8,128)S(1)}, f32[512,128]{1,0:T(8,128)}, f32[8,128]{1,0:T(8,128)S(1)}) custom-call(bf16[256,512]{1,0:T(8,128)(2,1)S(1)} %get-tuple-element.57.grads_t, bf16[512,1024]{1,0:T(8,128)(2,1)S(1)} %get-tuple-element.43.halo_h, bf16[512,1024]{1,0:T(8,128)(2,1)S(1)} %get-tuple-element.44.halo_l, ...), custom_call_target="tpu_custom_call" | custom-call | flops 536870912 | bytes 3932160 | tf_op jit(solution)/shard_map/beside_classify/pallas_call | solution.py:278
  33.1 1.9 %collective-permute-start.5 = (f32[128,512]{1,0:T(8,128)S(1)}, f32[128,512]{1,0:T(8,128)S(1)}, u32[]{:S(2)}, u32[]{:S(2)}) collective-permute-start(f32[128,512]{1,0:T(8,128)S(1)} %get-tuple-element.62), channel_id=1, source_target_pairs={{0,1},{1,0},{2,3},{3,2},{4,5},{5,4},{6,7},{7,6},{8,9},{9,8},{10,11... | collective-permute-start | bytes 786440 | tf_op jit(solution)/shard_map/ppermute | solution.py:25
  35.0 1.6 %collective-permute-done.4 = f32[128,512]{1,0:T(8,128)S(1)} collective-permute-done((f32[128,512]{1,0:T(8,128)S(1)}, f32[128,512]{1,0:T(8,128)S(1)}, u32[]{:S(2)}, u32[]{:S(2)}) %collective-permute-start.4) | collective-permute-done | bytes 262176 | tf_op jit(solution)/shard_map/ppermute | solution.py:30
  36.7 0.0 collective-permute-done.5.ret_i
  36.7 0.9 backward.1
  37.6 1.9 %collective-permute-start.6 = (f32[768,128]{1,0:T(8,128)S(1)}, f32[768,128]{1,0:T(8,128)S(1)}, u32[]{:S(2)}, u32[]{:S(2)}) collective-permute-start(f32[768,128]{1,0:T(8,128)S(1)} %get-tuple-element.76), channel_id=1, source_target_pairs={{0,1},{1,0},{2,3},{3,2},{4,5},{5,4},{6,7},{7,6},{8,9},{9,8},{10,11... | collective-permute-start | bytes 1179656 | tf_op jit(solution)/shard_map/ppermute | solution.py:25
  39.5 1.5 %beside_backward.1 = (f32[512,512]{1,0:T(8,128)}, f32[768,128]{1,0:T(8,128)S(1)}) custom-call(f32[512,512]{1,0:T(8,128)S(1)} %get-tuple-element.71.grad, bf16[512,512]{1,0:T(8,128)(2,1)S(1)} %get-tuple-element.72.pre_h, bf16[512,512]{1,0:T(8,128)(2,1)S(1)} %get-tuple-element.73.pre_l, bf16[512,256]{1,0:T(8,128)(2,1)S(1)} %get-tuple-element.74.pair, ...), custom_call_target="tpu_custom_call" | custom-call | flops 402653184 | bytes 3936256 | tf_op jit(solution)/shard_map/beside_backward/pallas_call | solution.py:278
  41.0 0.2 collective-permute-done.6
  41.3 31.0 %all_to_all.15 = f32[32,24,128]{2,1,0:T(8,128)S(1)} all-to-all(f32[32,24,128]{2,1,0:T(8,128)S(1)} %bitcast.6), channel_id=1, replica_groups={{0,2,4,6,8,10,12,14,128,130,132,134,136,138,140,142,256,258,260,262,264..., dimensions={0} | all-to-all | bytes 786432 | tf_op jit(solution)/shard_map/all_to_all | solution.py:44
  72.3 13.1 %all_to_all.16 = f32[8,24,128]{2,1,0:T(8,128)S(1)} all-to-all(f32[8,24,128]{2,1,0:T(8,128)S(1)} %broadcast_in_dim.4), channel_id=1, replica_groups={{0,16,32,48,64,80,96,112},{2,18,34,50,66,82,98,114},{4,20,36,52,68,84,1..., dimensions={0} | all-to-all | bytes 196608 | tf_op jit(solution)/shard_map/all_to_all | solution.py:44
  85.5 15.6 %all_to_all.17 = f32[32,24,128]{2,1,0:T(8,128)S(1)} all-to-all(f32[32,24,128]{2,1,0:T(8,128)S(1)} %broadcast_in_dim.5), channel_id=1, replica_groups={{0,2,4,6,8,10,12,14,128,130,132,134,136,138,140,142,256,258,260,262,264..., dimensions={0} | all-to-all | bytes 786432 | tf_op jit(solution)/shard_map/all_to_all | solution.py:44
  101.1 6.1 %collective-permute-start.7 = (f32[768,128]{1,0:T(8,128)S(1)}, f32[768,128]{1,0:T(8,128)S(1)}, u32[]{:S(2)}, u32[]{:S(2)}) collective-permute-start(f32[768,128]{1,0:T(8,128)S(1)} %bitcast.4), channel_id=1, source_target_pairs={{0,1},{1,0},{2,3},{3,2},{4,5},{5,4},{6,7},{7,6},{8,9},{9,8},{10,11... | collective-permute-start | bytes 1179656 | tf_op jit(solution)/shard_map/ppermute | solution.py:25
  107.2 1.3 %collective-permute-done.7.other = f32[768,128]{1,0:T(8,128)S(1)} collective-permute-done((f32[768,128]{1,0:T(8,128)S(1)}, f32[768,128]{1,0:T(8,128)S(1)}, u32[]{:S(2)}, u32[]{:S(2)}) %collective-permute-start.7) | collective-permute-done | bytes 393248 | tf_op jit(solution)/shard_map/ppermute | solution.py:25
  108.5 1.5 %assemble.1 = (f32[256,512]{1,0:T(8,128)}, f32[512,128]{1,0:T(8,128)}, f32[1,1]{1,0:T(1,128)}) custom-call(f32[768,128]{1,0:T(8,128)S(1)} %bitcast.5, f32[768,128]{1,0:T(8,128)S(1)} %collective-permute-done.7.other), custom_call_target="tpu_custom_call" | custom-call | bytes 786432 | tf_op jit(solution)/shard_map/assemble/pallas_call | solution.py:278
  (6 shorter events, 0.2 us)
Async XLA Ops:
  0.6 14.0 %collective-permute-start = (f32[512,256]{1,0:T(8,128)}, f32[512,256]{1,0:T(8,128)S(1)}, u32[]{:S(2)}, u32[]{:S(2)}) collective-permute-start(f32[512,256]{1,0:T(8,128)} %features.1), channel_id=1, source_target_pairs={{1,2},{3,4},{5,6},{7,8},{9,10},{11,12},{13,14},{15,16},{17,18},{19... | collective-permute-start | bytes 1572872 | tf_op jit(solution)/shard_map/ppermute | solution.py:30
  9.7 6.4 %collective-permute-start.1 = (f32[512,256]{1,0:T(8,128)S(1)}, f32[512,256]{1,0:T(8,128)S(1)}, u32[]{:S(2)}, u32[]{:S(2)}) collective-permute-start(f32[512,256]{1,0:T(8,128)S(1)} %get-tuple-element.48), channel_id=1, source_target_pairs={{0,1},{1,0},{2,3},{3,2},{4,5},{5,4},{6,7},{7,6},{8,9},{9,8},{10,11... | collective-permute-start | bytes 1572872 | tf_op jit(solution)/shard_map/ppermute | solution.py:25
  19.3 7.7 %collective-permute-start.2 = (f32[512,128]{1,0:T(8,128)S(1)}, f32[512,128]{1,0:T(8,128)S(1)}, u32[]{:S(2)}, u32[]{:S(2)}) collective-permute-start(f32[512,128]{1,0:T(8,128)S(1)} %get-tuple-element.53.scores), channel_id=1, source_target_pairs={{1,2},{3,4},{5,6},{7,8},{9,10},{11,12},{13,14},{15,16},{17,18},{19... | collective-permute-start | bytes 786440 | tf_op jit(solution)/shard_map/ppermute | solution.py:30
  23.3 4.1 %collective-permute-start.3 = (f32[512,128]{1,0:T(8,128)S(1)}, f32[512,128]{1,0:T(8,128)S(1)}, u32[]{:S(2)}, u32[]{:S(2)}) collective-permute-start(f32[512,128]{1,0:T(8,128)S(1)} %get-tuple-element.55), channel_id=1, source_target_pairs={{0,1},{1,0},{2,3},{3,2},{4,5},{5,4},{6,7},{7,6},{8,9},{9,8},{10,11... | collective-permute-start | bytes 786440 | tf_op jit(solution)/shard_map/ppermute | solution.py:25
  28.9 7.7 %collective-permute-start.4 = (f32[128,512]{1,0:T(8,128)S(1)}, f32[128,512]{1,0:T(8,128)S(1)}, u32[]{:S(2)}, u32[]{:S(2)}) collective-permute-start(f32[128,512]{1,0:T(8,128)S(1)} %get-tuple-element.61), channel_id=1, source_target_pairs={{1,2},{3,4},{5,6},{7,8},{9,10},{11,12},{13,14},{15,16},{17,18},{19... | collective-permute-start | bytes 786440 | tf_op jit(solution)/shard_map/ppermute | solution.py:30
  33.1 3.6 %collective-permute-start.5 = (f32[128,512]{1,0:T(8,128)S(1)}, f32[128,512]{1,0:T(8,128)S(1)}, u32[]{:S(2)}, u32[]{:S(2)}) collective-permute-start(f32[128,512]{1,0:T(8,128)S(1)} %get-tuple-element.62), channel_id=1, source_target_pairs={{0,1},{1,0},{2,3},{3,2},{4,5},{5,4},{6,7},{7,6},{8,9},{9,8},{10,11... | collective-permute-start | bytes 786440 | tf_op jit(solution)/shard_map/ppermute | solution.py:25
  37.6 3.6 %collective-permute-start.6 = (f32[768,128]{1,0:T(8,128)S(1)}, f32[768,128]{1,0:T(8,128)S(1)}, u32[]{:S(2)}, u32[]{:S(2)}) collective-permute-start(f32[768,128]{1,0:T(8,128)S(1)} %get-tuple-element.76), channel_id=1, source_target_pairs={{0,1},{1,0},{2,3},{3,2},{4,5},{5,4},{6,7},{7,6},{8,9},{9,8},{10,11... | collective-permute-start | bytes 1179656 | tf_op jit(solution)/shard_map/ppermute | solution.py:25
  101.1 7.4 %collective-permute-start.7 = (f32[768,128]{1,0:T(8,128)S(1)}, f32[768,128]{1,0:T(8,128)S(1)}, u32[]{:S(2)}, u32[]{:S(2)}) collective-permute-start(f32[768,128]{1,0:T(8,128)S(1)} %bitcast.4), channel_id=1, source_target_pairs={{0,1},{1,0},{2,3},{3,2},{4,5},{5,4},{6,7},{7,6},{8,9},{9,8},{10,11... | collective-permute-start | bytes 1179656 | tf_op jit(solution)/shard_map/ppermute | solution.py:25

commit v5 on v4

v5 whole, which is shorter than its diff:
```python
import functools
import math

import jax
import jax.numpy as jnp
import numpy as np
from jax import lax
from jax.experimental import pallas as pl
from jax.experimental.pallas import tpu as pltpu
from jax.sharding import PartitionSpec as P

AXIS = "rows"
GRID = (4, 8, 8, 2)
X, Z, Y = range(3)
LANES = 128
F32 = jnp.float32
BF16 = jnp.bfloat16
VMEM_LIMIT = 24 * 1024 * 1024
CHUNK = 256
SQRT_HALF = 0.7071067811865476
INV_SQRT_2PI = 0.3989422804014327


def mate(value):
    return lax.ppermute(value, AXIS, [(i, i ^ 1) for i in range(lax.axis_size(AXIS))])


def beside(value):
    pairs = [(i, i + 1) for i in range(1, lax.axis_size(AXIS) - 1, 2)]
    return lax.ppermute(value, AXIS, pairs + [(b, a) for a, b in pairs])


def groups(*per_core):
    ids = np.arange(math.prod(GRID)).reshape(GRID)
    found = []
    for core, axes in enumerate(per_core):
        rest = [axis for axis in range(3) if axis not in axes]
        size = math.prod(GRID[axis] for axis in axes)
        found += ids[..., core].transpose(rest + list(axes)).reshape(-1, size).tolist()
    return found


def exchange(value, members):
    return lax.all_to_all(value, AXIS, 0, 0, axis_index_groups=members, tiled=True)


def repeated(value, count):
    return jnp.broadcast_to(value[None], (count,) + value.shape)


def halves(value):
    high = value.astype(BF16)
    return high, (value - high.astype(F32)).astype(BF16)


def mm(a, b, dims=((1,), (0,))):
    return lax.dot_general(a, b, (dims, ((), ())), preferred_element_type=F32)


def fold(wide):
    half = wide.shape[1] // 2
    return wide[:, :half] + wide[:, half:]


def erfc(value):
    size = jnp.abs(value)
    t = 1.0 / (1.0 + 0.5 * size)
    poly = jnp.full_like(t, 0.17087277)
    for term in (-0.82215223, 1.48851587, -1.13520398, 0.27886807, -0.18628806, 0.09678418,
                 0.37409196, 1.00002368, -1.26551223):
        poly = poly * t + term
    tail = t * jnp.exp(poly - size * size)
    return jnp.where(value < 0, 2.0 - tail, tail)


def prepare(block_index, block_counts, adjacency, features, w_in, w_out, labels,
            loc_h, loc_l, halo_h, halo_l, s_loc, win_h, win_l, wout_hl, wout_hh, wout_ll, onehot, feat_out,
            slots_in, feat_in, win_in, wout_in, labels_in, band, sems):
    here, slots, rows, _ = adjacency.shape
    moves = [(features, feat_in), (w_in, win_in), (w_out, wout_in), (labels, labels_in)]
    moves += [(adjacency.at[b, k], slots_in.at[b, k]) for b in range(here) for k in range(slots)]
    moves = [pltpu.make_async_copy(source, target, sems.at[i]) for i, (source, target) in enumerate(moves)]
    for move in moves:
        move.start()
    me = lax.axis_index(AXIS)
    core = lax.rem(me, 2)
    first = me * here
    band[...] = jnp.zeros_like(band)
    for move in moves[:4]:
        move.wait()
    high, low = halves(win_in[...])
    win_h[...] = high
    win_l[...] = low
    high, low = halves(wout_in[...])
    classes = high.shape[1]
    for ref, left, right in ((wout_hl, high, low), (wout_hh, high, high), (wout_ll, low, low)):
        ref[:, :classes] = left
        ref[:, classes:] = right
    columns = lax.broadcasted_iota(jnp.int32, (classes, labels_in.shape[1]), 0)
    onehot[...] = jnp.where(columns == labels_in[...], 1.0, 0.0).T
    feat_out[...] = feat_in[...]
    feat_h, feat_l = halves(feat_in[...])
    for b in range(here):
        for k in range(slots):
            moves[4 + b * slots + k].wait()
            near = block_index[b, k] - first
            right = near >= here
            outside = jnp.where(right, near - here, near + here)
            outside += jnp.where(right == (core == 0), 0, 2 * here)
            place = jnp.where((near >= 0) & (near < here), here + near, outside)

            @pl.when(k < block_counts[b])
            def _():
                band[b, place] += slots_in[b, k]

        at = pl.ds(b * rows, rows)
        for s in range(3 * here):
            high, low = halves(band[b, s])
            if here <= s < 2 * here:
                cols = pl.ds((s - here) * rows, rows)
                loc_h[at, cols] = high
                loc_l[at, cols] = low
            else:
                cols = pl.ds((s if s < here else s - here) * rows, rows)
                halo_h[at, cols] = high
                halo_l[at, cols] = low
        s_loc[at, :] = mm(loc_h[at, :], feat_h) + mm(loc_h[at, :], feat_l) + mm(loc_l[at, :], feat_h)


def add_features(halo_h, halo_l, s_loc, feat_e, out):
    half = feat_e.shape[0]
    high, low = halves(feat_e[...])
    he, le = halo_h[:, half:], halo_l[:, half:]
    out[...] = s_loc[...] + mm(he, high) + mm(he, low) + mm(le, high)


def spread(halo_h, halo_l, s_loc, feat_i, spread_in):
    half = feat_i.shape[0]
    high, low = halves(feat_i[...])
    hi, li = halo_h[:, :half], halo_l[:, :half]
    spread_in[...] = s_loc[...] + mm(hi, high) + mm(hi, low) + mm(li, high)


def layer(spread_in, win_h, win_l):
    s_h, s_l = halves(spread_in)
    pre = mm(s_h, win_h[...]) + mm(s_h, win_l[...]) + mm(s_l, win_h[...])
    gate = 0.5 * erfc(-SQRT_HALF * pre)
    return pre * gate, gate + pre * (INV_SQRT_2PI * jnp.exp(-0.5 * pre * pre))


def forward(high_band, low_band, spread_in, win_h, win_l, wout_hl, logits_before,
            scores_sum, slope, hid_h, hid_l, *in_t, first, part):
    hidden, slope[...] = layer(spread_in[...], win_h, win_l)
    high, low = halves(hidden)
    hid_h[...] = high
    hid_l[...] = low
    pair = jnp.concatenate(halves(fold(mm(high, wout_hl[...]) + mm(low, wout_hl[...]))), axis=1)
    nodes = spread_in.shape[0]
    cols = slice(part * nodes, (part + 1) * nodes)
    logits = fold(mm(high_band[:, cols], pair) + mm(low_band[:, cols], pair))
    scores_sum[...] = logits if first else logits_before[...] + logits
    if in_t:
        turn(spread_in, *in_t)


def turn(spread_in, in_th, in_tl):
    high, low = halves(spread_in[...].T)
    in_th[...] = high
    in_tl[...] = low


def stacked(grads, high, low):
    tall = mm(grads, high) + mm(grads, low)
    half = tall.shape[0] // 2
    return tall[:half] + tall[half:]


def classify(values, onehot, grads_t, loss):
    scores = values[...]
    totals = jnp.log(jnp.sum(jnp.exp(scores), axis=1, keepdims=True))
    hot = onehot[...]
    grads_t[...] = jnp.concatenate(halves((jnp.exp(scores - totals) - hot).T), axis=0)
    row_loss = totals - jnp.sum(hot * scores, axis=1, keepdims=True)
    loss[...] = jnp.broadcast_to(jnp.sum(row_loss, axis=0, keepdims=True), loss.shape)


def gradient_half(which, in_ts, pre, grad_out_t, loss, out):
    deep = in_ts[0][0].shape[0] // 2
    at = pl.ds(pl.multiple_of(which * deep, deep), deep)
    grad_in = 0.0
    for (in_th, in_tl), (pre_h, pre_l) in zip(in_ts, pre, strict=True):
        high, low = in_th[at, :], in_tl[at, :]
        tall = mm(jnp.concatenate([high, low], axis=0), pre_h)
        grad_in = grad_in + (tall[:deep] + tall[deep:] + mm(high, pre_l))
    for t in range(grad_in.shape[1] // LANES):
        out[pl.ds(t * deep, deep), :] = grad_in[:, t * LANES : (t + 1) * LANES]
    hid = grad_out_t.shape[1] // 2
    grad_out = jnp.where(which == 1, grad_out_t[:, hid:], grad_out_t[:, :hid]).T
    grad_out = jnp.where(last_element(grad_out) & (which == 1), loss[:1, :], grad_out)
    rows = deep * (grad_in.shape[1] // LANES)
    out[pl.ds(rows, hid), :] = grad_out
    return rows + hid


def last_element(value):
    row = lax.broadcasted_iota(jnp.int32, value.shape, 0)
    column = lax.broadcasted_iota(jnp.int32, value.shape, 1)
    return (row == value.shape[0] - 1) & (column == value.shape[1] - 1)


def backward(grads_t, halo_h, halo_l, loc_h, loc_l, slope_o, slope_i, slope_e, hid_oh, hid_ol, hid_ih, hid_il, hid_eh, hid_el,
             in_oh, in_ol, in_ih, in_il, in_eh, in_el, wout_hh, wout_ll, loss,
             pre_oh, pre_ol, pre_ih, pre_il, pre_eh, pre_el, total_out_t, ret_loc, out_e, give):
    grads = grads_t[...]
    half = loc_h.shape[1]
    own = stacked(grads, loc_h[...], loc_l[...])
    near = stacked(grads, halo_h[:, :half], halo_l[:, :half])
    far = stacked(grads, halo_h[:, half:], halo_l[:, half:])
    ret_loc[...] = own
    out_e[...] = far
    across = ((1,), (1,))
    grad_out_t = 0.0
    pre = []
    for returned_t, slope, hid_h, hid_l, pre_h, pre_l in (
        (own, slope_o, hid_oh, hid_ol, pre_oh, pre_ol),
        (near, slope_i, hid_ih, hid_il, pre_ih, pre_il),
        (far, slope_e, hid_eh, hid_el, pre_eh, pre_el),
    ):
        both = jnp.concatenate(halves(returned_t.T), axis=1)
        hidden_grad = mm(both, wout_hh[...], across) + mm(both, wout_ll[...], across)
        high, low = halves(hidden_grad * slope[...])
        pre_h[...] = high
        pre_l[...] = low
        pre.append((high, low))
        tall = jnp.concatenate(halves(returned_t), axis=0)
        grad_out_t = grad_out_t + stacked(tall, hid_h[...], hid_l[...])
    total_out_t[...] = grad_out_t
    other = 1 - lax.rem(lax.axis_index(AXIS), 2)
    in_ts = ((in_oh, in_ol), (in_ih, in_il), (in_eh, in_el))
    end = gradient_half(other, in_ts, pre, grad_out_t, loss, give)
    classes = near.shape[0]
    for t in range(half // LANES):
        give[pl.ds(end + t * classes, classes), :] = near[:, t * LANES : (t + 1) * LANES]


def backward_kept(in_oh, in_ol, in_ih, in_il, in_eh, in_el, pre_oh, pre_ol, pre_ih, pre_il, pre_eh, pre_el,
                  total_out_t, loss, values, keep, logits):
    core = lax.rem(lax.axis_index(AXIS), 2)
    in_ts = ((in_oh, in_ol), (in_ih, in_il), (in_eh, in_el))
    pre = [(h[...], l[...]) for h, l in ((pre_oh, pre_ol), (pre_ih, pre_il), (pre_eh, pre_el))]
    gradient_half(core, in_ts, pre, total_out_t[...], loss, keep)
    logits[...] = values[...]


def finish_hidden(ret_loc, ret_e, got, wout_hh, wout_ll, hidden_grad):
    classes, nodes = ret_loc.shape
    start = got.shape[0] - classes * (nodes // LANES)
    ret_i = [got[pl.ds(start + t * classes, classes), :] for t in range(nodes // LANES)]
    returned_t = ret_loc[...] + ret_e[...] + jnp.concatenate(ret_i, axis=1)
    both = jnp.concatenate(halves(returned_t.T), axis=1)
    across = ((1,), (1,))
    hidden_grad[...] = mm(both, wout_hh[...], across) + mm(both, wout_ll[...], across)


def add_halves(keep, got, out):
    out[...] = keep[...] + got[: keep.shape[0], :]


def sum_repeated(received, passed, out, copied):
    total = received[0]
    for k in range(1, received.shape[0]):
        total = total + received[k]
    out[...] = jnp.broadcast_to(total[None], out.shape)
    copied[...] = passed[...]


def sum_repeated_after(received, after, out):
    del after
    total = received[0]
    for k in range(1, received.shape[0]):
        total = total + received[k]
    out[...] = jnp.broadcast_to(total[None], out.shape)


def assemble(nodes_total, own, other, grad_in, grad_out, mean_loss):
    deep = grad_in.shape[0] // 2
    hid = grad_out.shape[0] // 2
    tiles = grad_in.shape[1] // LANES
    core = lax.rem(lax.axis_index(AXIS), 2)
    for half, which in ((own, core), (other, 1 - core)):
        at = pl.ds(pl.multiple_of(which * deep, deep), deep)
        for t in range(tiles):
            grad_in[at, t * LANES : (t + 1) * LANES] = half[pl.ds(t * deep, deep), :]
        at = pl.ds(pl.multiple_of(which * hid, hid), hid)
        grad_out[at, :] = half[pl.ds(tiles * deep, hid), :]
    end = pl.ds(2 * hid - 8, 8)
    value = grad_out[end, :]
    there = last_element(value)
    mean_loss[0, 0] = jnp.sum(jnp.where(there, value, 0.0)) / nodes_total
    others = jnp.sum(jnp.where(there, 0.0, value), axis=1, keepdims=True)
    grad_out[end, :] = jnp.where(there, -others, value)


def call(body, outs, args, scalars=0, anywhere=0, flops=0, scratch=(), space=pltpu.VMEM, name=""):
    smem = pl.BlockSpec(memory_space=pltpu.SMEM)
    vmem = pl.BlockSpec(memory_space=pltpu.VMEM)
    moved = sum(a.size * a.dtype.itemsize for a in args)
    return pl.pallas_call(
        body,
        out_shape=[jax.ShapeDtypeStruct(shape, kind) for shape, kind in outs],
        in_specs=[smem] * scalars
        + [pl.BlockSpec(memory_space=space)] * (len(args) - scalars - anywhere)
        + [pl.BlockSpec(memory_space=pl.ANY)] * anywhere,
        out_specs=[smem if shape == (1, 1) else vmem for shape, _ in outs],
        scratch_shapes=scratch,
        cost_estimate=pl.CostEstimate(flops=flops, bytes_accessed=moved, transcendentals=0),
        compiler_params=pltpu.CompilerParams(vmem_limit_bytes=VMEM_LIMIT),
        name=name or body.__name__,
    )(*args)


def per_device(features, adjacency, block_index, block_counts, labels, weight_in, weight_out):
    here, slots, rows = adjacency.shape[:3]
    nodes = here * rows
    deep, hid = weight_in.shape
    classes = weight_out.shape[1]

    feat_e = beside(features)
    loc = ((nodes, nodes), BF16)
    halo = ((nodes, 2 * nodes), BF16)
    w_pair = ((hid, 2 * classes), BF16)
    loc_h, loc_l, halo_h, halo_l, s_loc, win_h, win_l, wout_hl, wout_hh, wout_ll, onehot, feat_out = call(
        prepare,
        [loc, loc, halo, halo, ((nodes, deep), F32), ((deep, hid), BF16), ((deep, hid), BF16),
         w_pair, w_pair, w_pair, ((nodes, classes), F32), ((nodes, deep), F32)],
        [pltpu.with_memory_space_constraint(v, pltpu.HBM)
         for v in (block_index, block_counts, adjacency, features, weight_in, weight_out, labels.reshape(1, nodes))],
        scalars=2,
        flops=6 * nodes * nodes * deep,
        scratch=[
            pltpu.VMEM(adjacency.shape, F32),
            pltpu.VMEM(features.shape, F32),
            pltpu.VMEM(weight_in.shape, F32),
            pltpu.VMEM(weight_out.shape, F32),
            pltpu.VMEM((1, nodes), jnp.int32),
            pltpu.VMEM((here, 3 * here, rows, rows), F32),
            pltpu.SemaphoreType.DMA((4 + here * slots,)),
        ],
        space=pltpu.HBM,
    )
    feat_i = mate(feat_out)
    (s_loc,) = call(
        add_features,
        [((nodes, deep), F32)],
        [halo_h, halo_l, s_loc, feat_e],
        flops=6 * nodes * nodes * deep,
    )
    wide_f, wide_h = ((nodes, hid), F32), ((nodes, hid), BF16)
    thin, thin_t, in_t = ((nodes, classes), F32), ((classes, nodes), F32), ((deep, nodes), BF16)
    (spread_in,) = call(
        spread, [((nodes, deep), F32)], [halo_h, halo_l, s_loc, feat_i], flops=6 * nodes * nodes * deep
    )
    spread_e = beside(spread_in)
    spread_i = mate(spread_in)
    in_oh, in_ol = call(turn, [in_t, in_t], [spread_in])

    def layer_of(high, low, rows_in, before, name, part):
        return call(
            functools.partial(forward, first=name == "forward_own", part=part),
            [thin, wide_f, wide_h, wide_h] + [in_t] * (0 if name == "forward_own" else 2),
            [high, low, rows_in, win_h, win_l, wout_hl, before],
            flops=16 * nodes * nodes * deep,
            name=name,
        )

    logits_o, slope_o, *kept_o = layer_of(loc_h, loc_l, spread_in, onehot, "forward_own", 0)
    logits_i, slope_i, *kept_i = layer_of(halo_h, halo_l, spread_i, logits_o, "forward_mate", 0)
    values, slope_e, *kept_e = layer_of(halo_h, halo_l, spread_e, logits_i, "forward_beside", 1)
    grads_t, loss = call(classify, [((2 * classes, nodes), BF16), ((8, LANES), F32)], [values, onehot])
    half = (deep * hid + hid * classes) // LANES // 2
    in_ts = [in_oh, in_ol, *kept_i[2:], *kept_e[2:]]
    *pre, total_out_t, ret_loc, out_e, give = call(
        backward,
        [wide_h] * 6 + [((classes, hid), F32), thin_t, thin_t, ((half + classes * (nodes // LANES), LANES), F32)],
        [grads_t, halo_h, halo_l, loc_h, loc_l, slope_o, slope_i, slope_e, *kept_o[:2], *kept_i[:2], *kept_e[:2],
         *in_ts, wout_hh, wout_ll, loss],
        flops=30 * nodes * nodes * deep,
    )
    got = mate(give)
    keep, logits = call(
        backward_kept,
        [((half, LANES), F32), thin],
        [*in_ts, *pre, total_out_t, loss, values],
        flops=10 * nodes * nodes * deep,
    )
    big, mid = groups((X, Y), (X, Z)), groups((Z,), (Y,))
    wide, narrow = len(big[0]), len(mid[0])
    shard = half // wide
    (mine,) = call(add_halves, [((half, LANES), F32)], [keep, got])
    received = exchange(mine.reshape(wide, shard, LANES), big)
    summed, out_e = call(sum_repeated, [((narrow, shard, LANES), F32), thin_t], [received, out_e])
    ret_e = beside(out_e)
    received = exchange(summed, mid)
    (summed,) = call(sum_repeated_after, [((wide, shard, LANES), F32)], [received, ret_e], anywhere=1)
    own = exchange(summed, big).reshape(half, LANES)
    other = mate(own)
    (hidden_grad,) = call(
        finish_hidden, [wide_f], [ret_loc, ret_e, got, wout_hh, wout_ll], flops=4 * nodes * nodes * deep
    )
    grad_in, grad_out, mean_loss = call(
        functools.partial(assemble, nodes * lax.axis_size(AXIS)),
        [((deep, hid), F32), ((hid, classes), F32), ((1, 1), F32)],
        [own, other],
        name="assemble",
    )
    return (logits, mean_loss.reshape(()), hidden_grad, grad_in, grad_out)


def solution(mesh):
    split = P(AXIS)
    return jax.shard_map(
        per_device,
        mesh=mesh,
        in_specs=(split, split, split, split, split, P(), P()),
        out_specs=(split, P(), split, P(), P()),
        check_vma=False,
    )
```

time: 111 us -> 108 us (0.973)
  blocking collectives: 59.7 us -> 54.1 us
  Pallas kernels: 17.3 us -> 22.8 us
  waiting for transfers between devices: 5.8 us -> 3.62 us
    all_to_all x3, blocking collectives: 59.7 us -> 54.1 us  [exchange(): lax.all_to_all(value, AXIS, 0, 0, axis_index_groups=members, tiled=True)]
    pallas_call x10 -> x15, Pallas kernels: 17.3 us -> 22.8 us  [call(): pl.pallas_call(body, out_shape=[jax.ShapeDtypeStruct(shape, kind) for sha...]
    ppermute x5 -> x4, starting transfers between devices: 16.7 us -> 13.8 us  [mate(): lax.ppermute(value, AXIS, [(i, i ^ 1) for i in range(lax.axis_size(AXIS))])]
    ppermute x3, starting transfers between devices: 9.47 us -> 12.1 us  [beside(): return lax.ppermute(value, AXIS, pairs + [(b, a) for a, b in pairs])]
    ppermute x3, waiting for transfers between devices: 3.33 us -> 2.06 us  [beside(): return lax.ppermute(value, AXIS, pairs + [(b, a) for a, b in pairs])]
    ppermute x5 -> x4, waiting for transfers between devices: 2.47 us -> 1.56 us  [mate(): lax.ppermute(value, AXIS, [(i, i ^ 1) for i in range(lax.axis_size(AXIS))])]
  transfers between devices with their start and end apart: 8 -> 7, of which waited for: 5 -> 3; matrix products, arithmetic and copies ran while one was open for 0% -> 0% of each run, Pallas kernels for 9% -> 13%
where the time goes in v5:
time: 108 us; the launch traced here: 107 us
  blocking collectives  54.1 us (50%)
  starting transfers between devices  25.9 us (24%)
  Pallas kernels  22.8 us (21%)
  waiting for transfers between devices  3.62 us (3%)
    all_to_all x3, blocking collectives, exchange(): lax.all_to_all(value, AXIS, 0, 0, axis_index_groups=members, tiled=True)  54.1 us
    pallas_call x15, Pallas kernels, call(): pl.pallas_call(body, out_shape=[jax.ShapeDtypeStruct(shape, kind) for sha...  22.8 us
    ppermute x4, starting transfers between devices, mate(): lax.ppermute(value, AXIS, [(i, i ^ 1) for i in range(lax.axis_size(AXIS))])  13.8 us
    ppermute x3, starting transfers between devices, beside(): return lax.ppermute(value, AXIS, pairs + [(b, a) for a, b in pairs])  12.1 us
  transfers between devices with their start and end apart: 7, of which 3 were waited for; matrix products, arithmetic and copies ran while one was open for 0% of the time, Pallas kernels for 13%

profile of v5, /device:TPU:1, one launch (start us, length us, event | category | flops | bytes accessed | tf_op | source)
XLA Modules:
  0.0 107.5 jit_solution(12375256127295083583)
XLA Ops:
  0.6 4.6 %collective-permute-start = (f32[512,256]{1,0:T(8,128)}, f32[512,256]{1,0:T(8,128)S(1)}, u32[]{:S(2)}, u32[]{:S(2)}) collective-permute-start(f32[512,256]{1,0:T(8,128)} %features.1), channel_id=1, source_target_pairs={{1,2},{3,4},{5,6},{7,8},{9,10},{11,12},{13,14},{15,16},{17,18},{19... | collective-permute-start | bytes 1572872 | tf_op jit(solution)/shard_map/ppermute | solution.py:30
  5.2 4.5 %prepare.1 = (bf16[512,512]{1,0:T(8,128)(2,1)S(1)}, bf16[512,512]{1,0:T(8,128)(2,1)S(1)}, bf16[512,1024]{1,0:T(8,128)(2,1)S(1)}, bf16[512,1024]{1,0:T(8,128)(2,1...) custom-call(s32[2,6]{1,0:T(2,128)} %block_index.1, ...), custom_call_target="tpu_custom_call" | custom-call | flops 402653184 | bytes 4458552 | tf_op jit(solution)/shard_map/prepare/pallas_call | solution.py:308
  9.8 4.9 %collective-permute-start.1 = (f32[512,256]{1,0:T(8,128)S(1)}, f32[512,256]{1,0:T(8,128)S(1)}, u32[]{:S(2)}, u32[]{:S(2)}) collective-permute-start(f32[512,256]{1,0:T(8,128)S(1)} %get-tuple-element.57), channel_id=1, source_target_pairs={{0,1},{1,0},{2,3},{3,2},{4,5},{5,4},{6,7},{7,6},{8,9},{9,8},{10,11... | collective-permute-start | bytes 1572872 | tf_op jit(solution)/shard_map/ppermute | solution.py:25
  14.7 0.0 collective-permute-done.feat_e
  14.7 0.6 add_features.1.s_loc
  15.3 0.9 collective-permute-done.1.feat_i
  16.2 0.6 spread.1.spread_in
  16.8 2.3 %collective-permute-start.2 = (f32[512,256]{1,0:T(8,128)S(1)}, f32[512,256]{1,0:T(8,128)S(1)}, u32[]{:S(2)}, u32[]{:S(2)}) collective-permute-start(f32[512,256]{1,0:T(8,128)S(1)} %spread.1.spread_in), channel_id=1, source_target_pairs={{0,1},{1,0},{2,3},{3,2},{4,5},{5,4},{6,7},{7,6},{8,9},{9,8},{10,11... | collective-permute-start | bytes 1572872 | tf_op jit(solution)/shard_map/ppermute | solution.py:25
  19.1 2.1 %collective-permute-start.3 = (f32[512,256]{1,0:T(8,128)S(1)}, f32[512,256]{1,0:T(8,128)S(1)}, u32[]{:S(2)}, u32[]{:S(2)}) collective-permute-start(f32[512,256]{1,0:T(8,128)S(1)} %spread.1.spread_in), channel_id=1, source_target_pairs={{1,2},{3,4},{5,6},{7,8},{9,10},{11,12},{13,14},{15,16},{17,18},{19... | collective-permute-start | bytes 1572872 | tf_op jit(solution)/shard_map/ppermute | solution.py:30
  21.2 0.2 turn.1
  21.4 3.0 %forward_own.1 = (f32[512,128]{1,0:T(8,128)S(1)}, f32[512,512]{1,0:T(8,128)S(1)}, bf16[512,512]{1,0:T(8,128)(2,1)S(1)}, bf16[512,512]{1,0:T(8,128)(2,1)S(1)}) custom-call(bf16[512,512]{1,0:T(8,128)(2,1)S(1)} %get-tuple-element.63.high_band.loc_h, bf16[512,512]{1,0:T(8,128)(2,1)S(1)} %get-tuple-element.64.low_band.loc_l, f32[512,256]{1,0:T(8,128)S(1)} %spread.1.spread_in, ...), custom_call_target="tpu_custom_call" | custom-call | flops 1073741824 | bytes 2621440 | tf_op jit(solution)/shard_map/forward_own/pallas_call | solution.py:308
  24.5 0.0 collective-permute-done.2.spread_in
  24.5 3.0 %forward_mate.1 = (f32[512,128]{1,0:T(8,128)S(1)}, f32[512,512]{1,0:T(8,128)S(1)}, bf16[512,512]{1,0:T(8,128)(2,1)S(1)}, bf16[512,512]{1,0:T(8,128)(2,1)S(1)}, b...) custom-call(bf16[512,1024]{1,0:T(8,128)(2,1)S(1)} %get-tuple-element.54.halo_h.high_band, ...), custom_call_target="tpu_custom_call" | custom-call | flops 1073741824 | bytes 3670016 | tf_op jit(solution)/shard_map/forward_mate/pallas_call | solution.py:308
  27.6 2.1 %collective-permute-done.3.spread_in = f32[512,256]{1,0:T(8,128)S(1)} collective-permute-done((f32[512,256]{1,0:T(8,128)S(1)}, f32[512,256]{1,0:T(8,128)S(1)}, u32[]{:S(2)}, u32[]{:S(2)}) %collective-permute-start.3) | collective-permute-done | bytes 524320 | tf_op jit(solution)/shard_map/ppermute | solution.py:30
  29.6 3.1 %forward_beside.1 = (f32[512,128]{1,0:T(8,128)S(1)}, f32[512,512]{1,0:T(8,128)S(1)}, bf16[512,512]{1,0:T(8,128)(2,1)S(1)}, bf16[512,512]{1,0:T(8,128)(2,1)S(1)},...) custom-call(bf16[512,1024]{1,0:T(8,128)(2,1)S(1)} %get-tuple-element.54.halo_h.high_band, ...), custom_call_target="tpu_custom_call" | custom-call | flops 1073741824 | bytes 3670016 | tf_op jit(solution)/shard_map/forward_beside/pallas_call | solution.py:308
  32.7 0.3 classify.1
  33.0 3.5 %backward.1 = (bf16[512,512]{1,0:T(8,128)(2,1)S(1)}, bf16[512,512]{1,0:T(8,128)(2,1)S(1)}, bf16[512,512]{1,0:T(8,128)(2,1)S(1)}, bf16[512,512]{1,0:T(8,128)(2,1)...) custom-call(bf16[256,512]{1,0:T(8,128)(2,1)S(1)} %get-tuple-element., ...), custom_call_target="tpu_custom_call" | custom-call | flops 2013265920 | bytes 11800576 | tf_op jit(solution)/shard_map/backward/pallas_call | solution.py:308
  36.5 1.9 %collective-permute-start.4 = (f32[1280,128]{1,0:T(8,128)S(1)}, f32[1280,128]{1,0:T(8,128)S(1)}, u32[]{:S(2)}, u32[]{:S(2)}) collective-permute-start(f32[1280,128]{1,0:T(8,128)S(1)} %get-tuple-element.95), channel_id=1, source_target_pairs={{0,1},{1,0},{2,3},{3,2},{4,5},{5,4},{6,7},{7,6},{8,9},{9,8},{10,11... | collective-permute-start | bytes 1966088 | tf_op jit(solution)/shard_map/ppermute | solution.py:25
  38.4 1.4 %backward_kept.1 = (f32[768,128]{1,0:T(8,128)S(1)}, f32[512,128]{1,0:T(8,128)}) custom-call(bf16[256,512]{1,0:T(8,128)(2,1)S(1)} %get-tuple-element.58.in_oh, bf16[256,512]{1,0:T(8,128)(2,1)S(1)} %get-tuple-element.59.in_ol, bf16[256,512]{1,0:T(8,128)(2,1)S(1)} %get-tuple-element.67.in_ih, bf16[256,512]{1,0:T(8,128)(2,1)S(1)} %get-tuple-element.68.in_il, ...), custom_call_target="tpu_custom_call" | custom-call | flops 671088640 | bytes 5246976 | tf_op jit(solution)/shard_map/backward_kept/pallas_call | solution.py:308
  39.8 0.6 collective-permute-done.4.got
  40.5 26.3 %all_to_all.15.received = f32[32,24,128]{2,1,0:T(8,128)S(1)} all-to-all(f32[32,24,128]{2,1,0:T(8,128)S(1)} %bitcast.6), channel_id=1, replica_groups={{0,2,4,6,8,10,12,14,128,130,132,134,136,138,140,142,256,258,260,262,264..., dimensions={0} | all-to-all | bytes 786432 | tf_op jit(solution)/shard_map/all_to_all | solution.py:44
  66.8 5.4 %collective-permute-start.5 = (f32[128,512]{1,0:T(8,128)S(1)}, f32[128,512]{1,0:T(8,128)S(1)}, u32[]{:S(2)}, u32[]{:S(2)}) collective-permute-start(f32[128,512]{1,0:T(8,128)S(1)} %get-tuple-element.98), channel_id=1, source_target_pairs={{1,2},{3,4},{5,6},{7,8},{9,10},{11,12},{13,14},{15,16},{17,18},{19... | collective-permute-start | bytes 786440 | tf_op jit(solution)/shard_map/ppermute | solution.py:30
  72.3 10.0 %all_to_all.16.received = f32[8,24,128]{2,1,0:T(8,128)S(1)} all-to-all(f32[8,24,128]{2,1,0:T(8,128)S(1)} %get-tuple-element.97), channel_id=1, replica_groups={{0,16,32,48,64,80,96,112},{2,18,34,50,66,82,98,114},{4,20,36,52,68,84,1..., dimensions={0} | all-to-all | bytes 196608 | tf_op jit(solution)/shard_map/all_to_all | solution.py:44
  82.2 0.0 collective-permute-done.5.after.ret_e
  82.2 17.9 %all_to_all.17 = f32[32,24,128]{2,1,0:T(8,128)S(1)} all-to-all(f32[32,24,128]{2,1,0:T(8,128)S(1)} %sum_repeated_after.1), channel_id=1, replica_groups={{0,2,4,6,8,10,12,14,128,130,132,134,136,138,140,142,256,258,260,262,264..., dimensions={0} | all-to-all | bytes 786432 | tf_op jit(solution)/shard_map/all_to_all | solution.py:44
  100.2 4.7 %collective-permute-start.6 = (f32[768,128]{1,0:T(8,128)S(1)}, f32[768,128]{1,0:T(8,128)S(1)}, u32[]{:S(2)}, u32[]{:S(2)}) collective-permute-start(f32[768,128]{1,0:T(8,128)S(1)} %bitcast.4), channel_id=1, source_target_pairs={{0,1},{1,0},{2,3},{3,2},{4,5},{5,4},{6,7},{7,6},{8,9},{9,8},{10,11... | collective-permute-start | bytes 1179656 | tf_op jit(solution)/shard_map/ppermute | solution.py:25
  104.9 1.5 %finish_hidden.1 = f32[512,512]{1,0:T(8,128)} custom-call(f32[128,512]{1,0:T(8,128)S(1)} %get-tuple-element.100.ret_loc, f32[128,512]{1,0:T(8,128)S(1)} %collective-permute-done.5.after.ret_e, f32[1280,128]{1,0:T(8,128)S(1)} %collective-permute-done.4.got, bf16[512,256]{1,0:T(8,128)(2,1)S(1)} %get-tuple-element.83.wout_hh, ...), custom_call_target="tpu_custom_call" | custom-call | flops 268435456 | bytes 1703936 | tf_op jit(solution)/shard_map/finish_hidden/pallas_call | solution.py:308
  106.3 0.0 collective-permute-done.6.other
  106.3 1.0 assemble.1
  (3 shorter events, 0.1 us)
Async XLA Ops:
  0.6 14.1 %collective-permute-start = (f32[512,256]{1,0:T(8,128)}, f32[512,256]{1,0:T(8,128)S(1)}, u32[]{:S(2)}, u32[]{:S(2)}) collective-permute-start(f32[512,256]{1,0:T(8,128)} %features.1), channel_id=1, source_target_pairs={{1,2},{3,4},{5,6},{7,8},{9,10},{11,12},{13,14},{15,16},{17,18},{19... | collective-permute-start | bytes 1572872 | tf_op jit(solution)/shard_map/ppermute | solution.py:30
  9.8 6.5 %collective-permute-start.1 = (f32[512,256]{1,0:T(8,128)S(1)}, f32[512,256]{1,0:T(8,128)S(1)}, u32[]{:S(2)}, u32[]{:S(2)}) collective-permute-start(f32[512,256]{1,0:T(8,128)S(1)} %get-tuple-element.57), channel_id=1, source_target_pairs={{0,1},{1,0},{2,3},{3,2},{4,5},{5,4},{6,7},{7,6},{8,9},{9,8},{10,11... | collective-permute-start | bytes 1572872 | tf_op jit(solution)/shard_map/ppermute | solution.py:25
  16.8 7.7 %collective-permute-start.2 = (f32[512,256]{1,0:T(8,128)S(1)}, f32[512,256]{1,0:T(8,128)S(1)}, u32[]{:S(2)}, u32[]{:S(2)}) collective-permute-start(f32[512,256]{1,0:T(8,128)S(1)} %spread.1.spread_in), channel_id=1, source_target_pairs={{0,1},{1,0},{2,3},{3,2},{4,5},{5,4},{6,7},{7,6},{8,9},{9,8},{10,11... | collective-permute-start | bytes 1572872 | tf_op jit(solution)/shard_map/ppermute | solution.py:25
  19.1 10.5 %collective-permute-start.3 = (f32[512,256]{1,0:T(8,128)S(1)}, f32[512,256]{1,0:T(8,128)S(1)}, u32[]{:S(2)}, u32[]{:S(2)}) collective-permute-start(f32[512,256]{1,0:T(8,128)S(1)} %spread.1.spread_in), channel_id=1, source_target_pairs={{1,2},{3,4},{5,6},{7,8},{9,10},{11,12},{13,14},{15,16},{17,18},{19... | collective-permute-start | bytes 1572872 | tf_op jit(solution)/shard_map/ppermute | solution.py:30
  36.5 4.0 %collective-permute-start.4 = (f32[1280,128]{1,0:T(8,128)S(1)}, f32[1280,128]{1,0:T(8,128)S(1)}, u32[]{:S(2)}, u32[]{:S(2)}) collective-permute-start(f32[1280,128]{1,0:T(8,128)S(1)} %get-tuple-element.95), channel_id=1, source_target_pairs={{0,1},{1,0},{2,3},{3,2},{4,5},{5,4},{6,7},{7,6},{8,9},{9,8},{10,11... | collective-permute-start | bytes 1966088 | tf_op jit(solution)/shard_map/ppermute | solution.py:25
  66.8 15.4 %collective-permute-start.5 = (f32[128,512]{1,0:T(8,128)S(1)}, f32[128,512]{1,0:T(8,128)S(1)}, u32[]{:S(2)}, u32[]{:S(2)}) collective-permute-start(f32[128,512]{1,0:T(8,128)S(1)} %get-tuple-element.98), channel_id=1, source_target_pairs={{1,2},{3,4},{5,6},{7,8},{9,10},{11,12},{13,14},{15,16},{17,18},{19... | collective-permute-start | bytes 786440 | tf_op jit(solution)/shard_map/ppermute | solution.py:30
  100.2 6.2 %collective-permute-start.6 = (f32[768,128]{1,0:T(8,128)S(1)}, f32[768,128]{1,0:T(8,128)S(1)}, u32[]{:S(2)}, u32[]{:S(2)}) collective-permute-start(f32[768,128]{1,0:T(8,128)S(1)} %bitcast.4), channel_id=1, source_target_pairs={{0,1},{1,0},{2,3},{3,2},{4,5},{5,4},{6,7},{7,6},{8,9},{9,8},{10,11... | collective-permute-start | bytes 1179656 | tf_op jit(solution)/shard_map/ppermute | solution.py:25

commit v6 on v5

--- a/solution.py
+++ b/solution.py
@@ -19,6 +19,17 @@
 CHUNK = 256
 SQRT_HALF = 0.7071067811865476
 INV_SQRT_2PI = 0.3989422804014327
+HALF_ERFC = (
+    0.0251311707,
+    -0.0914511383,
+    0.0845433265,
+    -0.00280424249,
+    0.0707159187,
+    0.0842709431,
+    0.103921354,
+    0.112834799,
+    0.112837931,
+)
 
 
 def mate(value):
@@ -60,17 +71,6 @@
 def fold(wide):
     half = wide.shape[1] // 2
     return wide[:, :half] + wide[:, half:]
-
-
-def erfc(value):
-    size = jnp.abs(value)
-    t = 1.0 / (1.0 + 0.5 * size)
-    poly = jnp.full_like(t, 0.17087277)
-    for term in (-0.82215223, 1.48851587, -1.13520398, 0.27886807, -0.18628806, 0.09678418,
-                 0.37409196, 1.00002368, -1.26551223):
-        poly = poly * t + term
-    tail = t * jnp.exp(poly - size * size)
-    return jnp.where(value < 0, 2.0 - tail, tail)
 
 
 def prepare(block_index, block_counts, adjacency, features, w_in, w_out, labels,
@@ -144,8 +144,14 @@
 def layer(spread_in, win_h, win_l):
     s_h, s_l = halves(spread_in)
     pre = mm(s_h, win_h[...]) + mm(s_h, win_l[...]) + mm(s_l, win_h[...])
-    gate = 0.5 * erfc(-SQRT_HALF * pre)
-    return pre * gate, gate + pre * (INV_SQRT_2PI * jnp.exp(-0.5 * pre * pre))
+    bell = jnp.exp(-0.5 * pre * pre)
+    t = 1.0 / (1.0 + (0.4 * SQRT_HALF) * jnp.abs(pre))
+    poly = jnp.full_like(t, HALF_ERFC[0])
+    for term in HALF_ERFC[1:]:
+        poly = poly * t + term
+    tail = bell * (t * poly)
+    gate = jnp.where(pre < 0, tail, 1.0 - tail)
+    return pre * gate, gate + pre * (INV_SQRT_2PI * bell)
 
 
 def forward(high_band, low_band, spread_in, win_h, win_l, wout_hl, logits_before,
@@ -184,18 +190,20 @@
     loss[...] = jnp.broadcast_to(jnp.sum(row_loss, axis=0, keepdims=True), loss.shape)
 
 
-def gradient_half(which, in_ts, pre, grad_out_t, loss, out):
-    deep = in_ts[0][0].shape[0] // 2
+def gradient_half(which, parts, loss, out):
+    deep, hid = parts[0][2][0].shape[0] // 2, parts[0][1][0].shape[1] // 2
     at = pl.ds(pl.multiple_of(which * deep, deep), deep)
-    grad_in = 0.0
-    for (in_th, in_tl), (pre_h, pre_l) in zip(in_ts, pre, strict=True):
+    cols = pl.ds(pl.multiple_of(which * hid, hid), hid)
+    grad_in = grad_out_t = 0.0
+    for returned_t, (hid_h, hid_l), (in_th, in_tl), (pre_h, pre_l) in parts:
         high, low = in_th[at, :], in_tl[at, :]
         tall = mm(jnp.concatenate([high, low], axis=0), pre_h)
         grad_in = grad_in + (tall[:deep] + tall[deep:] + mm(high, pre_l))
+        tall = jnp.concatenate(halves(returned_t), axis=0)
+        grad_out_t = grad_out_t + stacked(tall, hid_h[:, cols], hid_l[:, cols])
     for t in range(grad_in.shape[1] // LANES):
         out[pl.ds(t * deep, deep), :] = grad_in[:, t * LANES : (t + 1) * LANES]
-    hid = grad_out_t.shape[1] // 2
-    grad_out = jnp.where(which == 1, grad_out_t[:, hid:], grad_out_t[:, :hid]).T
+    grad_out = grad_out_t.T
     grad_out = jnp.where(last_element(grad_out) & (which == 1), loss[:1, :], grad_out)
     rows = deep * (grad_in.shape[1] // LANES)
     out[pl.ds(rows, hid), :] = grad_out
@@ -210,45 +218,45 @@
 
 def backward(grads_t, halo_h, halo_l, loc_h, loc_l, slope_o, slope_i, slope_e, hid_oh, hid_ol, hid_ih, hid_il, hid_eh, hid_el,
              in_oh, in_ol, in_ih, in_il, in_eh, in_el, wout_hh, wout_ll, loss,
-             pre_oh, pre_ol, pre_ih, pre_il, pre_eh, pre_el, total_out_t, ret_loc, out_e, give):
+             pre_oh, pre_ol, pre_ih, pre_il, pre_eh, pre_el, ret_loc, out_i, out_e, give):
     grads = grads_t[...]
     half = loc_h.shape[1]
     own = stacked(grads, loc_h[...], loc_l[...])
     near = stacked(grads, halo_h[:, :half], halo_l[:, :half])
     far = stacked(grads, halo_h[:, half:], halo_l[:, half:])
     ret_loc[...] = own
+    out_i[...] = near
     out_e[...] = far
     across = ((1,), (1,))
-    grad_out_t = 0.0
-    pre = []
-    for returned_t, slope, hid_h, hid_l, pre_h, pre_l in (
-        (own, slope_o, hid_oh, hid_ol, pre_oh, pre_ol),
-        (near, slope_i, hid_ih, hid_il, pre_ih, pre_il),
-        (far, slope_e, hid_eh, hid_el, pre_eh, pre_el),
+    parts = []
+    for returned_t, slope, hidden, inputs, pre_h, pre_l in (
+        (own, slope_o, (hid_oh, hid_ol), (in_oh, in_ol), pre_oh, pre_ol),
+        (near, slope_i, (hid_ih, hid_il), (in_ih, in_il), pre_ih, pre_il),
+        (far, slope_e, (hid_eh, hid_el), (in_eh, in_el), pre_eh, pre_el),
     ):
         both = jnp.concatenate(halves(returned_t.T), axis=1)
         hidden_grad = mm(both, wout_hh[...], across) + mm(both, wout_ll[...], across)
         high, low = halves(hidden_grad * slope[...])
         pre_h[...] = high
         pre_l[...] = low
-        pre.append((high, low))
-        tall = jnp.concatenate(halves(returned_t), axis=0)
-        grad_out_t = grad_out_t + stacked(tall, hid_h[...], hid_l[...])
-    total_out_t[...] = grad_out_t
+        parts.append((returned_t, hidden, inputs, (high, low)))
     other = 1 - lax.rem(lax.axis_index(AXIS), 2)
-    in_ts = ((in_oh, in_ol), (in_ih, in_il), (in_eh, in_el))
-    end = gradient_half(other, in_ts, pre, grad_out_t, loss, give)
+    end = gradient_half(other, parts, loss, give)
     classes = near.shape[0]
     for t in range(half // LANES):
         give[pl.ds(end + t * classes, classes), :] = near[:, t * LANES : (t + 1) * LANES]
 
 
-def backward_kept(in_oh, in_ol, in_ih, in_il, in_eh, in_el, pre_oh, pre_ol, pre_ih, pre_il, pre_eh, pre_el,
-                  total_out_t, loss, values, keep, logits):
+def backward_kept(hid_oh, hid_ol, hid_ih, hid_il, hid_eh, hid_el, in_oh, in_ol, in_ih, in_il, in_eh, in_el,
+                  pre_oh, pre_ol, pre_ih, pre_il, pre_eh, pre_el, ret_loc, out_i, out_e, loss, values,
+                  keep, logits):
     core = lax.rem(lax.axis_index(AXIS), 2)
-    in_ts = ((in_oh, in_ol), (in_ih, in_il), (in_eh, in_el))
-    pre = [(h[...], l[...]) for h, l in ((pre_oh, pre_ol), (pre_ih, pre_il), (pre_eh, pre_el))]
-    gradient_half(core, in_ts, pre, total_out_t[...], loss, keep)
+    parts = (
+        (ret_loc[...], (hid_oh, hid_ol), (in_oh, in_ol), (pre_oh[...], pre_ol[...])),
+        (out_i[...], (hid_ih, hid_il), (in_ih, in_il), (pre_ih[...], pre_il[...])),
+        (out_e[...], (hid_eh, hid_el), (in_eh, in_el), (pre_eh[...], pre_el[...])),
+    )
+    gradient_half(core, parts, loss, keep)
     logits[...] = values[...]
 
 
@@ -266,16 +274,8 @@
     out[...] = keep[...] + got[: keep.shape[0], :]
 
 
-def sum_repeated(received, passed, out, copied):
-    total = received[0]
-    for k in range(1, received.shape[0]):
-        total = total + received[k]
-    out[...] = jnp.broadcast_to(total[None], out.shape)
-    copied[...] = passed[...]
-
-
-def sum_repeated_after(received, after, out):
-    del after
+def sum_repeated(received, *refs):
+    out = refs[-1]
     total = received[0]
     for k in range(1, received.shape[0]):
         total = total + received[k]
@@ -378,11 +378,12 @@
     values, slope_e, *kept_e = layer_of(halo_h, halo_l, spread_e, logits_i, "forward_beside", 1)
     grads_t, loss = call(classify, [((2 * classes, nodes), BF16), ((8, LANES), F32)], [values, onehot])
     half = (deep * hid + hid * classes) // LANES // 2
+    hids = [*kept_o[:2], *kept_i[:2], *kept_e[:2]]
     in_ts = [in_oh, in_ol, *kept_i[2:], *kept_e[2:]]
-    *pre, total_out_t, ret_loc, out_e, give = call(
+    *pre, ret_loc, out_i, out_e, give = call(
         backward,
-        [wide_h] * 6 + [((classes, hid), F32), thin_t, thin_t, ((half + classes * (nodes // LANES), LANES), F32)],
-        [grads_t, halo_h, halo_l, loc_h, loc_l, slope_o, slope_i, slope_e, *kept_o[:2], *kept_i[:2], *kept_e[:2],
+        [wide_h] * 6 + [thin_t] * 3 + [((half + classes * (nodes // LANES), LANES), F32)],
+        [grads_t, halo_h, halo_l, loc_h, loc_l, slope_o, slope_i, slope_e, *hids,
          *in_ts, wout_hh, wout_ll, loss],
         flops=30 * nodes * nodes * deep,
     )
@@ -390,7 +391,7 @@
     keep, logits = call(
         backward_kept,
         [((half, LANES), F32), thin],
-        [*in_ts, *pre, total_out_t, loss, values],
+        [*hids, *in_ts, *pre, ret_loc, out_i, out_e, loss, values],
         flops=10 * nodes * nodes * deep,
     )
     big, mid = groups((X, Y), (X, Z)), groups((Z,), (Y,))
@@ -398,10 +399,10 @@
     shard = half // wide
     (mine,) = call(add_halves, [((half, LANES), F32)], [keep, got])
     received = exchange(mine.reshape(wide, shard, LANES), big)
-    summed, out_e = call(sum_repeated, [((narrow, shard, LANES), F32), thin_t], [received, out_e])
     ret_e = beside(out_e)
+    (summed,) = call(sum_repeated, [((narrow, shard, LANES), F32)], [received, ret_e], anywhere=1)
     received = exchange(summed, mid)
-    (summed,) = call(sum_repeated_after, [((wide, shard, LANES), F32)], [received, ret_e], anywhere=1)
+    (summed,) = call(sum_repeated, [((wide, shard, LANES), F32)], [received])
     own = exchange(summed, big).reshape(half, LANES)
     other = mate(own)
     (hidden_grad,) = call(

time: 108 us -> 108 us (level)
  blocking collectives: 54.1 us -> 32 us
  starting transfers between devices: 25.9 us -> 40.4 us
  waiting for transfers between devices: 3.62 us -> 10.9 us
    all_to_all x3 -> x2, blocking collectives: 54.1 us -> 32 us  [exchange(): lax.all_to_all(value, AXIS, 0, 0, axis_index_groups=members, tiled=True)]
    all_to_all x0 -> x1, starting transfers between devices: none -> 16.3 us  [exchange(): lax.all_to_all(value, AXIS, 0, 0, axis_index_groups=members, tiled=True)]
    ppermute x3, waiting for transfers between devices: 2.06 us -> 9.49 us  [beside(): return lax.ppermute(value, AXIS, pairs + [(b, a) for a, b in pairs])]
    ppermute x3, starting transfers between devices: 12.1 us -> 10 us  [beside(): return lax.ppermute(value, AXIS, pairs + [(b, a) for a, b in pairs])]
  transfers between devices with their start and end apart: 7 -> 8, of which waited for: 3 -> 5; matrix products, arithmetic and copies ran while one was open for 0% -> 0% of each run, Pallas kernels for 13% -> 13%
where the time goes in v6:
time: 108 us; the launch traced here: 107 us
  starting transfers between devices  40.4 us (37%)
  blocking collectives  32 us (30%)
  Pallas kernels  22.7 us (21%)
  waiting for transfers between devices  10.9 us (10%)
    all_to_all x2, blocking collectives, exchange(): lax.all_to_all(value, AXIS, 0, 0, axis_index_groups=members, tiled=True)  32 us
    pallas_call x15, Pallas kernels, call(): pl.pallas_call(body, out_shape=[jax.ShapeDtypeStruct(shape, kind) for sha...  22.7 us
    all_to_all x1, starting transfers between devices, exchange(): lax.all_to_all(value, AXIS, 0, 0, axis_index_groups=members, tiled=True)  16.3 us
    ppermute x4, starting transfers between devices, mate(): lax.ppermute(value, AXIS, [(i, i ^ 1) for i in range(lax.axis_size(AXIS))])  14.1 us
    ppermute x3, starting transfers between devices, beside(): return lax.ppermute(value, AXIS, pairs + [(b, a) for a, b in pairs])  10 us
    ppermute x3, waiting for transfers between devices, beside(): return lax.ppermute(value, AXIS, pairs + [(b, a) for a, b in pairs])  9.49 us
  transfers between devices with their start and end apart: 8, of which 5 were waited for; matrix products, arithmetic and copies ran while one was open for 0% of the time, Pallas kernels for 13%

profile of v6, /device:TPU:1, one launch (start us, length us, event | category | flops | bytes accessed | tf_op | source)
XLA Modules:
  0.0 107.0 jit_solution(18282520276433922046)
XLA Ops:
  0.6 4.6 %collective-permute-start = (f32[512,256]{1,0:T(8,128)}, f32[512,256]{1,0:T(8,128)S(1)}, u32[]{:S(2)}, u32[]{:S(2)}) collective-permute-start(f32[512,256]{1,0:T(8,128)} %features.1), channel_id=1, source_target_pairs={{1,2},{3,4},{5,6},{7,8},{9,10},{11,12},{13,14},{15,16},{17,18},{19... | collective-permute-start | bytes 1572872 | tf_op jit(solution)/shard_map/ppermute | solution.py:41
  5.2 4.6 %prepare.1 = (bf16[512,512]{1,0:T(8,128)(2,1)S(1)}, bf16[512,512]{1,0:T(8,128)(2,1)S(1)}, bf16[512,1024]{1,0:T(8,128)(2,1)S(1)}, bf16[512,1024]{1,0:T(8,128)(2,1...) custom-call(s32[2,6]{1,0:T(2,128)} %block_index.1, ...), custom_call_target="tpu_custom_call" | custom-call | flops 402653184 | bytes 4458552 | tf_op jit(solution)/shard_map/prepare/pallas_call | solution.py:308
  9.9 4.8 %collective-permute-start.1 = (f32[512,256]{1,0:T(8,128)S(1)}, f32[512,256]{1,0:T(8,128)S(1)}, u32[]{:S(2)}, u32[]{:S(2)}) collective-permute-start(f32[512,256]{1,0:T(8,128)S(1)} %get-tuple-element.57), channel_id=1, source_target_pairs={{0,1},{1,0},{2,3},{3,2},{4,5},{5,4},{6,7},{7,6},{8,9},{9,8},{10,11... | collective-permute-start | bytes 1572872 | tf_op jit(solution)/shard_map/ppermute | solution.py:36
  14.6 0.0 collective-permute-done.feat_e
  14.7 0.6 add_features.1.s_loc
  15.3 0.9 collective-permute-done.1.feat_i
  16.2 0.6 spread.1.spread_in
  16.7 2.3 %collective-permute-start.2 = (f32[512,256]{1,0:T(8,128)S(1)}, f32[512,256]{1,0:T(8,128)S(1)}, u32[]{:S(2)}, u32[]{:S(2)}) collective-permute-start(f32[512,256]{1,0:T(8,128)S(1)} %spread.1.spread_in), channel_id=1, source_target_pairs={{0,1},{1,0},{2,3},{3,2},{4,5},{5,4},{6,7},{7,6},{8,9},{9,8},{10,11... | collective-permute-start | bytes 1572872 | tf_op jit(solution)/shard_map/ppermute | solution.py:36
  19.0 2.1 %collective-permute-start.3 = (f32[512,256]{1,0:T(8,128)S(1)}, f32[512,256]{1,0:T(8,128)S(1)}, u32[]{:S(2)}, u32[]{:S(2)}) collective-permute-start(f32[512,256]{1,0:T(8,128)S(1)} %spread.1.spread_in), channel_id=1, source_target_pairs={{1,2},{3,4},{5,6},{7,8},{9,10},{11,12},{13,14},{15,16},{17,18},{19... | collective-permute-start | bytes 1572872 | tf_op jit(solution)/shard_map/ppermute | solution.py:41
  21.2 0.2 turn.1
  21.4 2.7 %forward_own.1 = (f32[512,128]{1,0:T(8,128)S(1)}, f32[512,512]{1,0:T(8,128)S(1)}, bf16[512,512]{1,0:T(8,128)(2,1)S(1)}, bf16[512,512]{1,0:T(8,128)(2,1)S(1)}) custom-call(bf16[512,512]{1,0:T(8,128)(2,1)S(1)} %get-tuple-element.52.high_band.loc_h, bf16[512,512]{1,0:T(8,128)(2,1)S(1)} %get-tuple-element.53.low_band.loc_l, f32[512,256]{1,0:T(8,128)S(1)} %spread.1.spread_in, ...), custom_call_target="tpu_custom_call" | custom-call | flops 1073741824 | bytes 2621440 | tf_op jit(solution)/shard_map/forward_own/pallas_call | solution.py:308
  24.1 0.0 collective-permute-done.2.spread_in
  24.1 2.7 %forward_mate.1 = (f32[512,128]{1,0:T(8,128)S(1)}, f32[512,512]{1,0:T(8,128)S(1)}, bf16[512,512]{1,0:T(8,128)(2,1)S(1)}, bf16[512,512]{1,0:T(8,128)(2,1)S(1)}, b...) custom-call(bf16[512,1024]{1,0:T(8,128)(2,1)S(1)} %get-tuple-element.54.halo_h.high_band, ...), custom_call_target="tpu_custom_call" | custom-call | flops 1073741824 | bytes 3670016 | tf_op jit(solution)/shard_map/forward_mate/pallas_call | solution.py:308
  26.8 2.8 %collective-permute-done.3.spread_in = f32[512,256]{1,0:T(8,128)S(1)} collective-permute-done((f32[512,256]{1,0:T(8,128)S(1)}, f32[512,256]{1,0:T(8,128)S(1)}, u32[]{:S(2)}, u32[]{:S(2)}) %collective-permute-start.3) | collective-permute-done | bytes 524320 | tf_op jit(solution)/shard_map/ppermute | solution.py:41
  29.5 2.7 %forward_beside.1 = (f32[512,128]{1,0:T(8,128)S(1)}, f32[512,512]{1,0:T(8,128)S(1)}, bf16[512,512]{1,0:T(8,128)(2,1)S(1)}, bf16[512,512]{1,0:T(8,128)(2,1)S(1)},...) custom-call(bf16[512,1024]{1,0:T(8,128)(2,1)S(1)} %get-tuple-element.54.halo_h.high_band, ...), custom_call_target="tpu_custom_call" | custom-call | flops 1073741824 | bytes 3670016 | tf_op jit(solution)/shard_map/forward_beside/pallas_call | solution.py:308
  32.3 0.3 classify.1
  32.6 3.1 %backward.1 = (bf16[512,512]{1,0:T(8,128)(2,1)S(1)}, bf16[512,512]{1,0:T(8,128)(2,1)S(1)}, bf16[512,512]{1,0:T(8,128)(2,1)S(1)}, bf16[512,512]{1,0:T(8,128)(2,1)...) custom-call(bf16[256,512]{1,0:T(8,128)(2,1)S(1)} %get-tuple-element., ...), custom_call_target="tpu_custom_call" | custom-call | flops 2013265920 | bytes 11800576 | tf_op jit(solution)/shard_map/backward/pallas_call | solution.py:308
  35.7 1.9 %collective-permute-start.4 = (f32[1280,128]{1,0:T(8,128)S(1)}, f32[1280,128]{1,0:T(8,128)S(1)}, u32[]{:S(2)}, u32[]{:S(2)}) collective-permute-start(f32[1280,128]{1,0:T(8,128)S(1)} %get-tuple-element.95), channel_id=1, source_target_pairs={{0,1},{1,0},{2,3},{3,2},{4,5},{5,4},{6,7},{7,6},{8,9},{9,8},{10,11... | collective-permute-start | bytes 1966088 | tf_op jit(solution)/shard_map/ppermute | solution.py:36
  37.6 1.9 %backward_kept.1 = (f32[768,128]{1,0:T(8,128)S(1)}, f32[512,128]{1,0:T(8,128)}) custom-call(bf16[512,512]{1,0:T(8,128)(2,1)S(1)} %get-tuple-element.62.hid_oh, bf16[512,512]{1,0:T(8,128)(2,1)S(1)} %get-tuple-element.63.hid_ol, bf16[512,512]{1,0:T(8,128)(2,1)S(1)} %get-tuple-element.65.hid_ih, bf16[512,512]{1,0:T(8,128)(2,1)S(1)} %get-tuple-element.66.hid_il, ...), custom_call_target="tpu_custom_call" | custom-call | flops 671088640 | bytes 8916992 | tf_op jit(solution)/shard_map/backward_kept/pallas_call | solution.py:308
  39.6 0.1 collective-permute-done.4.got
  39.7 0.8 add_halves.1
  40.5 16.3 %all-to-all-start = ((f32[32,24,128]{2,1,0:T(8,128)}), f32[32,24,128]{2,1,0:T(8,128)S(1)}, u32[]{:S(2)}, u32[]{:S(2)}) async-start(f32[32,24,128]{2,1,0:T(8,128)} %bitcast.1), calls=%async_computation | async-start | bytes 786432 | tf_op jit(solution)/shard_map/all_to_all | solution.py:55
  56.7 3.3 %collective-permute-start.5 = (f32[128,512]{1,0:T(8,128)S(1)}, f32[128,512]{1,0:T(8,128)S(1)}, u32[]{:S(2)}, u32[]{:S(2)}) collective-permute-start(f32[128,512]{1,0:T(8,128)S(1)} %get-tuple-element.92.out_e), channel_id=1, source_target_pairs={{1,2},{3,4},{5,6},{7,8},{9,10},{11,12},{13,14},{15,16},{17,18},{19... | collective-permute-start | bytes 786440 | tf_op jit(solution)/shard_map/ppermute | solution.py:41
  60.1 6.7 %collective-permute-done.5.refs_0_.ret_e = f32[128,512]{1,0:T(8,128)S(1)} collective-permute-done((f32[128,512]{1,0:T(8,128)S(1)}, f32[128,512]{1,0:T(8,128)S(1)}, u32[]{:S(2)}, u32[]{:S(2)}) %collective-permute-start.5) | collective-permute-done | bytes 262176 | tf_op jit(solution)/shard_map/ppermute | solution.py:41
  66.8 0.4 all-to-all-done.received
  67.3 12.9 %all_to_all.15.received = f32[8,24,128]{2,1,0:T(8,128)S(1)} all-to-all(f32[8,24,128]{2,1,0:T(8,128)S(1)} %sum_repeated.2), channel_id=1, replica_groups={{0,16,32,48,64,80,96,112},{2,18,34,50,66,82,98,114},{4,20,36,52,68,84,1..., dimensions={0} | all-to-all | bytes 196608 | tf_op jit(solution)/shard_map/all_to_all | solution.py:55
  80.2 19.1 %all_to_all.16 = f32[32,24,128]{2,1,0:T(8,128)S(1)} all-to-all(f32[32,24,128]{2,1,0:T(8,128)S(1)} %sum_repeated.3), channel_id=1, replica_groups={{0,2,4,6,8,10,12,14,128,130,132,134,136,138,140,142,256,258,260,262,264..., dimensions={0} | all-to-all | bytes 786432 | tf_op jit(solution)/shard_map/all_to_all | solution.py:55
  99.3 5.1 %collective-permute-start.6 = (f32[768,128]{1,0:T(8,128)S(1)}, f32[768,128]{1,0:T(8,128)S(1)}, u32[]{:S(2)}, u32[]{:S(2)}) collective-permute-start(f32[768,128]{1,0:T(8,128)S(1)} %bitcast.4), channel_id=1, source_target_pairs={{0,1},{1,0},{2,3},{3,2},{4,5},{5,4},{6,7},{7,6},{8,9},{9,8},{10,11... | collective-permute-start | bytes 1179656 | tf_op jit(solution)/shard_map/ppermute | solution.py:36
  104.4 1.5 %finish_hidden.1 = f32[512,512]{1,0:T(8,128)} custom-call(f32[128,512]{1,0:T(8,128)S(1)} %get-tuple-element.90.ret_loc, f32[128,512]{1,0:T(8,128)S(1)} %collective-permute-done.5.refs_0_.ret_e, f32[1280,128]{1,0:T(8,128)S(1)} %collective-permute-done.4.got, bf16[512,256]{1,0:T(8,128)(2,1)S(1)} %get-tuple-element.81.wout_hh, ...), custom_call_target="tpu_custom_call" | custom-call | flops 268435456 | bytes 1703936 | tf_op jit(solution)/shard_map/finish_hidden/pallas_call | solution.py:308
  105.9 0.0 collective-permute-done.6.other
  105.9 1.0 assemble.1
  (2 shorter events, 0.1 us)
Async XLA Ops:
  0.6 14.0 %collective-permute-start = (f32[512,256]{1,0:T(8,128)}, f32[512,256]{1,0:T(8,128)S(1)}, u32[]{:S(2)}, u32[]{:S(2)}) collective-permute-start(f32[512,256]{1,0:T(8,128)} %features.1), channel_id=1, source_target_pairs={{1,2},{3,4},{5,6},{7,8},{9,10},{11,12},{13,14},{15,16},{17,18},{19... | collective-permute-start | bytes 1572872 | tf_op jit(solution)/shard_map/ppermute | solution.py:41
  9.9 6.3 %collective-permute-start.1 = (f32[512,256]{1,0:T(8,128)S(1)}, f32[512,256]{1,0:T(8,128)S(1)}, u32[]{:S(2)}, u32[]{:S(2)}) collective-permute-start(f32[512,256]{1,0:T(8,128)S(1)} %get-tuple-element.57), channel_id=1, source_target_pairs={{0,1},{1,0},{2,3},{3,2},{4,5},{5,4},{6,7},{7,6},{8,9},{9,8},{10,11... | collective-permute-start | bytes 1572872 | tf_op jit(solution)/shard_map/ppermute | solution.py:36
  16.7 7.3 %collective-permute-start.2 = (f32[512,256]{1,0:T(8,128)S(1)}, f32[512,256]{1,0:T(8,128)S(1)}, u32[]{:S(2)}, u32[]{:S(2)}) collective-permute-start(f32[512,256]{1,0:T(8,128)S(1)} %spread.1.spread_in), channel_id=1, source_target_pairs={{0,1},{1,0},{2,3},{3,2},{4,5},{5,4},{6,7},{7,6},{8,9},{9,8},{10,11... | collective-permute-start | bytes 1572872 | tf_op jit(solution)/shard_map/ppermute | solution.py:36
  19.0 10.5 %collective-permute-start.3 = (f32[512,256]{1,0:T(8,128)S(1)}, f32[512,256]{1,0:T(8,128)S(1)}, u32[]{:S(2)}, u32[]{:S(2)}) collective-permute-start(f32[512,256]{1,0:T(8,128)S(1)} %spread.1.spread_in), channel_id=1, source_target_pairs={{1,2},{3,4},{5,6},{7,8},{9,10},{11,12},{13,14},{15,16},{17,18},{19... | collective-permute-start | bytes 1572872 | tf_op jit(solution)/shard_map/ppermute | solution.py:41
  35.7 4.0 %collective-permute-start.4 = (f32[1280,128]{1,0:T(8,128)S(1)}, f32[1280,128]{1,0:T(8,128)S(1)}, u32[]{:S(2)}, u32[]{:S(2)}) collective-permute-start(f32[1280,128]{1,0:T(8,128)S(1)} %get-tuple-element.95), channel_id=1, source_target_pairs={{0,1},{1,0},{2,3},{3,2},{4,5},{5,4},{6,7},{7,6},{8,9},{9,8},{10,11... | collective-permute-start | bytes 1966088 | tf_op jit(solution)/shard_map/ppermute | solution.py:36
  40.5 26.8 %all-to-all-start = ((f32[32,24,128]{2,1,0:T(8,128)}), f32[32,24,128]{2,1,0:T(8,128)S(1)}, u32[]{:S(2)}, u32[]{:S(2)}) async-start(f32[32,24,128]{2,1,0:T(8,128)} %bitcast.1), calls=%async_computation | async-start | bytes 786432 | tf_op jit(solution)/shard_map/all_to_all | solution.py:55
  56.7 10.1 %collective-permute-start.5 = (f32[128,512]{1,0:T(8,128)S(1)}, f32[128,512]{1,0:T(8,128)S(1)}, u32[]{:S(2)}, u32[]{:S(2)}) collective-permute-start(f32[128,512]{1,0:T(8,128)S(1)} %get-tuple-element.92.out_e), channel_id=1, source_target_pairs={{1,2},{3,4},{5,6},{7,8},{9,10},{11,12},{13,14},{15,16},{17,18},{19... | collective-permute-start | bytes 786440 | tf_op jit(solution)/shard_map/ppermute | solution.py:41
  99.3 6.6 %collective-permute-start.6 = (f32[768,128]{1,0:T(8,128)S(1)}, f32[768,128]{1,0:T(8,128)S(1)}, u32[]{:S(2)}, u32[]{:S(2)}) collective-permute-start(f32[768,128]{1,0:T(8,128)S(1)} %bitcast.4), channel_id=1, source_target_pairs={{0,1},{1,0},{2,3},{3,2},{4,5},{5,4},{6,7},{7,6},{8,9},{9,8},{10,11... | collective-permute-start | bytes 1179656 | tf_op jit(solution)/shard_map/ppermute | solution.py:36

commit v7 on v6

--- a/solution.py
+++ b/solution.py
@@ -270,10 +270,6 @@
     hidden_grad[...] = mm(both, wout_hh[...], across) + mm(both, wout_ll[...], across)
 
 
-def add_halves(keep, got, out):
-    out[...] = keep[...] + got[: keep.shape[0], :]
-
-
 def sum_repeated(received, *refs):
     out = refs[-1]
     total = received[0]
@@ -397,12 +393,11 @@
     big, mid = groups((X, Y), (X, Z)), groups((Z,), (Y,))
     wide, narrow = len(big[0]), len(mid[0])
     shard = half // wide
-    (mine,) = call(add_halves, [((half, LANES), F32)], [keep, got])
-    received = exchange(mine.reshape(wide, shard, LANES), big)
+    received = exchange((keep + got[:half]).reshape(wide, shard, LANES), big)
     ret_e = beside(out_e)
-    (summed,) = call(sum_repeated, [((narrow, shard, LANES), F32)], [received, ret_e], anywhere=1)
+    (summed,) = call(sum_repeated, [((narrow, shard, LANES), F32)], [received])
     received = exchange(summed, mid)
-    (summed,) = call(sum_repeated, [((wide, shard, LANES), F32)], [received])
+    (summed,) = call(sum_repeated, [((wide, shard, LANES), F32)], [received, ret_e], anywhere=1)
     own = exchange(summed, big).reshape(half, LANES)
     other = mate(own)
     (hidden_grad,) = call(

time: 108 us -> 107 us (level)
  blocking collectives: 32 us -> 16.2 us
  waiting for transfers between devices: 10.9 us -> 18.6 us
  starting transfers between devices: 40.4 us -> 47.1 us
    all_to_all x2 -> x1, blocking collectives: 32 us -> 16.2 us  [exchange(): lax.all_to_all(value, AXIS, 0, 0, axis_index_groups=members, tiled=True)]
    all_to_all x1 -> x2, waiting for transfers between devices: 0.43 us -> 14.8 us  [exchange(): lax.all_to_all(value, AXIS, 0, 0, axis_index_groups=members, tiled=True)]
    ppermute x3, waiting for transfers between devices: 9.49 us -> 2.75 us  [beside(): return lax.ppermute(value, AXIS, pairs + [(b, a) for a, b in pairs])]
    all_to_all x1 -> x2, starting transfers between devices: 16.3 us -> 21.8 us  [exchange(): lax.all_to_all(value, AXIS, 0, 0, axis_index_groups=members, tiled=True)]
    ppermute x4, starting transfers between devices: 14.1 us -> 15.3 us  [mate(): lax.ppermute(value, AXIS, [(i, i ^ 1) for i in range(lax.axis_size(AXIS))])]
    pallas_call x15 -> x14, Pallas kernels: 22.7 us -> 22.5 us  [call(): pl.pallas_call(body, out_shape=[jax.ShapeDtypeStruct(shape, kind) for sha...]
  transfers between devices with their start and end apart: 8 -> 9, of which waited for: 5 -> 5; matrix products, arithmetic and copies ran while one was open for 0% -> 0% of each run, Pallas kernels for 13% -> 14%
where the time goes in v7:
time: 107 us; the launch traced here: 106 us
  starting transfers between devices  47.1 us (44%)
  Pallas kernels  22.5 us (21%)
  waiting for transfers between devices  18.6 us (17%)
  blocking collectives  16.2 us (15%)
    pallas_call x14, Pallas kernels, call(): pl.pallas_call(body, out_shape=[jax.ShapeDtypeStruct(shape, kind) for sha...  22.5 us
    all_to_all x2, starting transfers between devices, exchange(): lax.all_to_all(value, AXIS, 0, 0, axis_index_groups=members, tiled=True)  21.8 us
    all_to_all x1, blocking collectives, exchange(): lax.all_to_all(value, AXIS, 0, 0, axis_index_groups=members, tiled=True)  16.2 us
    ppermute x4, starting transfers between devices, mate(): lax.ppermute(value, AXIS, [(i, i ^ 1) for i in range(lax.axis_size(AXIS))])  15.3 us
    all_to_all x2, waiting for transfers between devices, exchange(): lax.all_to_all(value, AXIS, 0, 0, axis_index_groups=members, tiled=True)  14.8 us
    ppermute x3, starting transfers between devices, beside(): return lax.ppermute(value, AXIS, pairs + [(b, a) for a, b in pairs])  9.95 us
    ppermute x3, waiting for transfers between devices, beside(): return lax.ppermute(value, AXIS, pairs + [(b, a) for a, b in pairs])  2.75 us
  transfers between devices with their start and end apart: 9, of which 5 were waited for; matrix products, arithmetic and copies ran while one was open for 0% of the time, Pallas kernels for 14%

profile of v7, /device:TPU:1, one launch (start us, length us, event | category | flops | bytes accessed | tf_op | source)
XLA Modules:
  0.0 106.1 jit_solution(1528128605982298851)
XLA Ops:
  0.6 4.6 %collective-permute-start = (f32[512,256]{1,0:T(8,128)}, f32[512,256]{1,0:T(8,128)S(1)}, u32[]{:S(2)}, u32[]{:S(2)}) collective-permute-start(f32[512,256]{1,0:T(8,128)} %features.1), channel_id=1, source_target_pairs={{1,2},{3,4},{5,6},{7,8},{9,10},{11,12},{13,14},{15,16},{17,18},{19... | collective-permute-start | bytes 1572872 | tf_op jit(solution)/shard_map/ppermute | solution.py:41
  5.2 4.5 %prepare.1 = (bf16[512,512]{1,0:T(8,128)(2,1)S(1)}, bf16[512,512]{1,0:T(8,128)(2,1)S(1)}, bf16[512,1024]{1,0:T(8,128)(2,1)S(1)}, bf16[512,1024]{1,0:T(8,128)(2,1...) custom-call(s32[2,6]{1,0:T(2,128)} %block_index.1, ...), custom_call_target="tpu_custom_call" | custom-call | flops 402653184 | bytes 4458552 | tf_op jit(solution)/shard_map/prepare/pallas_call | solution.py:304
  9.8 4.8 %collective-permute-start.1 = (f32[512,256]{1,0:T(8,128)S(1)}, f32[512,256]{1,0:T(8,128)S(1)}, u32[]{:S(2)}, u32[]{:S(2)}) collective-permute-start(f32[512,256]{1,0:T(8,128)S(1)} %get-tuple-element.57), channel_id=1, source_target_pairs={{0,1},{1,0},{2,3},{3,2},{4,5},{5,4},{6,7},{7,6},{8,9},{9,8},{10,11... | collective-permute-start | bytes 1572872 | tf_op jit(solution)/shard_map/ppermute | solution.py:36
  14.6 0.0 collective-permute-done.feat_e
  14.6 0.6 add_features.1.s_loc
  15.2 0.9 collective-permute-done.1.feat_i
  16.1 0.6 spread.1.spread_in
  16.7 2.3 %collective-permute-start.2 = (f32[512,256]{1,0:T(8,128)S(1)}, f32[512,256]{1,0:T(8,128)S(1)}, u32[]{:S(2)}, u32[]{:S(2)}) collective-permute-start(f32[512,256]{1,0:T(8,128)S(1)} %spread.1.spread_in), channel_id=1, source_target_pairs={{0,1},{1,0},{2,3},{3,2},{4,5},{5,4},{6,7},{7,6},{8,9},{9,8},{10,11... | collective-permute-start | bytes 1572872 | tf_op jit(solution)/shard_map/ppermute | solution.py:36
  19.0 2.1 %collective-permute-start.3 = (f32[512,256]{1,0:T(8,128)S(1)}, f32[512,256]{1,0:T(8,128)S(1)}, u32[]{:S(2)}, u32[]{:S(2)}) collective-permute-start(f32[512,256]{1,0:T(8,128)S(1)} %spread.1.spread_in), channel_id=1, source_target_pairs={{1,2},{3,4},{5,6},{7,8},{9,10},{11,12},{13,14},{15,16},{17,18},{19... | collective-permute-start | bytes 1572872 | tf_op jit(solution)/shard_map/ppermute | solution.py:41
  21.1 0.2 turn.1
  21.3 2.7 %forward_own.1 = (f32[512,128]{1,0:T(8,128)S(1)}, f32[512,512]{1,0:T(8,128)S(1)}, bf16[512,512]{1,0:T(8,128)(2,1)S(1)}, bf16[512,512]{1,0:T(8,128)(2,1)S(1)}) custom-call(bf16[512,512]{1,0:T(8,128)(2,1)S(1)} %get-tuple-element.52.high_band.loc_h, bf16[512,512]{1,0:T(8,128)(2,1)S(1)} %get-tuple-element.53.low_band.loc_l, f32[512,256]{1,0:T(8,128)S(1)} %spread.1.spread_in, ...), custom_call_target="tpu_custom_call" | custom-call | flops 1073741824 | bytes 2621440 | tf_op jit(solution)/shard_map/forward_own/pallas_call | solution.py:304
  24.0 0.0 collective-permute-done.2.spread_in
  24.0 2.7 %forward_mate.1 = (f32[512,128]{1,0:T(8,128)S(1)}, f32[512,512]{1,0:T(8,128)S(1)}, bf16[512,512]{1,0:T(8,128)(2,1)S(1)}, bf16[512,512]{1,0:T(8,128)(2,1)S(1)}, b...) custom-call(bf16[512,1024]{1,0:T(8,128)(2,1)S(1)} %get-tuple-element.54.halo_h.high_band, ...), custom_call_target="tpu_custom_call" | custom-call | flops 1073741824 | bytes 3670016 | tf_op jit(solution)/shard_map/forward_mate/pallas_call | solution.py:304
  26.7 2.7 %collective-permute-done.3.spread_in = f32[512,256]{1,0:T(8,128)S(1)} collective-permute-done((f32[512,256]{1,0:T(8,128)S(1)}, f32[512,256]{1,0:T(8,128)S(1)}, u32[]{:S(2)}, u32[]{:S(2)}) %collective-permute-start.3) | collective-permute-done | bytes 524320 | tf_op jit(solution)/shard_map/ppermute | solution.py:41
  29.5 2.7 %forward_beside.1 = (f32[512,128]{1,0:T(8,128)S(1)}, f32[512,512]{1,0:T(8,128)S(1)}, bf16[512,512]{1,0:T(8,128)(2,1)S(1)}, bf16[512,512]{1,0:T(8,128)(2,1)S(1)},...) custom-call(bf16[512,1024]{1,0:T(8,128)(2,1)S(1)} %get-tuple-element.54.halo_h.high_band, ...), custom_call_target="tpu_custom_call" | custom-call | flops 1073741824 | bytes 3670016 | tf_op jit(solution)/shard_map/forward_beside/pallas_call | solution.py:304
  32.2 0.3 classify.1
  32.5 3.1 %backward.1 = (bf16[512,512]{1,0:T(8,128)(2,1)S(1)}, bf16[512,512]{1,0:T(8,128)(2,1)S(1)}, bf16[512,512]{1,0:T(8,128)(2,1)S(1)}, bf16[512,512]{1,0:T(8,128)(2,1)...) custom-call(bf16[256,512]{1,0:T(8,128)(2,1)S(1)} %get-tuple-element., ...), custom_call_target="tpu_custom_call" | custom-call | flops 2013265920 | bytes 11800576 | tf_op jit(solution)/shard_map/backward/pallas_call | solution.py:304
  35.6 1.9 %collective-permute-start.4 = (f32[1280,128]{1,0:T(8,128)S(1)}, f32[1280,128]{1,0:T(8,128)S(1)}, u32[]{:S(2)}, u32[]{:S(2)}) collective-permute-start(f32[1280,128]{1,0:T(8,128)S(1)} %get-tuple-element.95), channel_id=1, source_target_pairs={{0,1},{1,0},{2,3},{3,2},{4,5},{5,4},{6,7},{7,6},{8,9},{9,8},{10,11... | collective-permute-start | bytes 1966088 | tf_op jit(solution)/shard_map/ppermute | solution.py:36
  37.5 1.9 %backward_kept.1 = (f32[768,128]{1,0:T(8,128)S(1)}, f32[512,128]{1,0:T(8,128)}) custom-call(bf16[512,512]{1,0:T(8,128)(2,1)S(1)} %get-tuple-element.62.hid_oh, bf16[512,512]{1,0:T(8,128)(2,1)S(1)} %get-tuple-element.63.hid_ol, bf16[512,512]{1,0:T(8,128)(2,1)S(1)} %get-tuple-element.65.hid_ih, bf16[512,512]{1,0:T(8,128)(2,1)S(1)} %get-tuple-element.66.hid_il, ...), custom_call_target="tpu_custom_call" | custom-call | flops 671088640 | bytes 8916992 | tf_op jit(solution)/shard_map/backward_kept/pallas_call | solution.py:304
  39.5 0.1 collective-permute-done.4.got
  39.6 0.8 slice_add_fusion
  40.4 16.3 %all-to-all-start = ((f32[32,24,128]{2,1,0:T(8,128)}), f32[32,24,128]{2,1,0:T(8,128)S(1)}, u32[]{:S(2)}, u32[]{:S(2)}) async-start(f32[32,24,128]{2,1,0:T(8,128)} %bitcast.1), calls=%async_computation | async-start | bytes 786432 | tf_op jit(solution)/shard_map/all_to_all | solution.py:55
  56.7 3.3 %collective-permute-start.5 = (f32[128,512]{1,0:T(8,128)S(1)}, f32[128,512]{1,0:T(8,128)S(1)}, u32[]{:S(2)}, u32[]{:S(2)}) collective-permute-start(f32[128,512]{1,0:T(8,128)S(1)} %get-tuple-element.92.out_e), channel_id=1, source_target_pairs={{1,2},{3,4},{5,6},{7,8},{9,10},{11,12},{13,14},{15,16},{17,18},{19... | collective-permute-start | bytes 786440 | tf_op jit(solution)/shard_map/ppermute | solution.py:41
  60.0 7.2 %all-to-all-done.received = f32[32,24,128]{2,1,0:T(8,128)S(1)} async-done(((f32[32,24,128]{2,1,0:T(8,128)}), f32[32,24,128]{2,1,0:T(8,128)S(1)}, u32[]{:S(2)}, u32[]{:S(2)}) %all-to-all-start) | async-done | bytes 393248 | tf_op jit(solution)/shard_map/all_to_all | solution.py:55
  67.2 0.7 sum_repeated.2
  67.9 5.5 %all-to-all-start.1 = ((f32[8,24,128]{2,1,0:T(8,128)}), f32[8,24,128]{2,1,0:T(8,128)S(1)}, u32[]{:S(2)}, u32[]{:S(2)}) async-start(f32[8,24,128]{2,1,0:T(8,128)} %sum_repeated.2), calls=%async_computation.1 | async-start | bytes 196608 | tf_op jit(solution)/shard_map/all_to_all | solution.py:55
  73.4 0.0 collective-permute-done.5.refs_0_.ret_e
  73.4 7.6 %all-to-all-done.1.received = f32[8,24,128]{2,1,0:T(8,128)S(1)} async-done(((f32[8,24,128]{2,1,0:T(8,128)}), f32[8,24,128]{2,1,0:T(8,128)S(1)}, u32[]{:S(2)}, u32[]{:S(2)}) %all-to-all-start.1) | async-done | bytes 98336 | tf_op jit(solution)/shard_map/all_to_all | solution.py:55
  81.1 16.2 %all_to_all.15 = f32[32,24,128]{2,1,0:T(8,128)S(1)} all-to-all(f32[32,24,128]{2,1,0:T(8,128)S(1)} %sum_repeated.3), channel_id=1, replica_groups={{0,2,4,6,8,10,12,14,128,130,132,134,136,138,140,142,256,258,260,262,264..., dimensions={0} | all-to-all | bytes 786432 | tf_op jit(solution)/shard_map/all_to_all | solution.py:55
  97.3 6.3 %collective-permute-start.6 = (f32[768,128]{1,0:T(8,128)S(1)}, f32[768,128]{1,0:T(8,128)S(1)}, u32[]{:S(2)}, u32[]{:S(2)}) collective-permute-start(f32[768,128]{1,0:T(8,128)S(1)} %bitcast.4), channel_id=1, source_target_pairs={{0,1},{1,0},{2,3},{3,2},{4,5},{5,4},{6,7},{7,6},{8,9},{9,8},{10,11... | collective-permute-start | bytes 1179656 | tf_op jit(solution)/shard_map/ppermute | solution.py:36
  103.6 1.5 %finish_hidden.1 = f32[512,512]{1,0:T(8,128)} custom-call(f32[128,512]{1,0:T(8,128)S(1)} %get-tuple-element.90.ret_loc, f32[128,512]{1,0:T(8,128)S(1)} %collective-permute-done.5.refs_0_.ret_e, f32[1280,128]{1,0:T(8,128)S(1)} %collective-permute-done.4.got, bf16[512,256]{1,0:T(8,128)(2,1)S(1)} %get-tuple-element.81.wout_hh, ...), custom_call_target="tpu_custom_call" | custom-call | flops 268435456 | bytes 1703936 | tf_op jit(solution)/shard_map/finish_hidden/pallas_call | solution.py:304
  105.0 0.0 collective-permute-done.6.other
  105.0 1.0 assemble.1
  (1 shorter events, 0.0 us)
Async XLA Ops:
  0.6 14.0 %collective-permute-start = (f32[512,256]{1,0:T(8,128)}, f32[512,256]{1,0:T(8,128)S(1)}, u32[]{:S(2)}, u32[]{:S(2)}) collective-permute-start(f32[512,256]{1,0:T(8,128)} %features.1), channel_id=1, source_target_pairs={{1,2},{3,4},{5,6},{7,8},{9,10},{11,12},{13,14},{15,16},{17,18},{19... | collective-permute-start | bytes 1572872 | tf_op jit(solution)/shard_map/ppermute | solution.py:41
  9.8 6.3 %collective-permute-start.1 = (f32[512,256]{1,0:T(8,128)S(1)}, f32[512,256]{1,0:T(8,128)S(1)}, u32[]{:S(2)}, u32[]{:S(2)}) collective-permute-start(f32[512,256]{1,0:T(8,128)S(1)} %get-tuple-element.57), channel_id=1, source_target_pairs={{0,1},{1,0},{2,3},{3,2},{4,5},{5,4},{6,7},{7,6},{8,9},{9,8},{10,11... | collective-permute-start | bytes 1572872 | tf_op jit(solution)/shard_map/ppermute | solution.py:36
  16.7 7.3 %collective-permute-start.2 = (f32[512,256]{1,0:T(8,128)S(1)}, f32[512,256]{1,0:T(8,128)S(1)}, u32[]{:S(2)}, u32[]{:S(2)}) collective-permute-start(f32[512,256]{1,0:T(8,128)S(1)} %spread.1.spread_in), channel_id=1, source_target_pairs={{0,1},{1,0},{2,3},{3,2},{4,5},{5,4},{6,7},{7,6},{8,9},{9,8},{10,11... | collective-permute-start | bytes 1572872 | tf_op jit(solution)/shard_map/ppermute | solution.py:36
  19.0 10.5 %collective-permute-start.3 = (f32[512,256]{1,0:T(8,128)S(1)}, f32[512,256]{1,0:T(8,128)S(1)}, u32[]{:S(2)}, u32[]{:S(2)}) collective-permute-start(f32[512,256]{1,0:T(8,128)S(1)} %spread.1.spread_in), channel_id=1, source_target_pairs={{1,2},{3,4},{5,6},{7,8},{9,10},{11,12},{13,14},{15,16},{17,18},{19... | collective-permute-start | bytes 1572872 | tf_op jit(solution)/shard_map/ppermute | solution.py:41
  35.6 4.0 %collective-permute-start.4 = (f32[1280,128]{1,0:T(8,128)S(1)}, f32[1280,128]{1,0:T(8,128)S(1)}, u32[]{:S(2)}, u32[]{:S(2)}) collective-permute-start(f32[1280,128]{1,0:T(8,128)S(1)} %get-tuple-element.95), channel_id=1, source_target_pairs={{0,1},{1,0},{2,3},{3,2},{4,5},{5,4},{6,7},{7,6},{8,9},{9,8},{10,11... | collective-permute-start | bytes 1966088 | tf_op jit(solution)/shard_map/ppermute | solution.py:36
  40.4 26.8 %all-to-all-start = ((f32[32,24,128]{2,1,0:T(8,128)}), f32[32,24,128]{2,1,0:T(8,128)S(1)}, u32[]{:S(2)}, u32[]{:S(2)}) async-start(f32[32,24,128]{2,1,0:T(8,128)} %bitcast.1), calls=%async_computation | async-start | bytes 786432 | tf_op jit(solution)/shard_map/all_to_all | solution.py:55
  56.7 16.7 %collective-permute-start.5 = (f32[128,512]{1,0:T(8,128)S(1)}, f32[128,512]{1,0:T(8,128)S(1)}, u32[]{:S(2)}, u32[]{:S(2)}) collective-permute-start(f32[128,512]{1,0:T(8,128)S(1)} %get-tuple-element.92.out_e), channel_id=1, source_target_pairs={{1,2},{3,4},{5,6},{7,8},{9,10},{11,12},{13,14},{15,16},{17,18},{19... | collective-permute-start | bytes 786440 | tf_op jit(solution)/shard_map/ppermute | solution.py:41
  67.9 13.1 %all-to-all-start.1 = ((f32[8,24,128]{2,1,0:T(8,128)}), f32[8,24,128]{2,1,0:T(8,128)S(1)}, u32[]{:S(2)}, u32[]{:S(2)}) async-start(f32[8,24,128]{2,1,0:T(8,128)} %sum_repeated.2), calls=%async_computation.1 | async-start | bytes 196608 | tf_op jit(solution)/shard_map/all_to_all | solution.py:55
  97.3 7.8 %collective-permute-start.6 = (f32[768,128]{1,0:T(8,128)S(1)}, f32[768,128]{1,0:T(8,128)S(1)}, u32[]{:S(2)}, u32[]{:S(2)}) collective-permute-start(f32[768,128]{1,0:T(8,128)S(1)} %bitcast.4), channel_id=1, source_target_pairs={{0,1},{1,0},{2,3},{3,2},{4,5},{5,4},{6,7},{7,6},{8,9},{9,8},{10,11... | collective-permute-start | bytes 1179656 | tf_op jit(solution)/shard_map/ppermute | solution.py:36

commit v8 on v7

--- a/solution.py
+++ b/solution.py
@@ -397,7 +397,8 @@
     ret_e = beside(out_e)
     (summed,) = call(sum_repeated, [((narrow, shard, LANES), F32)], [received])
     received = exchange(summed, mid)
-    (summed,) = call(sum_repeated, [((wide, shard, LANES), F32)], [received, ret_e], anywhere=1)
+    (summed,) = call(sum_repeated, [((1, shard, LANES), F32)], [received])
+    (summed,) = call(sum_repeated, [((wide, shard, LANES), F32)], [summed, ret_e], anywhere=1)
     own = exchange(summed, big).reshape(half, LANES)
     other = mate(own)
     (hidden_grad,) = call(

time: 107 us -> 106 us (level)
  blocking collectives: 16.2 us -> 29.2 us
  waiting for transfers between devices: 18.6 us -> 10.8 us
  starting transfers between devices: 47.1 us -> 41.7 us
    all_to_all x1 -> x2, blocking collectives: 16.2 us -> 29.2 us  [exchange(): lax.all_to_all(value, AXIS, 0, 0, axis_index_groups=members, tiled=True)]
    all_to_all x2 -> x1, waiting for transfers between devices: 14.8 us -> 7.04 us  [exchange(): lax.all_to_all(value, AXIS, 0, 0, axis_index_groups=members, tiled=True)]
    all_to_all x2 -> x1, starting transfers between devices: 21.8 us -> 16.2 us  [exchange(): lax.all_to_all(value, AXIS, 0, 0, axis_index_groups=members, tiled=True)]
    pallas_call x14 -> x15, Pallas kernels: 22.5 us -> 21.9 us  [call(): pl.pallas_call(body, out_shape=[jax.ShapeDtypeStruct(shape, kind) for sha...]
  transfers between devices with their start and end apart: 9 -> 8, of which waited for: 5 -> 4; matrix products, arithmetic and copies ran while one was open for 0% -> 0% of each run, Pallas kernels for 14% -> 13%
where the time goes in v8:
time: 106 us; the launch traced here: 105 us
  starting transfers between devices  41.7 us (39%)
  blocking collectives  29.2 us (28%)
  Pallas kernels  21.9 us (21%)
  waiting for transfers between devices  10.8 us (10%)
    all_to_all x2, blocking collectives, exchange(): lax.all_to_all(value, AXIS, 0, 0, axis_index_groups=members, tiled=True)  29.2 us
    pallas_call x15, Pallas kernels, call(): pl.pallas_call(body, out_shape=[jax.ShapeDtypeStruct(shape, kind) for sha...  21.9 us
    all_to_all x1, starting transfers between devices, exchange(): lax.all_to_all(value, AXIS, 0, 0, axis_index_groups=members, tiled=True)  16.2 us
    ppermute x4, starting transfers between devices, mate(): lax.ppermute(value, AXIS, [(i, i ^ 1) for i in range(lax.axis_size(AXIS))])  15.4 us
    ppermute x3, starting transfers between devices, beside(): return lax.ppermute(value, AXIS, pairs + [(b, a) for a, b in pairs])  10.1 us
    all_to_all x1, waiting for transfers between devices, exchange(): lax.all_to_all(value, AXIS, 0, 0, axis_index_groups=members, tiled=True)  7.04 us
    ppermute x3, waiting for transfers between devices, beside(): return lax.ppermute(value, AXIS, pairs + [(b, a) for a, b in pairs])  2.75 us
  transfers between devices with their start and end apart: 8, of which 4 were waited for; matrix products, arithmetic and copies ran while one was open for 0% of the time, Pallas kernels for 13%

profile of v8, /device:TPU:1, one launch (start us, length us, event | category | flops | bytes accessed | tf_op | source)
XLA Modules:
  0.0 105.3 jit_solution(6076858500742963470)
XLA Ops:
  0.6 4.6 %collective-permute-start = (f32[512,256]{1,0:T(8,128)}, f32[512,256]{1,0:T(8,128)S(1)}, u32[]{:S(2)}, u32[]{:S(2)}) collective-permute-start(f32[512,256]{1,0:T(8,128)} %features.1), channel_id=1, source_target_pairs={{1,2},{3,4},{5,6},{7,8},{9,10},{11,12},{13,14},{15,16},{17,18},{19... | collective-permute-start | bytes 1572872 | tf_op jit(solution)/shard_map/ppermute | solution.py:41
  5.2 4.5 %prepare.1 = (bf16[512,512]{1,0:T(8,128)(2,1)S(1)}, bf16[512,512]{1,0:T(8,128)(2,1)S(1)}, bf16[512,1024]{1,0:T(8,128)(2,1)S(1)}, bf16[512,1024]{1,0:T(8,128)(2,1...) custom-call(s32[2,6]{1,0:T(2,128)} %block_index.1, ...), custom_call_target="tpu_custom_call" | custom-call | flops 402653184 | bytes 4458552 | tf_op jit(solution)/shard_map/prepare/pallas_call | solution.py:304
  9.8 4.9 %collective-permute-start.1 = (f32[512,256]{1,0:T(8,128)S(1)}, f32[512,256]{1,0:T(8,128)S(1)}, u32[]{:S(2)}, u32[]{:S(2)}) collective-permute-start(f32[512,256]{1,0:T(8,128)S(1)} %get-tuple-element.57), channel_id=1, source_target_pairs={{0,1},{1,0},{2,3},{3,2},{4,5},{5,4},{6,7},{7,6},{8,9},{9,8},{10,11... | collective-permute-start | bytes 1572872 | tf_op jit(solution)/shard_map/ppermute | solution.py:36
  14.7 0.0 collective-permute-done.feat_e
  14.7 0.6 add_features.1.s_loc
  15.3 0.9 collective-permute-done.1.feat_i
  16.2 0.6 spread.1.spread_in
  16.8 2.3 %collective-permute-start.2 = (f32[512,256]{1,0:T(8,128)S(1)}, f32[512,256]{1,0:T(8,128)S(1)}, u32[]{:S(2)}, u32[]{:S(2)}) collective-permute-start(f32[512,256]{1,0:T(8,128)S(1)} %spread.1.spread_in), channel_id=1, source_target_pairs={{0,1},{1,0},{2,3},{3,2},{4,5},{5,4},{6,7},{7,6},{8,9},{9,8},{10,11... | collective-permute-start | bytes 1572872 | tf_op jit(solution)/shard_map/ppermute | solution.py:36
  19.1 2.1 %collective-permute-start.3 = (f32[512,256]{1,0:T(8,128)S(1)}, f32[512,256]{1,0:T(8,128)S(1)}, u32[]{:S(2)}, u32[]{:S(2)}) collective-permute-start(f32[512,256]{1,0:T(8,128)S(1)} %spread.1.spread_in), channel_id=1, source_target_pairs={{1,2},{3,4},{5,6},{7,8},{9,10},{11,12},{13,14},{15,16},{17,18},{19... | collective-permute-start | bytes 1572872 | tf_op jit(solution)/shard_map/ppermute | solution.py:41
  21.2 0.2 turn.1
  21.4 2.7 %forward_own.1 = (f32[512,128]{1,0:T(8,128)S(1)}, f32[512,512]{1,0:T(8,128)S(1)}, bf16[512,512]{1,0:T(8,128)(2,1)S(1)}, bf16[512,512]{1,0:T(8,128)(2,1)S(1)}) custom-call(bf16[512,512]{1,0:T(8,128)(2,1)S(1)} %get-tuple-element.52.high_band.loc_h, bf16[512,512]{1,0:T(8,128)(2,1)S(1)} %get-tuple-element.53.low_band.loc_l, f32[512,256]{1,0:T(8,128)S(1)} %spread.1.spread_in, ...), custom_call_target="tpu_custom_call" | custom-call | flops 1073741824 | bytes 2621440 | tf_op jit(solution)/shard_map/forward_own/pallas_call | solution.py:304
  24.2 0.0 collective-permute-done.2.spread_in
  24.2 2.7 %forward_mate.1 = (f32[512,128]{1,0:T(8,128)S(1)}, f32[512,512]{1,0:T(8,128)S(1)}, bf16[512,512]{1,0:T(8,128)(2,1)S(1)}, bf16[512,512]{1,0:T(8,128)(2,1)S(1)}, b...) custom-call(bf16[512,1024]{1,0:T(8,128)(2,1)S(1)} %get-tuple-element.54.halo_h.high_band, ...), custom_call_target="tpu_custom_call" | custom-call | flops 1073741824 | bytes 3670016 | tf_op jit(solution)/shard_map/forward_mate/pallas_call | solution.py:304
  26.9 2.7 %collective-permute-done.3.spread_in = f32[512,256]{1,0:T(8,128)S(1)} collective-permute-done((f32[512,256]{1,0:T(8,128)S(1)}, f32[512,256]{1,0:T(8,128)S(1)}, u32[]{:S(2)}, u32[]{:S(2)}) %collective-permute-start.3) | collective-permute-done | bytes 524320 | tf_op jit(solution)/shard_map/ppermute | solution.py:41
  29.6 2.7 %forward_beside.1 = (f32[512,128]{1,0:T(8,128)S(1)}, f32[512,512]{1,0:T(8,128)S(1)}, bf16[512,512]{1,0:T(8,128)(2,1)S(1)}, bf16[512,512]{1,0:T(8,128)(2,1)S(1)},...) custom-call(bf16[512,1024]{1,0:T(8,128)(2,1)S(1)} %get-tuple-element.54.halo_h.high_band, ...), custom_call_target="tpu_custom_call" | custom-call | flops 1073741824 | bytes 3670016 | tf_op jit(solution)/shard_map/forward_beside/pallas_call | solution.py:304
  32.3 0.3 classify.1
  32.7 3.1 %backward.1 = (bf16[512,512]{1,0:T(8,128)(2,1)S(1)}, bf16[512,512]{1,0:T(8,128)(2,1)S(1)}, bf16[512,512]{1,0:T(8,128)(2,1)S(1)}, bf16[512,512]{1,0:T(8,128)(2,1)...) custom-call(bf16[256,512]{1,0:T(8,128)(2,1)S(1)} %get-tuple-element., ...), custom_call_target="tpu_custom_call" | custom-call | flops 2013265920 | bytes 11800576 | tf_op jit(solution)/shard_map/backward/pallas_call | solution.py:304
  35.8 1.9 %collective-permute-start.4 = (f32[1280,128]{1,0:T(8,128)S(1)}, f32[1280,128]{1,0:T(8,128)S(1)}, u32[]{:S(2)}, u32[]{:S(2)}) collective-permute-start(f32[1280,128]{1,0:T(8,128)S(1)} %get-tuple-element.95), channel_id=1, source_target_pairs={{0,1},{1,0},{2,3},{3,2},{4,5},{5,4},{6,7},{7,6},{8,9},{9,8},{10,11... | collective-permute-start | bytes 1966088 | tf_op jit(solution)/shard_map/ppermute | solution.py:36
  37.7 1.9 %backward_kept.1 = (f32[768,128]{1,0:T(8,128)S(1)}, f32[512,128]{1,0:T(8,128)}) custom-call(bf16[512,512]{1,0:T(8,128)(2,1)S(1)} %get-tuple-element.62.hid_oh, bf16[512,512]{1,0:T(8,128)(2,1)S(1)} %get-tuple-element.63.hid_ol, bf16[512,512]{1,0:T(8,128)(2,1)S(1)} %get-tuple-element.65.hid_ih, bf16[512,512]{1,0:T(8,128)(2,1)S(1)} %get-tuple-element.66.hid_il, ...), custom_call_target="tpu_custom_call" | custom-call | flops 671088640 | bytes 8916992 | tf_op jit(solution)/shard_map/backward_kept/pallas_call | solution.py:304
  39.6 0.1 collective-permute-done.4.got
  39.7 0.8 slice_add_fusion
  40.5 16.2 %all-to-all-start = ((f32[32,24,128]{2,1,0:T(8,128)}), f32[32,24,128]{2,1,0:T(8,128)S(1)}, u32[]{:S(2)}, u32[]{:S(2)}) async-start(f32[32,24,128]{2,1,0:T(8,128)} %bitcast.1), calls=%async_computation | async-start | bytes 786432 | tf_op jit(solution)/shard_map/all_to_all | solution.py:55
  56.7 3.4 %collective-permute-start.5 = (f32[128,512]{1,0:T(8,128)S(1)}, f32[128,512]{1,0:T(8,128)S(1)}, u32[]{:S(2)}, u32[]{:S(2)}) collective-permute-start(f32[128,512]{1,0:T(8,128)S(1)} %get-tuple-element.92.out_e), channel_id=1, source_target_pairs={{1,2},{3,4},{5,6},{7,8},{9,10},{11,12},{13,14},{15,16},{17,18},{19... | collective-permute-start | bytes 786440 | tf_op jit(solution)/shard_map/ppermute | solution.py:41
  60.1 7.0 %all-to-all-done.received = f32[32,24,128]{2,1,0:T(8,128)S(1)} async-done(((f32[32,24,128]{2,1,0:T(8,128)}), f32[32,24,128]{2,1,0:T(8,128)S(1)}, u32[]{:S(2)}, u32[]{:S(2)}) %all-to-all-start) | async-done | bytes 393248 | tf_op jit(solution)/shard_map/all_to_all | solution.py:55
  67.2 13.0 %all_to_all.15.received = f32[8,24,128]{2,1,0:T(8,128)S(1)} all-to-all(f32[8,24,128]{2,1,0:T(8,128)S(1)} %sum_repeated.3), channel_id=1, replica_groups={{0,16,32,48,64,80,96,112},{2,18,34,50,66,82,98,114},{4,20,36,52,68,84,1..., dimensions={0} | all-to-all | bytes 196608 | tf_op jit(solution)/shard_map/all_to_all | solution.py:55
  80.2 0.0 collective-permute-done.5.refs_0_.ret_e
  80.2 16.2 %all_to_all.16 = f32[32,24,128]{2,1,0:T(8,128)S(1)} all-to-all(f32[32,24,128]{2,1,0:T(8,128)S(1)} %sum_repeated.5), channel_id=1, replica_groups={{0,2,4,6,8,10,12,14,128,130,132,134,136,138,140,142,256,258,260,262,264..., dimensions={0} | all-to-all | bytes 786432 | tf_op jit(solution)/shard_map/all_to_all | solution.py:55
  96.5 6.3 %collective-permute-start.6 = (f32[768,128]{1,0:T(8,128)S(1)}, f32[768,128]{1,0:T(8,128)S(1)}, u32[]{:S(2)}, u32[]{:S(2)}) collective-permute-start(f32[768,128]{1,0:T(8,128)S(1)} %bitcast.4), channel_id=1, source_target_pairs={{0,1},{1,0},{2,3},{3,2},{4,5},{5,4},{6,7},{7,6},{8,9},{9,8},{10,11... | collective-permute-start | bytes 1179656 | tf_op jit(solution)/shard_map/ppermute | solution.py:36
  102.7 1.5 %finish_hidden.1 = f32[512,512]{1,0:T(8,128)} custom-call(f32[128,512]{1,0:T(8,128)S(1)} %get-tuple-element.90.ret_loc, f32[128,512]{1,0:T(8,128)S(1)} %collective-permute-done.5.refs_0_.ret_e, f32[1280,128]{1,0:T(8,128)S(1)} %collective-permute-done.4.got, bf16[512,256]{1,0:T(8,128)(2,1)S(1)} %get-tuple-element.81.wout_hh, ...), custom_call_target="tpu_custom_call" | custom-call | flops 268435456 | bytes 1703936 | tf_op jit(solution)/shard_map/finish_hidden/pallas_call | solution.py:304
  104.2 0.0 collective-permute-done.6.other
  104.2 1.0 assemble.1
  (3 shorter events, 0.1 us)
Async XLA Ops:
  0.6 14.1 %collective-permute-start = (f32[512,256]{1,0:T(8,128)}, f32[512,256]{1,0:T(8,128)S(1)}, u32[]{:S(2)}, u32[]{:S(2)}) collective-permute-start(f32[512,256]{1,0:T(8,128)} %features.1), channel_id=1, source_target_pairs={{1,2},{3,4},{5,6},{7,8},{9,10},{11,12},{13,14},{15,16},{17,18},{19... | collective-permute-start | bytes 1572872 | tf_op jit(solution)/shard_map/ppermute | solution.py:41
  9.8 6.5 %collective-permute-start.1 = (f32[512,256]{1,0:T(8,128)S(1)}, f32[512,256]{1,0:T(8,128)S(1)}, u32[]{:S(2)}, u32[]{:S(2)}) collective-permute-start(f32[512,256]{1,0:T(8,128)S(1)} %get-tuple-element.57), channel_id=1, source_target_pairs={{0,1},{1,0},{2,3},{3,2},{4,5},{5,4},{6,7},{7,6},{8,9},{9,8},{10,11... | collective-permute-start | bytes 1572872 | tf_op jit(solution)/shard_map/ppermute | solution.py:36
  16.8 7.3 %collective-permute-start.2 = (f32[512,256]{1,0:T(8,128)S(1)}, f32[512,256]{1,0:T(8,128)S(1)}, u32[]{:S(2)}, u32[]{:S(2)}) collective-permute-start(f32[512,256]{1,0:T(8,128)S(1)} %spread.1.spread_in), channel_id=1, source_target_pairs={{0,1},{1,0},{2,3},{3,2},{4,5},{5,4},{6,7},{7,6},{8,9},{9,8},{10,11... | collective-permute-start | bytes 1572872 | tf_op jit(solution)/shard_map/ppermute | solution.py:36
  19.1 10.5 %collective-permute-start.3 = (f32[512,256]{1,0:T(8,128)S(1)}, f32[512,256]{1,0:T(8,128)S(1)}, u32[]{:S(2)}, u32[]{:S(2)}) collective-permute-start(f32[512,256]{1,0:T(8,128)S(1)} %spread.1.spread_in), channel_id=1, source_target_pairs={{1,2},{3,4},{5,6},{7,8},{9,10},{11,12},{13,14},{15,16},{17,18},{19... | collective-permute-start | bytes 1572872 | tf_op jit(solution)/shard_map/ppermute | solution.py:41
  35.8 4.0 %collective-permute-start.4 = (f32[1280,128]{1,0:T(8,128)S(1)}, f32[1280,128]{1,0:T(8,128)S(1)}, u32[]{:S(2)}, u32[]{:S(2)}) collective-permute-start(f32[1280,128]{1,0:T(8,128)S(1)} %get-tuple-element.95), channel_id=1, source_target_pairs={{0,1},{1,0},{2,3},{3,2},{4,5},{5,4},{6,7},{7,6},{8,9},{9,8},{10,11... | collective-permute-start | bytes 1966088 | tf_op jit(solution)/shard_map/ppermute | solution.py:36
  40.5 26.6 %all-to-all-start = ((f32[32,24,128]{2,1,0:T(8,128)}), f32[32,24,128]{2,1,0:T(8,128)S(1)}, u32[]{:S(2)}, u32[]{:S(2)}) async-start(f32[32,24,128]{2,1,0:T(8,128)} %bitcast.1), calls=%async_computation | async-start | bytes 786432 | tf_op jit(solution)/shard_map/all_to_all | solution.py:55
  56.7 23.5 %collective-permute-start.5 = (f32[128,512]{1,0:T(8,128)S(1)}, f32[128,512]{1,0:T(8,128)S(1)}, u32[]{:S(2)}, u32[]{:S(2)}) collective-permute-start(f32[128,512]{1,0:T(8,128)S(1)} %get-tuple-element.92.out_e), channel_id=1, source_target_pairs={{1,2},{3,4},{5,6},{7,8},{9,10},{11,12},{13,14},{15,16},{17,18},{19... | collective-permute-start | bytes 786440 | tf_op jit(solution)/shard_map/ppermute | solution.py:41
  96.5 7.7 %collective-permute-start.6 = (f32[768,128]{1,0:T(8,128)S(1)}, f32[768,128]{1,0:T(8,128)S(1)}, u32[]{:S(2)}, u32[]{:S(2)}) collective-permute-start(f32[768,128]{1,0:T(8,128)S(1)} %bitcast.4), channel_id=1, source_target_pairs={{0,1},{1,0},{2,3},{3,2},{4,5},{5,4},{6,7},{7,6},{8,9},{9,8},{10,11... | collective-permute-start | bytes 1179656 | tf_op jit(solution)/shard_map/ppermute | solution.py:36

commit v9 on v8

--- a/solution.py
+++ b/solution.py
@@ -134,11 +134,14 @@
     out[...] = s_loc[...] + mm(he, high) + mm(he, low) + mm(le, high)
 
 
-def spread(halo_h, halo_l, s_loc, feat_i, spread_in):
+def spread(halo_h, halo_l, s_loc, feat_i, spread_in, longer):
     half = feat_i.shape[0]
     high, low = halves(feat_i[...])
     hi, li = halo_h[:, :half], halo_l[:, :half]
-    spread_in[...] = s_loc[...] + mm(hi, high) + mm(hi, low) + mm(li, high)
+    value = s_loc[...] + mm(hi, high) + mm(hi, low) + mm(li, high)
+    spread_in[...] = value
+    longer[:half, :] = value
+    longer[half:, :] = jnp.zeros_like(longer[half:, :])
 
 
 def layer(spread_in, win_h, win_l):
@@ -156,17 +159,18 @@
 
 def forward(high_band, low_band, spread_in, win_h, win_l, wout_hl, logits_before,
             scores_sum, slope, hid_h, hid_l, *in_t, first, part):
-    hidden, slope[...] = layer(spread_in[...], win_h, win_l)
+    nodes = slope.shape[0]
+    rows_in = spread_in[:nodes, :]
+    hidden, slope[...] = layer(rows_in, win_h, win_l)
     high, low = halves(hidden)
     hid_h[...] = high
     hid_l[...] = low
     pair = jnp.concatenate(halves(fold(mm(high, wout_hl[...]) + mm(low, wout_hl[...]))), axis=1)
-    nodes = spread_in.shape[0]
     cols = slice(part * nodes, (part + 1) * nodes)
     logits = fold(mm(high_band[:, cols], pair) + mm(low_band[:, cols], pair))
     scores_sum[...] = logits if first else logits_before[...] + logits
     if in_t:
-        turn(spread_in, *in_t)
+        turn(rows_in, *in_t)
 
 
 def turn(spread_in, in_th, in_tl):
@@ -297,10 +301,11 @@
     grad_out[end, :] = jnp.where(there, -others, value)
 
 
-def call(body, outs, args, scalars=0, anywhere=0, flops=0, scratch=(), space=pltpu.VMEM, name=""):
+def call(body, outs, args, scalars=0, anywhere=0, flops=0, scratch=(), space=pltpu.VMEM, cheap=False, name=""):
     smem = pl.BlockSpec(memory_space=pltpu.SMEM)
     vmem = pl.BlockSpec(memory_space=pltpu.VMEM)
-    moved = sum(a.size * a.dtype.itemsize for a in args)
+    moved = 0 if cheap else sum(a.size * a.dtype.itemsize for a in args)
+    flops = 0 if cheap else flops
     return pl.pallas_call(
         body,
         out_shape=[jax.ShapeDtypeStruct(shape, kind) for shape, kind in outs],
@@ -353,10 +358,10 @@
     )
     wide_f, wide_h = ((nodes, hid), F32), ((nodes, hid), BF16)
     thin, thin_t, in_t = ((nodes, classes), F32), ((classes, nodes), F32), ((deep, nodes), BF16)
-    (spread_in,) = call(
-        spread, [((nodes, deep), F32)], [halo_h, halo_l, s_loc, feat_i], flops=6 * nodes * nodes * deep
-    )
-    spread_e = beside(spread_in)
+    spread_in, longer = call(
+        spread, [((nodes, deep), F32), ((nodes + 8, deep), F32)], [halo_h, halo_l, s_loc, feat_i], flops=6 * nodes * nodes * deep
+    )
+    spread_e = beside(longer)
     spread_i = mate(spread_in)
     in_oh, in_ol = call(turn, [in_t, in_t], [spread_in])
 
@@ -366,6 +371,7 @@
             [thin, wide_f, wide_h, wide_h] + [in_t] * (0 if name == "forward_own" else 2),
             [high, low, rows_in, win_h, win_l, wout_hl, before],
             flops=16 * nodes * nodes * deep,
+            cheap=name == "forward_mate",
             name=name,
         )
 

time: 106 us -> 104 us (0.981)
  waiting for transfers between devices: 10.8 us -> 8.67 us
    ppermute x3, waiting for transfers between devices: 2.75 us -> 0.89 us  [beside(): return lax.ppermute(value, AXIS, pairs + [(b, a) for a, b in pairs])]
  transfers between devices with their start and end apart: 8 -> 8, of which waited for: 4 -> 4; matrix products, arithmetic and copies ran while one was open for 0% -> 0% of each run, Pallas kernels for 13% -> 14%
where the time goes in v9:
time: 104 us
  starting transfers between devices  42 us (40%)
  blocking collectives  29.1 us (28%)
  Pallas kernels  22 us (21%)
  waiting for transfers between devices  8.67 us (8%)
    all_to_all x2, blocking collectives, exchange(): lax.all_to_all(value, AXIS, 0, 0, axis_index_groups=members, tiled=True)  29.1 us
    pallas_call x15, Pallas kernels, call(): pl.pallas_call(body, out_shape=[jax.ShapeDtypeStruct(shape, kind) for sha...  22 us
    all_to_all x1, starting transfers between devices, exchange(): lax.all_to_all(value, AXIS, 0, 0, axis_index_groups=members, tiled=True)  16.5 us
    ppermute x4, starting transfers between devices, mate(): lax.ppermute(value, AXIS, [(i, i ^ 1) for i in range(lax.axis_size(AXIS))])  15.2 us
    ppermute x3, starting transfers between devices, beside(): return lax.ppermute(value, AXIS, pairs + [(b, a) for a, b in pairs])  10.3 us
    all_to_all x1, waiting for transfers between devices, exchange(): lax.all_to_all(value, AXIS, 0, 0, axis_index_groups=members, tiled=True)  6.74 us
  transfers between devices with their start and end apart: 8, of which 4 were waited for; matrix products, arithmetic and copies ran while one was open for 0% of the time, Pallas kernels for 14%

profile of v9, /device:TPU:1, one launch (start us, length us, event | category | flops | bytes accessed | tf_op | source)
XLA Modules:
  0.0 103.6 jit_solution(17401214660236434652)
XLA Ops:
  0.6 4.6 %collective-permute-start = (f32[512,256]{1,0:T(8,128)}, f32[512,256]{1,0:T(8,128)S(1)}, u32[]{:S(2)}, u32[]{:S(2)}) collective-permute-start(f32[512,256]{1,0:T(8,128)} %features.1), channel_id=1, source_target_pairs={{1,2},{3,4},{5,6},{7,8},{9,10},{11,12},{13,14},{15,16},{17,18},{19... | collective-permute-start | bytes 1572872 | tf_op jit(solution)/shard_map/ppermute | solution.py:41
  5.2 4.6 %prepare.1 = (bf16[512,512]{1,0:T(8,128)(2,1)S(1)}, bf16[512,512]{1,0:T(8,128)(2,1)S(1)}, bf16[512,1024]{1,0:T(8,128)(2,1)S(1)}, bf16[512,1024]{1,0:T(8,128)(2,1...) custom-call(s32[2,6]{1,0:T(2,128)} %block_index.1, ...), custom_call_target="tpu_custom_call" | custom-call | flops 402653184 | bytes 4458552 | tf_op jit(solution)/shard_map/prepare/pallas_call | solution.py:309
  9.8 4.9 %collective-permute-start.1 = (f32[512,256]{1,0:T(8,128)S(1)}, f32[512,256]{1,0:T(8,128)S(1)}, u32[]{:S(2)}, u32[]{:S(2)}) collective-permute-start(f32[512,256]{1,0:T(8,128)S(1)} %get-tuple-element.59), channel_id=1, source_target_pairs={{0,1},{1,0},{2,3},{3,2},{4,5},{5,4},{6,7},{7,6},{8,9},{9,8},{10,11... | collective-permute-start | bytes 1572872 | tf_op jit(solution)/shard_map/ppermute | solution.py:36
  14.7 0.0 collective-permute-done.feat_e
  14.8 0.6 add_features.1.s_loc
  15.4 0.9 collective-permute-done.1.feat_i
  16.3 0.6 spread.1
  16.9 1.9 %collective-permute-start.3 = (f32[520,256]{1,0:T(8,128)S(1)}, f32[520,256]{1,0:T(8,128)S(1)}, u32[]{:S(2)}, u32[]{:S(2)}) collective-permute-start(f32[520,256]{1,0:T(8,128)S(1)} %get-tuple-element.70), channel_id=1, source_target_pairs={{1,2},{3,4},{5,6},{7,8},{9,10},{11,12},{13,14},{15,16},{17,18},{19... | collective-permute-start | bytes 1597448 | tf_op jit(solution)/shard_map/ppermute | solution.py:41
  18.8 2.1 %collective-permute-start.2 = (f32[512,256]{1,0:T(8,128)S(1)}, f32[512,256]{1,0:T(8,128)S(1)}, u32[]{:S(2)}, u32[]{:S(2)}) collective-permute-start(f32[512,256]{1,0:T(8,128)S(1)} %get-tuple-element.60.spread_in), channel_id=1, source_target_pairs={{0,1},{1,0},{2,3},{3,2},{4,5},{5,4},{6,7},{7,6},{8,9},{9,8},{10,11... | collective-permute-start | bytes 1572872 | tf_op jit(solution)/shard_map/ppermute | solution.py:36
  20.9 0.2 turn.1
  21.1 2.7 %forward_own.1 = (f32[512,128]{1,0:T(8,128)S(1)}, f32[512,512]{1,0:T(8,128)S(1)}, bf16[512,512]{1,0:T(8,128)(2,1)S(1)}, bf16[512,512]{1,0:T(8,128)(2,1)S(1)}) custom-call(bf16[512,512]{1,0:T(8,128)(2,1)S(1)} %get-tuple-element.54.high_band.loc_h, bf16[512,512]{1,0:T(8,128)(2,1)S(1)} %get-tuple-element.55.low_band.loc_l, ...), custom_call_target="tpu_custom_call" | custom-call | flops 1073741824 | bytes 2621440 | tf_op jit(solution)/shard_map/forward_own/pallas_call | solution.py:309
  23.8 0.0 collective-permute-done.2.spread_in
  23.8 2.7 %forward_mate.1 = (f32[512,128]{1,0:T(8,128)S(1)}, f32[512,512]{1,0:T(8,128)S(1)}, bf16[512,512]{1,0:T(8,128)(2,1)S(1)}, bf16[512,512]{1,0:T(8,128)(2,1)S(1)}, b...) custom-call(bf16[512,1024]{1,0:T(8,128)(2,1)S(1)} %get-tuple-element.56.halo_h.high_band, ...), custom_call_target="tpu_custom_call" | custom-call | tf_op jit(solution)/shard_map/forward_mate/pallas_call | solution.py:309
  26.6 0.9 collective-permute-done.3.spread_in
  27.4 2.7 %forward_beside.1 = (f32[512,128]{1,0:T(8,128)S(1)}, f32[512,512]{1,0:T(8,128)S(1)}, bf16[512,512]{1,0:T(8,128)(2,1)S(1)}, bf16[512,512]{1,0:T(8,128)(2,1)S(1)},...) custom-call(bf16[512,1024]{1,0:T(8,128)(2,1)S(1)} %get-tuple-element.56.halo_h.high_band, ...), custom_call_target="tpu_custom_call" | custom-call | flops 1073741824 | bytes 3678208 | tf_op jit(solution)/shard_map/forward_beside/pallas_call | solution.py:309
  30.2 0.3 classify.1
  30.5 3.1 %backward.1 = (bf16[512,512]{1,0:T(8,128)(2,1)S(1)}, bf16[512,512]{1,0:T(8,128)(2,1)S(1)}, bf16[512,512]{1,0:T(8,128)(2,1)S(1)}, bf16[512,512]{1,0:T(8,128)(2,1)...) custom-call(bf16[256,512]{1,0:T(8,128)(2,1)S(1)} %get-tuple-element., ...), custom_call_target="tpu_custom_call" | custom-call | flops 2013265920 | bytes 11800576 | tf_op jit(solution)/shard_map/backward/pallas_call | solution.py:309
  33.7 1.9 %collective-permute-start.4 = (f32[1280,128]{1,0:T(8,128)S(1)}, f32[1280,128]{1,0:T(8,128)S(1)}, u32[]{:S(2)}, u32[]{:S(2)}) collective-permute-start(f32[1280,128]{1,0:T(8,128)S(1)} %get-tuple-element.99), channel_id=1, source_target_pairs={{0,1},{1,0},{2,3},{3,2},{4,5},{5,4},{6,7},{7,6},{8,9},{9,8},{10,11... | collective-permute-start | bytes 1966088 | tf_op jit(solution)/shard_map/ppermute | solution.py:36
  35.6 1.9 %backward_kept.1 = (f32[768,128]{1,0:T(8,128)S(1)}, f32[512,128]{1,0:T(8,128)}) custom-call(bf16[512,512]{1,0:T(8,128)(2,1)S(1)} %get-tuple-element.65.hid_oh, bf16[512,512]{1,0:T(8,128)(2,1)S(1)} %get-tuple-element.66.hid_ol, bf16[512,512]{1,0:T(8,128)(2,1)S(1)} %get-tuple-element.68.hid_ih, bf16[512,512]{1,0:T(8,128)(2,1)S(1)} %get-tuple-element.69.hid_il, ...), custom_call_target="tpu_custom_call" | custom-call | flops 671088640 | bytes 8916992 | tf_op jit(solution)/shard_map/backward_kept/pallas_call | solution.py:309
  37.5 0.1 collective-permute-done.4.got
  37.6 0.8 slice_add_fusion
  38.4 16.5 %all-to-all-start = ((f32[32,24,128]{2,1,0:T(8,128)}), f32[32,24,128]{2,1,0:T(8,128)S(1)}, u32[]{:S(2)}, u32[]{:S(2)}) async-start(f32[32,24,128]{2,1,0:T(8,128)} %bitcast.1), calls=%async_computation | async-start | bytes 786432 | tf_op jit(solution)/shard_map/all_to_all | solution.py:55
  55.0 3.8 %collective-permute-start.5 = (f32[128,512]{1,0:T(8,128)S(1)}, f32[128,512]{1,0:T(8,128)S(1)}, u32[]{:S(2)}, u32[]{:S(2)}) collective-permute-start(f32[128,512]{1,0:T(8,128)S(1)} %get-tuple-element.96.out_e), channel_id=1, source_target_pairs={{1,2},{3,4},{5,6},{7,8},{9,10},{11,12},{13,14},{15,16},{17,18},{19... | collective-permute-start | bytes 786440 | tf_op jit(solution)/shard_map/ppermute | solution.py:41
  58.7 6.7 %all-to-all-done.received = f32[32,24,128]{2,1,0:T(8,128)S(1)} async-done(((f32[32,24,128]{2,1,0:T(8,128)}), f32[32,24,128]{2,1,0:T(8,128)S(1)}, u32[]{:S(2)}, u32[]{:S(2)}) %all-to-all-start) | async-done | bytes 393248 | tf_op jit(solution)/shard_map/all_to_all | solution.py:55
  65.5 12.9 %all_to_all.15.received = f32[8,24,128]{2,1,0:T(8,128)S(1)} all-to-all(f32[8,24,128]{2,1,0:T(8,128)S(1)} %sum_repeated.3), channel_id=1, replica_groups={{0,16,32,48,64,80,96,112},{2,18,34,50,66,82,98,114},{4,20,36,52,68,84,1..., dimensions={0} | all-to-all | bytes 196608 | tf_op jit(solution)/shard_map/all_to_all | solution.py:55
  78.4 0.0 collective-permute-done.5.refs_0_.ret_e
  78.5 16.2 %all_to_all.16 = f32[32,24,128]{2,1,0:T(8,128)S(1)} all-to-all(f32[32,24,128]{2,1,0:T(8,128)S(1)} %sum_repeated.5), channel_id=1, replica_groups={{0,2,4,6,8,10,12,14,128,130,132,134,136,138,140,142,256,258,260,262,264..., dimensions={0} | all-to-all | bytes 786432 | tf_op jit(solution)/shard_map/all_to_all | solution.py:55
  94.7 6.3 %collective-permute-start.6 = (f32[768,128]{1,0:T(8,128)S(1)}, f32[768,128]{1,0:T(8,128)S(1)}, u32[]{:S(2)}, u32[]{:S(2)}) collective-permute-start(f32[768,128]{1,0:T(8,128)S(1)} %bitcast.4), channel_id=1, source_target_pairs={{0,1},{1,0},{2,3},{3,2},{4,5},{5,4},{6,7},{7,6},{8,9},{9,8},{10,11... | collective-permute-start | bytes 1179656 | tf_op jit(solution)/shard_map/ppermute | solution.py:36
  101.0 1.5 %finish_hidden.1 = f32[512,512]{1,0:T(8,128)} custom-call(f32[128,512]{1,0:T(8,128)S(1)} %get-tuple-element.94.ret_loc, f32[128,512]{1,0:T(8,128)S(1)} %collective-permute-done.5.refs_0_.ret_e, f32[1280,128]{1,0:T(8,128)S(1)} %collective-permute-done.4.got, bf16[512,256]{1,0:T(8,128)(2,1)S(1)} %get-tuple-element.85.wout_hh, ...), custom_call_target="tpu_custom_call" | custom-call | flops 268435456 | bytes 1703936 | tf_op jit(solution)/shard_map/finish_hidden/pallas_call | solution.py:309
  102.4 0.0 collective-permute-done.6.other
  102.4 1.0 assemble.1
  (3 shorter events, 0.1 us)
Async XLA Ops:
  0.6 14.1 %collective-permute-start = (f32[512,256]{1,0:T(8,128)}, f32[512,256]{1,0:T(8,128)S(1)}, u32[]{:S(2)}, u32[]{:S(2)}) collective-permute-start(f32[512,256]{1,0:T(8,128)} %features.1), channel_id=1, source_target_pairs={{1,2},{3,4},{5,6},{7,8},{9,10},{11,12},{13,14},{15,16},{17,18},{19... | collective-permute-start | bytes 1572872 | tf_op jit(solution)/shard_map/ppermute | solution.py:41
  9.8 6.5 %collective-permute-start.1 = (f32[512,256]{1,0:T(8,128)S(1)}, f32[512,256]{1,0:T(8,128)S(1)}, u32[]{:S(2)}, u32[]{:S(2)}) collective-permute-start(f32[512,256]{1,0:T(8,128)S(1)} %get-tuple-element.59), channel_id=1, source_target_pairs={{0,1},{1,0},{2,3},{3,2},{4,5},{5,4},{6,7},{7,6},{8,9},{9,8},{10,11... | collective-permute-start | bytes 1572872 | tf_op jit(solution)/shard_map/ppermute | solution.py:36
  16.9 10.6 %collective-permute-start.3 = (f32[520,256]{1,0:T(8,128)S(1)}, f32[520,256]{1,0:T(8,128)S(1)}, u32[]{:S(2)}, u32[]{:S(2)}) collective-permute-start(f32[520,256]{1,0:T(8,128)S(1)} %get-tuple-element.70), channel_id=1, source_target_pairs={{1,2},{3,4},{5,6},{7,8},{9,10},{11,12},{13,14},{15,16},{17,18},{19... | collective-permute-start | bytes 1597448 | tf_op jit(solution)/shard_map/ppermute | solution.py:41
  18.8 5.0 %collective-permute-start.2 = (f32[512,256]{1,0:T(8,128)S(1)}, f32[512,256]{1,0:T(8,128)S(1)}, u32[]{:S(2)}, u32[]{:S(2)}) collective-permute-start(f32[512,256]{1,0:T(8,128)S(1)} %get-tuple-element.60.spread_in), channel_id=1, source_target_pairs={{0,1},{1,0},{2,3},{3,2},{4,5},{5,4},{6,7},{7,6},{8,9},{9,8},{10,11... | collective-permute-start | bytes 1572872 | tf_op jit(solution)/shard_map/ppermute | solution.py:36
  33.7 4.0 %collective-permute-start.4 = (f32[1280,128]{1,0:T(8,128)S(1)}, f32[1280,128]{1,0:T(8,128)S(1)}, u32[]{:S(2)}, u32[]{:S(2)}) collective-permute-start(f32[1280,128]{1,0:T(8,128)S(1)} %get-tuple-element.99), channel_id=1, source_target_pairs={{0,1},{1,0},{2,3},{3,2},{4,5},{5,4},{6,7},{7,6},{8,9},{9,8},{10,11... | collective-permute-start | bytes 1966088 | tf_op jit(solution)/shard_map/ppermute | solution.py:36
  38.4 27.0 %all-to-all-start = ((f32[32,24,128]{2,1,0:T(8,128)}), f32[32,24,128]{2,1,0:T(8,128)S(1)}, u32[]{:S(2)}, u32[]{:S(2)}) async-start(f32[32,24,128]{2,1,0:T(8,128)} %bitcast.1), calls=%async_computation | async-start | bytes 786432 | tf_op jit(solution)/shard_map/all_to_all | solution.py:55
  55.0 23.5 %collective-permute-start.5 = (f32[128,512]{1,0:T(8,128)S(1)}, f32[128,512]{1,0:T(8,128)S(1)}, u32[]{:S(2)}, u32[]{:S(2)}) collective-permute-start(f32[128,512]{1,0:T(8,128)S(1)} %get-tuple-element.96.out_e), channel_id=1, source_target_pairs={{1,2},{3,4},{5,6},{7,8},{9,10},{11,12},{13,14},{15,16},{17,18},{19... | collective-permute-start | bytes 786440 | tf_op jit(solution)/shard_map/ppermute | solution.py:41
  94.7 7.8 %collective-permute-start.6 = (f32[768,128]{1,0:T(8,128)S(1)}, f32[768,128]{1,0:T(8,128)S(1)}, u32[]{:S(2)}, u32[]{:S(2)}) collective-permute-start(f32[768,128]{1,0:T(8,128)S(1)} %bitcast.4), channel_id=1, source_target_pairs={{0,1},{1,0},{2,3},{3,2},{4,5},{5,4},{6,7},{7,6},{8,9},{9,8},{10,11... | collective-permute-start | bytes 1179656 | tf_op jit(solution)/shard_map/ppermute | solution.py:36

commit v10 on v9

--- a/solution.py
+++ b/solution.py
@@ -252,8 +252,8 @@
 
 
 def backward_kept(hid_oh, hid_ol, hid_ih, hid_il, hid_eh, hid_el, in_oh, in_ol, in_ih, in_il, in_eh, in_el,
-                  pre_oh, pre_ol, pre_ih, pre_il, pre_eh, pre_el, ret_loc, out_i, out_e, loss, values,
-                  keep, logits):
+                  pre_oh, pre_ol, pre_ih, pre_il, pre_eh, pre_el, ret_loc, out_i, out_e, loss,
+                  keep):
     core = lax.rem(lax.axis_index(AXIS), 2)
     parts = (
         (ret_loc[...], (hid_oh, hid_ol), (in_oh, in_ol), (pre_oh[...], pre_ol[...])),
@@ -261,7 +261,22 @@
         (out_e[...], (hid_eh, hid_el), (in_eh, in_el), (pre_eh[...], pre_el[...])),
     )
     gradient_half(core, parts, loss, keep)
+
+
+def from_beside(*refs):
+    halo_h, halo_l, loc_h, loc_l, spread_e, win_h, win_l, wout_hl, wout_hh, wout_ll, logits_i, onehot = refs[:12]
+    slope_o, slope_i, hid_oh, hid_ol, hid_ih, hid_il, in_oh, in_ol, in_ih, in_il = refs[12:22]
+    values, slope_e, hid_eh, hid_el, in_eh, in_el, grads_t, loss = refs[22:30]
+    forward(halo_h, halo_l, spread_e, win_h, win_l, wout_hl, logits_i,
+            values, slope_e, hid_eh, hid_el, in_eh, in_el, first=False, part=1)
+    classify(values, onehot, grads_t, loss)
+    backward(grads_t, halo_h, halo_l, loc_h, loc_l, slope_o, slope_i, slope_e, hid_oh, hid_ol, hid_ih, hid_il, hid_eh, hid_el,
+             in_oh, in_ol, in_ih, in_il, in_eh, in_el, wout_hh, wout_ll, loss, *refs[30:])
+
+
+def put_logits(values, logits, token):
     logits[...] = values[...]
+    token[...] = values[:8, :]
 
 
 def finish_hidden(ret_loc, ret_e, got, wout_hh, wout_ll, hidden_grad):
@@ -301,7 +316,7 @@
     grad_out[end, :] = jnp.where(there, -others, value)
 
 
-def call(body, outs, args, scalars=0, anywhere=0, flops=0, scratch=(), space=pltpu.VMEM, cheap=False, name=""):
+def call(body, outs, args, scalars=0, anywhere=0, flops=0, scratch=(), space=pltpu.VMEM, cheap=False, limit=VMEM_LIMIT, name=""):
     smem = pl.BlockSpec(memory_space=pltpu.SMEM)
     vmem = pl.BlockSpec(memory_space=pltpu.VMEM)
     moved = 0 if cheap else sum(a.size * a.dtype.itemsize for a in args)
@@ -315,7 +330,7 @@
         out_specs=[smem if shape == (1, 1) else vmem for shape, _ in outs],
         scratch_shapes=scratch,
         cost_estimate=pl.CostEstimate(flops=flops, bytes_accessed=moved, transcendentals=0),
-        compiler_params=pltpu.CompilerParams(vmem_limit_bytes=VMEM_LIMIT),
+        compiler_params=pltpu.CompilerParams(vmem_limit_bytes=limit),
         name=name or body.__name__,
     )(*args)
 
@@ -377,23 +392,24 @@
 
     logits_o, slope_o, *kept_o = layer_of(loc_h, loc_l, spread_in, onehot, "forward_own", 0)
     logits_i, slope_i, *kept_i = layer_of(halo_h, halo_l, spread_i, logits_o, "forward_mate", 0)
-    values, slope_e, *kept_e = layer_of(halo_h, halo_l, spread_e, logits_i, "forward_beside", 1)
-    grads_t, loss = call(classify, [((2 * classes, nodes), BF16), ((8, LANES), F32)], [values, onehot])
     half = (deep * hid + hid * classes) // LANES // 2
-    hids = [*kept_o[:2], *kept_i[:2], *kept_e[:2]]
-    in_ts = [in_oh, in_ol, *kept_i[2:], *kept_e[2:]]
-    *pre, ret_loc, out_i, out_e, give = call(
-        backward,
-        [wide_h] * 6 + [thin_t] * 3 + [((half + classes * (nodes // LANES), LANES), F32)],
-        [grads_t, halo_h, halo_l, loc_h, loc_l, slope_o, slope_i, slope_e, *hids,
-         *in_ts, wout_hh, wout_ll, loss],
-        flops=30 * nodes * nodes * deep,
-    )
+    values, slope_e, hid_eh, hid_el, in_eh, in_el, _, loss, *pre, ret_loc, out_i, out_e, give = call(
+        from_beside,
+        [thin, wide_f, wide_h, wide_h, in_t, in_t, ((2 * classes, nodes), BF16), ((8, LANES), F32)]
+        + [wide_h] * 6 + [thin_t] * 3 + [((half + classes * (nodes // LANES), LANES), F32)],
+        [halo_h, halo_l, loc_h, loc_l, spread_e, win_h, win_l, wout_hl, wout_hh, wout_ll, logits_i, onehot,
+         slope_o, slope_i, *kept_o[:2], *kept_i[:2], in_oh, in_ol, *kept_i[2:]],
+        flops=46 * nodes * nodes * deep,
+        limit=VMEM_LIMIT,
+    )
+    hids = [*kept_o[:2], *kept_i[:2], hid_eh, hid_el]
+    in_ts = [in_oh, in_ol, *kept_i[2:], in_eh, in_el]
     got = mate(give)
-    keep, logits = call(
+    logits, token = call(put_logits, [thin, ((8, LANES), F32)], [values])
+    (keep,) = call(
         backward_kept,
-        [((half, LANES), F32), thin],
-        [*hids, *in_ts, *pre, ret_loc, out_i, out_e, loss, values],
+        [((half, LANES), F32)],
+        [*hids, *in_ts, *pre, ret_loc, out_i, out_e, loss],
         flops=10 * nodes * nodes * deep,
     )
     big, mid = groups((X, Y), (X, Z)), groups((Z,), (Y,))
@@ -401,7 +417,7 @@
     shard = half // wide
     received = exchange((keep + got[:half]).reshape(wide, shard, LANES), big)
     ret_e = beside(out_e)
-    (summed,) = call(sum_repeated, [((narrow, shard, LANES), F32)], [received])
+    (summed,) = call(sum_repeated, [((narrow, shard, LANES), F32)], [received, token])
     received = exchange(summed, mid)
     (summed,) = call(sum_repeated, [((1, shard, LANES), F32)], [received])
     (summed,) = call(sum_repeated, [((wide, shard, LANES), F32)], [summed, ret_e], anywhere=1)

time: 104 us -> 105 us (level)
  Pallas kernels: 22 us -> 23.2 us
    pallas_call x15 -> x14, Pallas kernels: 22 us -> 23.2 us  [call(): pl.pallas_call(body, out_shape=[jax.ShapeDtypeStruct(shape, kind) for sha...]
where the time goes in v10:
time: 105 us; the launch traced here: 104 us
  starting transfers between devices  41.4 us (39%)
  blocking collectives  29.5 us (28%)
  Pallas kernels  23.2 us (22%)
  waiting for transfers between devices  8.6 us (8%)
    all_to_all x2, blocking collectives, exchange(): lax.all_to_all(value, AXIS, 0, 0, axis_index_groups=members, tiled=True)  29.5 us
    pallas_call x14, Pallas kernels, call(): pl.pallas_call(body, out_shape=[jax.ShapeDtypeStruct(shape, kind) for sha...  23.2 us
    all_to_all x1, starting transfers between devices, exchange(): lax.all_to_all(value, AXIS, 0, 0, axis_index_groups=members, tiled=True)  16.4 us
    ppermute x4, starting transfers between devices, mate(): lax.ppermute(value, AXIS, [(i, i ^ 1) for i in range(lax.axis_size(AXIS))])  14.7 us
    ppermute x3, starting transfers between devices, beside(): return lax.ppermute(value, AXIS, pairs + [(b, a) for a, b in pairs])  10.2 us
    all_to_all x1, waiting for transfers between devices, exchange(): lax.all_to_all(value, AXIS, 0, 0, axis_index_groups=members, tiled=True)  6.04 us
  transfers between devices with their start and end apart: 8, of which 4 were waited for; matrix products, arithmetic and copies ran while one was open for 0% of the time, Pallas kernels for 14%

profile of v10, /device:TPU:1, one launch (start us, length us, event | category | flops | bytes accessed | tf_op | source)
XLA Modules:
  0.0 104.4 jit_solution(8181343196271405307)
XLA Ops:
  0.6 4.6 %collective-permute-start = (f32[512,256]{1,0:T(8,128)}, f32[512,256]{1,0:T(8,128)S(1)}, u32[]{:S(2)}, u32[]{:S(2)}) collective-permute-start(f32[512,256]{1,0:T(8,128)} %features.1), channel_id=1, source_target_pairs={{1,2},{3,4},{5,6},{7,8},{9,10},{11,12},{13,14},{15,16},{17,18},{19... | collective-permute-start | bytes 1572872 | tf_op jit(solution)/shard_map/ppermute | solution.py:41
  5.2 4.5 %prepare.1 = (bf16[512,512]{1,0:T(8,128)(2,1)S(1)}, bf16[512,512]{1,0:T(8,128)(2,1)S(1)}, bf16[512,1024]{1,0:T(8,128)(2,1)S(1)}, bf16[512,1024]{1,0:T(8,128)(2,1...) custom-call(s32[2,6]{1,0:T(2,128)} %block_index.1, ...), custom_call_target="tpu_custom_call" | custom-call | flops 402653184 | bytes 4458552 | tf_op jit(solution)/shard_map/prepare/pallas_call | solution.py:324
  9.8 4.9 %collective-permute-start.1 = (f32[512,256]{1,0:T(8,128)S(1)}, f32[512,256]{1,0:T(8,128)S(1)}, u32[]{:S(2)}, u32[]{:S(2)}) collective-permute-start(f32[512,256]{1,0:T(8,128)S(1)} %get-tuple-element.57), channel_id=1, source_target_pairs={{0,1},{1,0},{2,3},{3,2},{4,5},{5,4},{6,7},{7,6},{8,9},{9,8},{10,11... | collective-permute-start | bytes 1572872 | tf_op jit(solution)/shard_map/ppermute | solution.py:36
  14.6 0.0 collective-permute-done.feat_e
  14.7 0.6 add_features.1.s_loc
  15.2 0.9 collective-permute-done.1.feat_i
  16.2 0.6 spread.1
  16.8 1.9 %collective-permute-start.2 = (f32[520,256]{1,0:T(8,128)S(1)}, f32[520,256]{1,0:T(8,128)S(1)}, u32[]{:S(2)}, u32[]{:S(2)}) collective-permute-start(f32[520,256]{1,0:T(8,128)S(1)} %get-tuple-element.58), channel_id=1, source_target_pairs={{1,2},{3,4},{5,6},{7,8},{9,10},{11,12},{13,14},{15,16},{17,18},{19... | collective-permute-start | bytes 1597448 | tf_op jit(solution)/shard_map/ppermute | solution.py:41
  18.7 2.1 %collective-permute-start.3 = (f32[512,256]{1,0:T(8,128)S(1)}, f32[512,256]{1,0:T(8,128)S(1)}, u32[]{:S(2)}, u32[]{:S(2)}) collective-permute-start(f32[512,256]{1,0:T(8,128)S(1)} %get-tuple-element.64.spread_in), channel_id=1, source_target_pairs={{0,1},{1,0},{2,3},{3,2},{4,5},{5,4},{6,7},{7,6},{8,9},{9,8},{10,11... | collective-permute-start | bytes 1572872 | tf_op jit(solution)/shard_map/ppermute | solution.py:36
  20.8 0.2 turn.1
  21.0 2.7 %forward_own.1 = (f32[512,128]{1,0:T(8,128)S(1)}, f32[512,512]{1,0:T(8,128)S(1)}, bf16[512,512]{1,0:T(8,128)(2,1)S(1)}, bf16[512,512]{1,0:T(8,128)(2,1)S(1)}) custom-call(bf16[512,512]{1,0:T(8,128)(2,1)S(1)} %get-tuple-element.54.high_band.refs_2_, bf16[512,512]{1,0:T(8,128)(2,1)S(1)} %get-tuple-element.55.low_band.refs_3_, ...), custom_call_target="tpu_custom_call" | custom-call | flops 1073741824 | bytes 2621440 | tf_op jit(solution)/shard_map/forward_own/pallas_call | solution.py:324
  23.7 0.0 collective-permute-done.3.spread_in
  23.7 2.7 %forward_mate.1 = (f32[512,128]{1,0:T(8,128)S(1)}, f32[512,512]{1,0:T(8,128)S(1)}, bf16[512,512]{1,0:T(8,128)(2,1)S(1)}, bf16[512,512]{1,0:T(8,128)(2,1)S(1)}, b...) custom-call(bf16[512,1024]{1,0:T(8,128)(2,1)S(1)} %get-tuple-element.52.halo_h.high_band.refs_0_, ...), custom_call_target="tpu_custom_call" | custom-call | tf_op jit(solution)/shard_map/forward_mate/pallas_call | solution.py:324
  26.4 0.9 collective-permute-done.2.refs_4_
  27.3 7.4 %from_beside.1 = (f32[512,128]{1,0:T(8,128)S(1)}, f32[512,512]{1,0:T(8,128)}, bf16[512,512]{1,0:T(8,128)(2,1)S(1)}, bf16[512,512]{1,0:T(8,128)(2,1)S(1)}, bf16[2...) custom-call(bf16[512,1024]{1,0:T(8,128)(2,1)S(1)} %get-tuple-element, ...), custom_call_target="tpu_custom_call" | custom-call | flops 3087007744 | bytes 10756096 | tf_op jit(solution)/shard_map/from_beside/pallas_call | solution.py:324
  34.7 1.9 %collective-permute-start.4 = (f32[1280,128]{1,0:T(8,128)S(1)}, f32[1280,128]{1,0:T(8,128)S(1)}, u32[]{:S(2)}, u32[]{:S(2)}) collective-permute-start(f32[1280,128]{1,0:T(8,128)S(1)} %get-tuple-element.94), channel_id=1, source_target_pairs={{0,1},{1,0},{2,3},{3,2},{4,5},{5,4},{6,7},{7,6},{8,9},{9,8},{10,11... | collective-permute-start | bytes 1966088 | tf_op jit(solution)/shard_map/ppermute | solution.py:36
  36.6 1.3 %backward_kept.1 = f32[768,128]{1,0:T(8,128)S(1)} custom-call(bf16[512,512]{1,0:T(8,128)(2,1)S(1)} %get-tuple-element.70.refs_14_.hid_oh, bf16[512,512]{1,0:T(8,128)(2,1)S(1)} %get-tuple-element.71.refs_15_.hid_ol, bf16[512,512]{1,0:T(8,128)(2,1)S(1)} %get-tuple-element.72.refs_16_.hid_ih, bf16[512,512]{1,0:T(8,128)(2,1)S(1)} %get-tuple-element.73.refs_17_.hid_il, ...), custom_call_target="tpu_custom_call" | custom-call | flops 671088640 | bytes 8654848 | tf_op jit(solution)/shard_map/backward_kept/pallas_call | solution.py:324
  37.9 0.7 collective-permute-done.4.got
  38.7 0.8 slice_add_fusion
  39.5 16.4 %all-to-all-start = ((f32[32,24,128]{2,1,0:T(8,128)}), f32[32,24,128]{2,1,0:T(8,128)S(1)}, u32[]{:S(2)}, u32[]{:S(2)}) async-start(f32[32,24,128]{2,1,0:T(8,128)} %bitcast.1), calls=%async_computation | async-start | bytes 786432 | tf_op jit(solution)/shard_map/all_to_all | solution.py:55
  55.9 3.7 %collective-permute-start.5 = (f32[128,512]{1,0:T(8,128)S(1)}, f32[128,512]{1,0:T(8,128)S(1)}, u32[]{:S(2)}, u32[]{:S(2)}) collective-permute-start(f32[128,512]{1,0:T(8,128)S(1)} %get-tuple-element.92.out_e), channel_id=1, source_target_pairs={{1,2},{3,4},{5,6},{7,8},{9,10},{11,12},{13,14},{15,16},{17,18},{19... | collective-permute-start | bytes 786440 | tf_op jit(solution)/shard_map/ppermute | solution.py:41
  59.7 0.7 put_logits.1
  60.4 6.0 %all-to-all-done.received = f32[32,24,128]{2,1,0:T(8,128)S(1)} async-done(((f32[32,24,128]{2,1,0:T(8,128)}), f32[32,24,128]{2,1,0:T(8,128)S(1)}, u32[]{:S(2)}, u32[]{:S(2)}) %all-to-all-start) | async-done | bytes 393248 | tf_op jit(solution)/shard_map/all_to_all | solution.py:55
  66.5 13.1 %all_to_all.15.received = f32[8,24,128]{2,1,0:T(8,128)S(1)} all-to-all(f32[8,24,128]{2,1,0:T(8,128)S(1)} %sum_repeated.3), channel_id=1, replica_groups={{0,16,32,48,64,80,96,112},{2,18,34,50,66,82,98,114},{4,20,36,52,68,84,1..., dimensions={0} | all-to-all | bytes 196608 | tf_op jit(solution)/shard_map/all_to_all | solution.py:55
  79.6 0.0 collective-permute-done.5.refs_0_.ret_e
  79.6 16.4 %all_to_all.16 = f32[32,24,128]{2,1,0:T(8,128)S(1)} all-to-all(f32[32,24,128]{2,1,0:T(8,128)S(1)} %sum_repeated.5), channel_id=1, replica_groups={{0,2,4,6,8,10,12,14,128,130,132,134,136,138,140,142,256,258,260,262,264..., dimensions={0} | all-to-all | bytes 786432 | tf_op jit(solution)/shard_map/all_to_all | solution.py:55
  96.1 5.8 %collective-permute-start.6 = (f32[768,128]{1,0:T(8,128)S(1)}, f32[768,128]{1,0:T(8,128)S(1)}, u32[]{:S(2)}, u32[]{:S(2)}) collective-permute-start(f32[768,128]{1,0:T(8,128)S(1)} %bitcast.4), channel_id=1, source_target_pairs={{0,1},{1,0},{2,3},{3,2},{4,5},{5,4},{6,7},{7,6},{8,9},{9,8},{10,11... | collective-permute-start | bytes 1179656 | tf_op jit(solution)/shard_map/ppermute | solution.py:36
  101.9 1.5 %finish_hidden.1 = f32[512,512]{1,0:T(8,128)} custom-call(f32[128,512]{1,0:T(8,128)S(1)} %get-tuple-element.90.ret_loc, f32[128,512]{1,0:T(8,128)S(1)} %collective-permute-done.5.refs_0_.ret_e, f32[1280,128]{1,0:T(8,128)S(1)} %collective-permute-done.4.got, bf16[512,256]{1,0:T(8,128)(2,1)S(1)} %get-tuple-element.62.refs_8_.wout_hh, ...), custom_call_target="tpu_custom_call" | custom-call | flops 268435456 | bytes 1703936 | tf_op jit(solution)/shard_map/finish_hidden/pallas_call | solution.py:324
  103.3 0.0 collective-permute-done.6.other
  103.3 1.0 assemble.1
  (3 shorter events, 0.1 us)
Async XLA Ops:
  0.6 14.0 %collective-permute-start = (f32[512,256]{1,0:T(8,128)}, f32[512,256]{1,0:T(8,128)S(1)}, u32[]{:S(2)}, u32[]{:S(2)}) collective-permute-start(f32[512,256]{1,0:T(8,128)} %features.1), channel_id=1, source_target_pairs={{1,2},{3,4},{5,6},{7,8},{9,10},{11,12},{13,14},{15,16},{17,18},{19... | collective-permute-start | bytes 1572872 | tf_op jit(solution)/shard_map/ppermute | solution.py:41
  9.8 6.4 %collective-permute-start.1 = (f32[512,256]{1,0:T(8,128)S(1)}, f32[512,256]{1,0:T(8,128)S(1)}, u32[]{:S(2)}, u32[]{:S(2)}) collective-permute-start(f32[512,256]{1,0:T(8,128)S(1)} %get-tuple-element.57), channel_id=1, source_target_pairs={{0,1},{1,0},{2,3},{3,2},{4,5},{5,4},{6,7},{7,6},{8,9},{9,8},{10,11... | collective-permute-start | bytes 1572872 | tf_op jit(solution)/shard_map/ppermute | solution.py:36
  16.8 10.6 %collective-permute-start.2 = (f32[520,256]{1,0:T(8,128)S(1)}, f32[520,256]{1,0:T(8,128)S(1)}, u32[]{:S(2)}, u32[]{:S(2)}) collective-permute-start(f32[520,256]{1,0:T(8,128)S(1)} %get-tuple-element.58), channel_id=1, source_target_pairs={{1,2},{3,4},{5,6},{7,8},{9,10},{11,12},{13,14},{15,16},{17,18},{19... | collective-permute-start | bytes 1597448 | tf_op jit(solution)/shard_map/ppermute | solution.py:41
  18.7 5.0 %collective-permute-start.3 = (f32[512,256]{1,0:T(8,128)S(1)}, f32[512,256]{1,0:T(8,128)S(1)}, u32[]{:S(2)}, u32[]{:S(2)}) collective-permute-start(f32[512,256]{1,0:T(8,128)S(1)} %get-tuple-element.64.spread_in), channel_id=1, source_target_pairs={{0,1},{1,0},{2,3},{3,2},{4,5},{5,4},{6,7},{7,6},{8,9},{9,8},{10,11... | collective-permute-start | bytes 1572872 | tf_op jit(solution)/shard_map/ppermute | solution.py:36
  34.7 4.0 %collective-permute-start.4 = (f32[1280,128]{1,0:T(8,128)S(1)}, f32[1280,128]{1,0:T(8,128)S(1)}, u32[]{:S(2)}, u32[]{:S(2)}) collective-permute-start(f32[1280,128]{1,0:T(8,128)S(1)} %get-tuple-element.94), channel_id=1, source_target_pairs={{0,1},{1,0},{2,3},{3,2},{4,5},{5,4},{6,7},{7,6},{8,9},{9,8},{10,11... | collective-permute-start | bytes 1966088 | tf_op jit(solution)/shard_map/ppermute | solution.py:36
  39.5 27.0 %all-to-all-start = ((f32[32,24,128]{2,1,0:T(8,128)}), f32[32,24,128]{2,1,0:T(8,128)S(1)}, u32[]{:S(2)}, u32[]{:S(2)}) async-start(f32[32,24,128]{2,1,0:T(8,128)} %bitcast.1), calls=%async_computation | async-start | bytes 786432 | tf_op jit(solution)/shard_map/all_to_all | solution.py:55
  55.9 23.6 %collective-permute-start.5 = (f32[128,512]{1,0:T(8,128)S(1)}, f32[128,512]{1,0:T(8,128)S(1)}, u32[]{:S(2)}, u32[]{:S(2)}) collective-permute-start(f32[128,512]{1,0:T(8,128)S(1)} %get-tuple-element.92.out_e), channel_id=1, source_target_pairs={{1,2},{3,4},{5,6},{7,8},{9,10},{11,12},{13,14},{15,16},{17,18},{19... | collective-permute-start | bytes 786440 | tf_op jit(solution)/shard_map/ppermute | solution.py:41
  96.1 7.3 %collective-permute-start.6 = (f32[768,128]{1,0:T(8,128)S(1)}, f32[768,128]{1,0:T(8,128)S(1)}, u32[]{:S(2)}, u32[]{:S(2)}) collective-permute-start(f32[768,128]{1,0:T(8,128)S(1)} %bitcast.4), channel_id=1, source_target_pairs={{0,1},{1,0},{2,3},{3,2},{4,5},{5,4},{6,7},{7,6},{8,9},{9,8},{10,11... | collective-permute-start | bytes 1179656 | tf_op jit(solution)/shard_map/ppermute | solution.py:36

commit v11 on v9

--- a/solution.py
+++ b/solution.py
@@ -211,7 +211,6 @@
     grad_out = jnp.where(last_element(grad_out) & (which == 1), loss[:1, :], grad_out)
     rows = deep * (grad_in.shape[1] // LANES)
     out[pl.ds(rows, hid), :] = grad_out
-    return rows + hid
 
 
 def last_element(value):
@@ -245,15 +244,12 @@
         pre_l[...] = low
         parts.append((returned_t, hidden, inputs, (high, low)))
     other = 1 - lax.rem(lax.axis_index(AXIS), 2)
-    end = gradient_half(other, parts, loss, give)
-    classes = near.shape[0]
-    for t in range(half // LANES):
-        give[pl.ds(end + t * classes, classes), :] = near[:, t * LANES : (t + 1) * LANES]
+    gradient_half(other, parts, loss, give)
 
 
 def backward_kept(hid_oh, hid_ol, hid_ih, hid_il, hid_eh, hid_el, in_oh, in_ol, in_ih, in_il, in_eh, in_el,
-                  pre_oh, pre_ol, pre_ih, pre_il, pre_eh, pre_el, ret_loc, out_i, out_e, loss, values,
-                  keep, logits):
+                  pre_oh, pre_ol, pre_ih, pre_il, pre_eh, pre_el, ret_loc, out_i, out_e, loss,
+                  keep):
     core = lax.rem(lax.axis_index(AXIS), 2)
     parts = (
         (ret_loc[...], (hid_oh, hid_ol), (in_oh, in_ol), (pre_oh[...], pre_ol[...])),
@@ -261,15 +257,16 @@
         (out_e[...], (hid_eh, hid_el), (in_eh, in_el), (pre_eh[...], pre_el[...])),
     )
     gradient_half(core, parts, loss, keep)
+
+
+def put_logits(values, logits, token):
     logits[...] = values[...]
-
-
-def finish_hidden(ret_loc, ret_e, got, wout_hh, wout_ll, hidden_grad):
-    classes, nodes = ret_loc.shape
-    start = got.shape[0] - classes * (nodes // LANES)
-    ret_i = [got[pl.ds(start + t * classes, classes), :] for t in range(nodes // LANES)]
-    returned_t = ret_loc[...] + ret_e[...] + jnp.concatenate(ret_i, axis=1)
-    both = jnp.concatenate(halves(returned_t.T), axis=1)
+    token[...] = values[:8, :]
+
+
+def finish_hidden(ret_loc, ret_e, ret_i, wout_hh, wout_ll, hidden_grad):
+    returned = (ret_loc[...] + ret_e[...] + ret_i[...]).T
+    both = jnp.concatenate(halves(returned), axis=1)
     across = ((1,), (1,))
     hidden_grad[...] = mm(both, wout_hh[...], across) + mm(both, wout_ll[...], across)
 
@@ -384,31 +381,33 @@
     in_ts = [in_oh, in_ol, *kept_i[2:], *kept_e[2:]]
     *pre, ret_loc, out_i, out_e, give = call(
         backward,
-        [wide_h] * 6 + [thin_t] * 3 + [((half + classes * (nodes // LANES), LANES), F32)],
+        [wide_h] * 6 + [thin_t] * 3 + [((half, LANES), F32)],
         [grads_t, halo_h, halo_l, loc_h, loc_l, slope_o, slope_i, slope_e, *hids,
          *in_ts, wout_hh, wout_ll, loss],
         flops=30 * nodes * nodes * deep,
     )
     got = mate(give)
-    keep, logits = call(
+    logits, token = call(put_logits, [thin, ((8, LANES), F32)], [values])
+    (keep,) = call(
         backward_kept,
-        [((half, LANES), F32), thin],
-        [*hids, *in_ts, *pre, ret_loc, out_i, out_e, loss, values],
+        [((half, LANES), F32)],
+        [*hids, *in_ts, *pre, ret_loc, out_i, out_e, loss],
         flops=10 * nodes * nodes * deep,
     )
     big, mid = groups((X, Y), (X, Z)), groups((Z,), (Y,))
     wide, narrow = len(big[0]), len(mid[0])
     shard = half // wide
-    received = exchange((keep + got[:half]).reshape(wide, shard, LANES), big)
+    received = exchange((keep + got).reshape(wide, shard, LANES), big)
     ret_e = beside(out_e)
-    (summed,) = call(sum_repeated, [((narrow, shard, LANES), F32)], [received])
+    ret_i = mate(out_i)
+    (summed,) = call(sum_repeated, [((narrow, shard, LANES), F32)], [received, token])
     received = exchange(summed, mid)
     (summed,) = call(sum_repeated, [((1, shard, LANES), F32)], [received])
-    (summed,) = call(sum_repeated, [((wide, shard, LANES), F32)], [summed, ret_e], anywhere=1)
+    (summed,) = call(sum_repeated, [((wide, shard, LANES), F32)], [summed, ret_e, ret_i], anywhere=2)
     own = exchange(summed, big).reshape(half, LANES)
     other = mate(own)
     (hidden_grad,) = call(
-        finish_hidden, [wide_f], [ret_loc, ret_e, got, wout_hh, wout_ll], flops=4 * nodes * nodes * deep
+        finish_hidden, [wide_f], [ret_loc, ret_e, ret_i, wout_hh, wout_ll], flops=4 * nodes * nodes * deep
     )
     grad_in, grad_out, mean_loss = call(
         functools.partial(assemble, nodes * lax.axis_size(AXIS)),

time: 104 us -> 103 us (level)
  waiting for transfers between devices: 8.67 us -> 6.28 us
  starting transfers between devices: 42 us -> 43.4 us
    all_to_all x1, waiting for transfers between devices: 6.74 us -> 4.1 us  [exchange(): lax.all_to_all(value, AXIS, 0, 0, axis_index_groups=members, tiled=True)]
    ppermute x4 -> x5, starting transfers between devices: 15.2 us -> 17.2 us  [mate(): lax.ppermute(value, AXIS, [(i, i ^ 1) for i in range(lax.axis_size(AXIS))])]
    pallas_call x15 -> x16, Pallas kernels: 22 us -> 22.1 us  [call(): pl.pallas_call(body, out_shape=[jax.ShapeDtypeStruct(shape, kind) for sha...]
  transfers between devices with their start and end apart: 8 -> 9, of which waited for: 4 -> 4; matrix products, arithmetic and copies ran while one was open for 0% -> 0% of each run, Pallas kernels for 14% -> 14%
where the time goes in v11:
time: 103 us; the launch traced here: 102 us
  starting transfers between devices  43.4 us (42%)
  blocking collectives  28.7 us (28%)
  Pallas kernels  22.1 us (21%)
  waiting for transfers between devices  6.28 us (6%)
    all_to_all x2, blocking collectives, exchange(): lax.all_to_all(value, AXIS, 0, 0, axis_index_groups=members, tiled=True)  28.7 us
    pallas_call x16, Pallas kernels, call(): pl.pallas_call(body, out_shape=[jax.ShapeDtypeStruct(shape, kind) for sha...  22.1 us
    ppermute x5, starting transfers between devices, mate(): lax.ppermute(value, AXIS, [(i, i ^ 1) for i in range(lax.axis_size(AXIS))])  17.2 us
    all_to_all x1, starting transfers between devices, exchange(): lax.all_to_all(value, AXIS, 0, 0, axis_index_groups=members, tiled=True)  16.4 us
    ppermute x3, starting transfers between devices, beside(): return lax.ppermute(value, AXIS, pairs + [(b, a) for a, b in pairs])  9.83 us
    all_to_all x1, waiting for transfers between devices, exchange(): lax.all_to_all(value, AXIS, 0, 0, axis_index_groups=members, tiled=True)  4.1 us
  transfers between devices with their start and end apart: 9, of which 4 were waited for; matrix products, arithmetic and copies ran while one was open for 0% of the time, Pallas kernels for 14%

profile of v11, /device:TPU:1, one launch (start us, length us, event | category | flops | bytes accessed | tf_op | source)
XLA Modules:
  0.0 102.3 jit_solution(7184826803060519843)
XLA Ops:
  0.6 4.6 %collective-permute-start = (f32[512,256]{1,0:T(8,128)}, f32[512,256]{1,0:T(8,128)S(1)}, u32[]{:S(2)}, u32[]{:S(2)}) collective-permute-start(f32[512,256]{1,0:T(8,128)} %features.1), channel_id=1, source_target_pairs={{1,2},{3,4},{5,6},{7,8},{9,10},{11,12},{13,14},{15,16},{17,18},{19... | collective-permute-start | bytes 1572872 | tf_op jit(solution)/shard_map/ppermute | solution.py:41
  5.2 4.6 %prepare.1 = (bf16[512,512]{1,0:T(8,128)(2,1)S(1)}, bf16[512,512]{1,0:T(8,128)(2,1)S(1)}, bf16[512,1024]{1,0:T(8,128)(2,1)S(1)}, bf16[512,1024]{1,0:T(8,128)(2,1...) custom-call(s32[2,6]{1,0:T(2,128)} %block_index.1, ...), custom_call_target="tpu_custom_call" | custom-call | flops 402653184 | bytes 4458552 | tf_op jit(solution)/shard_map/prepare/pallas_call | solution.py:306
  9.8 4.8 %collective-permute-start.1 = (f32[512,256]{1,0:T(8,128)S(1)}, f32[512,256]{1,0:T(8,128)S(1)}, u32[]{:S(2)}, u32[]{:S(2)}) collective-permute-start(f32[512,256]{1,0:T(8,128)S(1)} %get-tuple-element.57), channel_id=1, source_target_pairs={{0,1},{1,0},{2,3},{3,2},{4,5},{5,4},{6,7},{7,6},{8,9},{9,8},{10,11... | collective-permute-start | bytes 1572872 | tf_op jit(solution)/shard_map/ppermute | solution.py:36
  14.7 0.0 collective-permute-done.feat_e
  14.7 0.6 add_features.1.s_loc
  15.3 0.9 collective-permute-done.1.feat_i
  16.2 0.6 spread.1
  16.8 1.9 %collective-permute-start.2 = (f32[520,256]{1,0:T(8,128)S(1)}, f32[520,256]{1,0:T(8,128)S(1)}, u32[]{:S(2)}, u32[]{:S(2)}) collective-permute-start(f32[520,256]{1,0:T(8,128)S(1)} %get-tuple-element.58), channel_id=1, source_target_pairs={{1,2},{3,4},{5,6},{7,8},{9,10},{11,12},{13,14},{15,16},{17,18},{19... | collective-permute-start | bytes 1597448 | tf_op jit(solution)/shard_map/ppermute | solution.py:41
  18.7 2.1 %collective-permute-start.3 = (f32[512,256]{1,0:T(8,128)S(1)}, f32[512,256]{1,0:T(8,128)S(1)}, u32[]{:S(2)}, u32[]{:S(2)}) collective-permute-start(f32[512,256]{1,0:T(8,128)S(1)} %get-tuple-element.62.spread_in), channel_id=1, source_target_pairs={{0,1},{1,0},{2,3},{3,2},{4,5},{5,4},{6,7},{7,6},{8,9},{9,8},{10,11... | collective-permute-start | bytes 1572872 | tf_op jit(solution)/shard_map/ppermute | solution.py:36
  20.8 0.2 turn.1
  21.0 2.7 %forward_own.1 = (f32[512,128]{1,0:T(8,128)S(1)}, f32[512,512]{1,0:T(8,128)S(1)}, bf16[512,512]{1,0:T(8,128)(2,1)S(1)}, bf16[512,512]{1,0:T(8,128)(2,1)S(1)}) custom-call(bf16[512,512]{1,0:T(8,128)(2,1)S(1)} %get-tuple-element.63.high_band.loc_h, bf16[512,512]{1,0:T(8,128)(2,1)S(1)} %get-tuple-element.64.low_band.loc_l, ...), custom_call_target="tpu_custom_call" | custom-call | flops 1073741824 | bytes 2621440 | tf_op jit(solution)/shard_map/forward_own/pallas_call | solution.py:306
  23.7 0.0 collective-permute-done.3.spread_in
  23.8 2.7 %forward_mate.1 = (f32[512,128]{1,0:T(8,128)S(1)}, f32[512,512]{1,0:T(8,128)S(1)}, bf16[512,512]{1,0:T(8,128)(2,1)S(1)}, bf16[512,512]{1,0:T(8,128)(2,1)S(1)}, b...) custom-call(bf16[512,1024]{1,0:T(8,128)(2,1)S(1)} %get-tuple-element.54.halo_h.high_band, ...), custom_call_target="tpu_custom_call" | custom-call | tf_op jit(solution)/shard_map/forward_mate/pallas_call | solution.py:306
  26.5 0.9 collective-permute-done.2.spread_in
  27.4 2.7 %forward_beside.1 = (f32[512,128]{1,0:T(8,128)S(1)}, f32[512,512]{1,0:T(8,128)S(1)}, bf16[512,512]{1,0:T(8,128)(2,1)S(1)}, bf16[512,512]{1,0:T(8,128)(2,1)S(1)},...) custom-call(bf16[512,1024]{1,0:T(8,128)(2,1)S(1)} %get-tuple-element.54.halo_h.high_band, ...), custom_call_target="tpu_custom_call" | custom-call | flops 1073741824 | bytes 3678208 | tf_op jit(solution)/shard_map/forward_beside/pallas_call | solution.py:306
  30.1 0.3 classify.1
  30.4 3.2 %backward.1 = (bf16[512,512]{1,0:T(8,128)(2,1)S(1)}, bf16[512,512]{1,0:T(8,128)(2,1)S(1)}, bf16[512,512]{1,0:T(8,128)(2,1)S(1)}, bf16[512,512]{1,0:T(8,128)(2,1)...) custom-call(bf16[256,512]{1,0:T(8,128)(2,1)S(1)} %get-tuple-element., ...), custom_call_target="tpu_custom_call" | custom-call | flops 2013265920 | bytes 11800576 | tf_op jit(solution)/shard_map/backward/pallas_call | solution.py:306
  33.6 1.9 %collective-permute-start.4 = (f32[768,128]{1,0:T(8,128)S(1)}, f32[768,128]{1,0:T(8,128)S(1)}, u32[]{:S(2)}, u32[]{:S(2)}) collective-permute-start(f32[768,128]{1,0:T(8,128)S(1)} %get-tuple-element.98), channel_id=1, source_target_pairs={{0,1},{1,0},{2,3},{3,2},{4,5},{5,4},{6,7},{7,6},{8,9},{9,8},{10,11... | collective-permute-start | bytes 1179656 | tf_op jit(solution)/shard_map/ppermute | solution.py:36
  35.5 1.3 %backward_kept.1 = f32[768,128]{1,0:T(8,128)S(1)} custom-call(bf16[512,512]{1,0:T(8,128)(2,1)S(1)} %get-tuple-element.70.hid_oh, bf16[512,512]{1,0:T(8,128)(2,1)S(1)} %get-tuple-element.71.hid_ol, bf16[512,512]{1,0:T(8,128)(2,1)S(1)} %get-tuple-element.72.hid_ih, bf16[512,512]{1,0:T(8,128)(2,1)S(1)} %get-tuple-element.73.hid_il, ...), custom_call_target="tpu_custom_call" | custom-call | flops 671088640 | bytes 8654848 | tf_op jit(solution)/shard_map/backward_kept/pallas_call | solution.py:306
  36.9 0.4 collective-permute-done.4
  37.2 0.8 add.3
  38.0 16.4 %all-to-all-start = ((f32[32,24,128]{2,1,0:T(8,128)}), f32[32,24,128]{2,1,0:T(8,128)S(1)}, u32[]{:S(2)}, u32[]{:S(2)}) async-start(f32[32,24,128]{2,1,0:T(8,128)} %bitcast.1), calls=%async_computation | async-start | bytes 786432 | tf_op jit(solution)/shard_map/all_to_all | solution.py:55
  54.4 2.3 %collective-permute-start.6 = (f32[128,512]{1,0:T(8,128)S(1)}, f32[128,512]{1,0:T(8,128)S(1)}, u32[]{:S(2)}, u32[]{:S(2)}) collective-permute-start(f32[128,512]{1,0:T(8,128)S(1)} %get-tuple-element.96.out_i), channel_id=1, source_target_pairs={{0,1},{1,0},{2,3},{3,2},{4,5},{5,4},{6,7},{7,6},{8,9},{9,8},{10,11... | collective-permute-start | bytes 786440 | tf_op jit(solution)/shard_map/ppermute | solution.py:36
  56.8 3.3 %collective-permute-start.5 = (f32[128,512]{1,0:T(8,128)S(1)}, f32[128,512]{1,0:T(8,128)S(1)}, u32[]{:S(2)}, u32[]{:S(2)}) collective-permute-start(f32[128,512]{1,0:T(8,128)S(1)} %get-tuple-element.97.out_e), channel_id=1, source_target_pairs={{1,2},{3,4},{5,6},{7,8},{9,10},{11,12},{13,14},{15,16},{17,18},{19... | collective-permute-start | bytes 786440 | tf_op jit(solution)/shard_map/ppermute | solution.py:41
  60.1 0.7 put_logits.1
  60.8 4.1 %all-to-all-done.received = f32[32,24,128]{2,1,0:T(8,128)S(1)} async-done(((f32[32,24,128]{2,1,0:T(8,128)}), f32[32,24,128]{2,1,0:T(8,128)S(1)}, u32[]{:S(2)}, u32[]{:S(2)}) %all-to-all-start) | async-done | bytes 393248 | tf_op jit(solution)/shard_map/all_to_all | solution.py:55
  65.0 13.1 %all_to_all.15.received = f32[8,24,128]{2,1,0:T(8,128)S(1)} all-to-all(f32[8,24,128]{2,1,0:T(8,128)S(1)} %sum_repeated.3), channel_id=1, replica_groups={{0,16,32,48,64,80,96,112},{2,18,34,50,66,82,98,114},{4,20,36,52,68,84,1..., dimensions={0} | all-to-all | bytes 196608 | tf_op jit(solution)/shard_map/all_to_all | solution.py:55
  78.1 0.0 collective-permute-done.6.refs_1_.ret_i
  78.1 0.0 collective-permute-done.5.refs_0_.ret_e
  78.1 15.6 %all_to_all.16 = f32[32,24,128]{2,1,0:T(8,128)S(1)} all-to-all(f32[32,24,128]{2,1,0:T(8,128)S(1)} %sum_repeated.5), channel_id=1, replica_groups={{0,2,4,6,8,10,12,14,128,130,132,134,136,138,140,142,256,258,260,262,264..., dimensions={0} | all-to-all | bytes 786432 | tf_op jit(solution)/shard_map/all_to_all | solution.py:55
  93.8 5.9 %collective-permute-start.7 = (f32[768,128]{1,0:T(8,128)S(1)}, f32[768,128]{1,0:T(8,128)S(1)}, u32[]{:S(2)}, u32[]{:S(2)}) collective-permute-start(f32[768,128]{1,0:T(8,128)S(1)} %bitcast.4), channel_id=1, source_target_pairs={{0,1},{1,0},{2,3},{3,2},{4,5},{5,4},{6,7},{7,6},{8,9},{9,8},{10,11... | collective-permute-start | bytes 1179656 | tf_op jit(solution)/shard_map/ppermute | solution.py:36
  99.7 1.5 %finish_hidden.1 = f32[512,512]{1,0:T(8,128)} custom-call(f32[128,512]{1,0:T(8,128)S(1)} %get-tuple-element.95.ret_loc, f32[128,512]{1,0:T(8,128)S(1)} %collective-permute-done.5.refs_0_.ret_e, f32[128,512]{1,0:T(8,128)S(1)} %collective-permute-done.6.refs_1_.ret_i, bf16[512,256]{1,0:T(8,128)(2,1)S(1)} %get-tuple-element.86.wout_hh, ...), custom_call_target="tpu_custom_call" | custom-call | flops 268435456 | bytes 1310720 | tf_op jit(solution)/shard_map/finish_hidden/pallas_call | solution.py:306
  101.2 0.0 collective-permute-done.7.other
  101.2 1.0 assemble.1
  (3 shorter events, 0.1 us)
Async XLA Ops:
  0.6 14.0 %collective-permute-start = (f32[512,256]{1,0:T(8,128)}, f32[512,256]{1,0:T(8,128)S(1)}, u32[]{:S(2)}, u32[]{:S(2)}) collective-permute-start(f32[512,256]{1,0:T(8,128)} %features.1), channel_id=1, source_target_pairs={{1,2},{3,4},{5,6},{7,8},{9,10},{11,12},{13,14},{15,16},{17,18},{19... | collective-permute-start | bytes 1572872 | tf_op jit(solution)/shard_map/ppermute | solution.py:41
  9.8 6.4 %collective-permute-start.1 = (f32[512,256]{1,0:T(8,128)S(1)}, f32[512,256]{1,0:T(8,128)S(1)}, u32[]{:S(2)}, u32[]{:S(2)}) collective-permute-start(f32[512,256]{1,0:T(8,128)S(1)} %get-tuple-element.57), channel_id=1, source_target_pairs={{0,1},{1,0},{2,3},{3,2},{4,5},{5,4},{6,7},{7,6},{8,9},{9,8},{10,11... | collective-permute-start | bytes 1572872 | tf_op jit(solution)/shard_map/ppermute | solution.py:36
  16.8 10.6 %collective-permute-start.2 = (f32[520,256]{1,0:T(8,128)S(1)}, f32[520,256]{1,0:T(8,128)S(1)}, u32[]{:S(2)}, u32[]{:S(2)}) collective-permute-start(f32[520,256]{1,0:T(8,128)S(1)} %get-tuple-element.58), channel_id=1, source_target_pairs={{1,2},{3,4},{5,6},{7,8},{9,10},{11,12},{13,14},{15,16},{17,18},{19... | collective-permute-start | bytes 1597448 | tf_op jit(solution)/shard_map/ppermute | solution.py:41
  18.7 5.0 %collective-permute-start.3 = (f32[512,256]{1,0:T(8,128)S(1)}, f32[512,256]{1,0:T(8,128)S(1)}, u32[]{:S(2)}, u32[]{:S(2)}) collective-permute-start(f32[512,256]{1,0:T(8,128)S(1)} %get-tuple-element.62.spread_in), channel_id=1, source_target_pairs={{0,1},{1,0},{2,3},{3,2},{4,5},{5,4},{6,7},{7,6},{8,9},{9,8},{10,11... | collective-permute-start | bytes 1572872 | tf_op jit(solution)/shard_map/ppermute | solution.py:36
  33.6 3.6 %collective-permute-start.4 = (f32[768,128]{1,0:T(8,128)S(1)}, f32[768,128]{1,0:T(8,128)S(1)}, u32[]{:S(2)}, u32[]{:S(2)}) collective-permute-start(f32[768,128]{1,0:T(8,128)S(1)} %get-tuple-element.98), channel_id=1, source_target_pairs={{0,1},{1,0},{2,3},{3,2},{4,5},{5,4},{6,7},{7,6},{8,9},{9,8},{10,11... | collective-permute-start | bytes 1179656 | tf_op jit(solution)/shard_map/ppermute | solution.py:36
  38.0 26.9 %all-to-all-start = ((f32[32,24,128]{2,1,0:T(8,128)}), f32[32,24,128]{2,1,0:T(8,128)S(1)}, u32[]{:S(2)}, u32[]{:S(2)}) async-start(f32[32,24,128]{2,1,0:T(8,128)} %bitcast.1), calls=%async_computation | async-start | bytes 786432 | tf_op jit(solution)/shard_map/all_to_all | solution.py:55
  54.4 23.7 %collective-permute-start.6 = (f32[128,512]{1,0:T(8,128)S(1)}, f32[128,512]{1,0:T(8,128)S(1)}, u32[]{:S(2)}, u32[]{:S(2)}) collective-permute-start(f32[128,512]{1,0:T(8,128)S(1)} %get-tuple-element.96.out_i), channel_id=1, source_target_pairs={{0,1},{1,0},{2,3},{3,2},{4,5},{5,4},{6,7},{7,6},{8,9},{9,8},{10,11... | collective-permute-start | bytes 786440 | tf_op jit(solution)/shard_map/ppermute | solution.py:36
  56.8 21.3 %collective-permute-start.5 = (f32[128,512]{1,0:T(8,128)S(1)}, f32[128,512]{1,0:T(8,128)S(1)}, u32[]{:S(2)}, u32[]{:S(2)}) collective-permute-start(f32[128,512]{1,0:T(8,128)S(1)} %get-tuple-element.97.out_e), channel_id=1, source_target_pairs={{1,2},{3,4},{5,6},{7,8},{9,10},{11,12},{13,14},{15,16},{17,18},{19... | collective-permute-start | bytes 786440 | tf_op jit(solution)/shard_map/ppermute | solution.py:41
  93.8 7.4 %collective-permute-start.7 = (f32[768,128]{1,0:T(8,128)S(1)}, f32[768,128]{1,0:T(8,128)S(1)}, u32[]{:S(2)}, u32[]{:S(2)}) collective-permute-start(f32[768,128]{1,0:T(8,128)S(1)} %bitcast.4), channel_id=1, source_target_pairs={{0,1},{1,0},{2,3},{3,2},{4,5},{5,4},{6,7},{7,6},{8,9},{9,8},{10,11... | collective-permute-start | bytes 1179656 | tf_op jit(solution)/shard_map/ppermute | solution.py:36

commit v12 on v11

--- a/solution.py
+++ b/solution.py
@@ -185,13 +185,13 @@
     return tall[:half] + tall[half:]
 
 
-def classify(values, onehot, grads_t, loss):
+def classify(values, onehot, loss):
     scores = values[...]
     totals = jnp.log(jnp.sum(jnp.exp(scores), axis=1, keepdims=True))
     hot = onehot[...]
-    grads_t[...] = jnp.concatenate(halves((jnp.exp(scores - totals) - hot).T), axis=0)
     row_loss = totals - jnp.sum(hot * scores, axis=1, keepdims=True)
     loss[...] = jnp.broadcast_to(jnp.sum(row_loss, axis=0, keepdims=True), loss.shape)
+    return jnp.concatenate(halves((jnp.exp(scores - totals) - hot).T), axis=0)
 
 
 def gradient_half(which, parts, loss, out):
@@ -219,10 +219,10 @@
     return (row == value.shape[0] - 1) & (column == value.shape[1] - 1)
 
 
-def backward(grads_t, halo_h, halo_l, loc_h, loc_l, slope_o, slope_i, slope_e, hid_oh, hid_ol, hid_ih, hid_il, hid_eh, hid_el,
-             in_oh, in_ol, in_ih, in_il, in_eh, in_el, wout_hh, wout_ll, loss,
-             pre_oh, pre_ol, pre_ih, pre_il, pre_eh, pre_el, ret_loc, out_i, out_e, give):
-    grads = grads_t[...]
+def backward(values, onehot, halo_h, halo_l, loc_h, loc_l, slope_o, slope_i, slope_e, hid_oh, hid_ol, hid_ih, hid_il, hid_eh, hid_el,
+             in_oh, in_ol, in_ih, in_il, in_eh, in_el, wout_hh, wout_ll,
+             loss, pre_oh, pre_ol, pre_ih, pre_il, pre_eh, pre_el, ret_loc, out_i, out_e, give):
+    grads = classify(values, onehot, loss)
     half = loc_h.shape[1]
     own = stacked(grads, loc_h[...], loc_l[...])
     near = stacked(grads, halo_h[:, :half], halo_l[:, :half])
@@ -375,15 +375,14 @@
     logits_o, slope_o, *kept_o = layer_of(loc_h, loc_l, spread_in, onehot, "forward_own", 0)
     logits_i, slope_i, *kept_i = layer_of(halo_h, halo_l, spread_i, logits_o, "forward_mate", 0)
     values, slope_e, *kept_e = layer_of(halo_h, halo_l, spread_e, logits_i, "forward_beside", 1)
-    grads_t, loss = call(classify, [((2 * classes, nodes), BF16), ((8, LANES), F32)], [values, onehot])
     half = (deep * hid + hid * classes) // LANES // 2
     hids = [*kept_o[:2], *kept_i[:2], *kept_e[:2]]
     in_ts = [in_oh, in_ol, *kept_i[2:], *kept_e[2:]]
-    *pre, ret_loc, out_i, out_e, give = call(
+    loss, *pre, ret_loc, out_i, out_e, give = call(
         backward,
-        [wide_h] * 6 + [thin_t] * 3 + [((half, LANES), F32)],
-        [grads_t, halo_h, halo_l, loc_h, loc_l, slope_o, slope_i, slope_e, *hids,
-         *in_ts, wout_hh, wout_ll, loss],
+        [((8, LANES), F32)] + [wide_h] * 6 + [thin_t] * 3 + [((half, LANES), F32)],
+        [values, onehot, halo_h, halo_l, loc_h, loc_l, slope_o, slope_i, slope_e, *hids,
+         *in_ts, wout_hh, wout_ll],
         flops=30 * nodes * nodes * deep,
     )
     got = mate(give)

time: 103 us -> 103 us (level)
    pallas_call x16 -> x15, Pallas kernels: 22.1 us -> 21.8 us  [call(): pl.pallas_call(body, out_shape=[jax.ShapeDtypeStruct(shape, kind) for sha...]
where the time goes in v12:
time: 103 us; the launch traced here: 102 us
  starting transfers between devices  43.5 us (42%)
  blocking collectives  28.7 us (28%)
  Pallas kernels  21.8 us (21%)
  waiting for transfers between devices  6.29 us (6%)
    all_to_all x2, blocking collectives, exchange(): lax.all_to_all(value, AXIS, 0, 0, axis_index_groups=members, tiled=True)  28.7 us
    pallas_call x15, Pallas kernels, call(): pl.pallas_call(body, out_shape=[jax.ShapeDtypeStruct(shape, kind) for sha...  21.8 us
    ppermute x5, starting transfers between devices, mate(): lax.ppermute(value, AXIS, [(i, i ^ 1) for i in range(lax.axis_size(AXIS))])  17.3 us
    all_to_all x1, starting transfers between devices, exchange(): lax.all_to_all(value, AXIS, 0, 0, axis_index_groups=members, tiled=True)  16.3 us
    ppermute x3, starting transfers between devices, beside(): return lax.ppermute(value, AXIS, pairs + [(b, a) for a, b in pairs])  9.83 us
    all_to_all x1, waiting for transfers between devices, exchange(): lax.all_to_all(value, AXIS, 0, 0, axis_index_groups=members, tiled=True)  4.1 us
  transfers between devices with their start and end apart: 9, of which 4 were waited for; matrix products, arithmetic and copies ran while one was open for 0% of the time, Pallas kernels for 14%

profile of v12, /device:TPU:1, one launch (start us, length us, event | category | flops | bytes accessed | tf_op | source)
XLA Modules:
  0.0 102.1 jit_solution(16519819459997898453)
XLA Ops:
  0.6 4.6 %collective-permute-start = (f32[512,256]{1,0:T(8,128)}, f32[512,256]{1,0:T(8,128)S(1)}, u32[]{:S(2)}, u32[]{:S(2)}) collective-permute-start(f32[512,256]{1,0:T(8,128)} %features.1), channel_id=1, source_target_pairs={{1,2},{3,4},{5,6},{7,8},{9,10},{11,12},{13,14},{15,16},{17,18},{19... | collective-permute-start | bytes 1572872 | tf_op jit(solution)/shard_map/ppermute | solution.py:41
  5.2 4.5 %prepare.1 = (bf16[512,512]{1,0:T(8,128)(2,1)S(1)}, bf16[512,512]{1,0:T(8,128)(2,1)S(1)}, bf16[512,1024]{1,0:T(8,128)(2,1)S(1)}, bf16[512,1024]{1,0:T(8,128)(2,1...) custom-call(s32[2,6]{1,0:T(2,128)} %block_index.1, ...), custom_call_target="tpu_custom_call" | custom-call | flops 402653184 | bytes 4458552 | tf_op jit(solution)/shard_map/prepare/pallas_call | solution.py:306
  9.7 5.0 %collective-permute-start.1 = (f32[512,256]{1,0:T(8,128)S(1)}, f32[512,256]{1,0:T(8,128)S(1)}, u32[]{:S(2)}, u32[]{:S(2)}) collective-permute-start(f32[512,256]{1,0:T(8,128)S(1)} %get-tuple-element.56), channel_id=1, source_target_pairs={{0,1},{1,0},{2,3},{3,2},{4,5},{5,4},{6,7},{7,6},{8,9},{9,8},{10,11... | collective-permute-start | bytes 1572872 | tf_op jit(solution)/shard_map/ppermute | solution.py:36
  14.7 0.0 collective-permute-done.feat_e
  14.7 0.6 add_features.1.s_loc
  15.3 0.9 collective-permute-done.1.feat_i
  16.2 0.6 spread.1
  16.8 1.9 %collective-permute-start.2 = (f32[520,256]{1,0:T(8,128)S(1)}, f32[520,256]{1,0:T(8,128)S(1)}, u32[]{:S(2)}, u32[]{:S(2)}) collective-permute-start(f32[520,256]{1,0:T(8,128)S(1)} %get-tuple-element.57), channel_id=1, source_target_pairs={{1,2},{3,4},{5,6},{7,8},{9,10},{11,12},{13,14},{15,16},{17,18},{19... | collective-permute-start | bytes 1597448 | tf_op jit(solution)/shard_map/ppermute | solution.py:41
  18.8 2.1 %collective-permute-start.3 = (f32[512,256]{1,0:T(8,128)S(1)}, f32[512,256]{1,0:T(8,128)S(1)}, u32[]{:S(2)}, u32[]{:S(2)}) collective-permute-start(f32[512,256]{1,0:T(8,128)S(1)} %get-tuple-element.61.spread_in), channel_id=1, source_target_pairs={{0,1},{1,0},{2,3},{3,2},{4,5},{5,4},{6,7},{7,6},{8,9},{9,8},{10,11... | collective-permute-start | bytes 1572872 | tf_op jit(solution)/shard_map/ppermute | solution.py:36
  20.9 0.2 turn.1
  21.1 2.7 %forward_own.1 = (f32[512,128]{1,0:T(8,128)S(1)}, f32[512,512]{1,0:T(8,128)S(1)}, bf16[512,512]{1,0:T(8,128)(2,1)S(1)}, bf16[512,512]{1,0:T(8,128)(2,1)S(1)}) custom-call(bf16[512,512]{1,0:T(8,128)(2,1)S(1)} %get-tuple-element.62.high_band.loc_h, bf16[512,512]{1,0:T(8,128)(2,1)S(1)} %get-tuple-element.63.low_band.loc_l, ...), custom_call_target="tpu_custom_call" | custom-call | flops 1073741824 | bytes 2621440 | tf_op jit(solution)/shard_map/forward_own/pallas_call | solution.py:306
  23.8 0.0 collective-permute-done.3.spread_in
  23.8 2.7 %forward_mate.1 = (f32[512,128]{1,0:T(8,128)S(1)}, f32[512,512]{1,0:T(8,128)S(1)}, bf16[512,512]{1,0:T(8,128)(2,1)S(1)}, bf16[512,512]{1,0:T(8,128)(2,1)S(1)}, b...) custom-call(bf16[512,1024]{1,0:T(8,128)(2,1)S(1)} %get-tuple-element.53.halo_h.high_band, ...), custom_call_target="tpu_custom_call" | custom-call | tf_op jit(solution)/shard_map/forward_mate/pallas_call | solution.py:306
  26.5 0.9 collective-permute-done.2.spread_in
  27.4 2.7 %forward_beside.1 = (f32[512,128]{1,0:T(8,128)S(1)}, f32[512,512]{1,0:T(8,128)S(1)}, bf16[512,512]{1,0:T(8,128)(2,1)S(1)}, bf16[512,512]{1,0:T(8,128)(2,1)S(1)},...) custom-call(bf16[512,1024]{1,0:T(8,128)(2,1)S(1)} %get-tuple-element.53.halo_h.high_band, ...), custom_call_target="tpu_custom_call" | custom-call | flops 1073741824 | bytes 3678208 | tf_op jit(solution)/shard_map/forward_beside/pallas_call | solution.py:306
  30.1 3.3 %backward.1 = (f32[8,128]{1,0:T(8,128)S(1)}, bf16[512,512]{1,0:T(8,128)(2,1)S(1)}, bf16[512,512]{1,0:T(8,128)(2,1)S(1)}, bf16[512,512]{1,0:T(8,128)(2,1)S(1)}, b...) custom-call(f32[512,128]{1,0:T(8,128)S(1)} %get-tuple-element.67.val, ...), custom_call_target="tpu_custom_call" | custom-call | flops 2013265920 | bytes 12058624 | tf_op jit(solution)/shard_map/backward/pallas_call | solution.py:306
  33.5 1.9 %collective-permute-start.4 = (f32[768,128]{1,0:T(8,128)S(1)}, f32[768,128]{1,0:T(8,128)S(1)}, u32[]{:S(2)}, u32[]{:S(2)}) collective-permute-start(f32[768,128]{1,0:T(8,128)S(1)} %get-tuple-element.96), channel_id=1, source_target_pairs={{0,1},{1,0},{2,3},{3,2},{4,5},{5,4},{6,7},{7,6},{8,9},{9,8},{10,11... | collective-permute-start | bytes 1179656 | tf_op jit(solution)/shard_map/ppermute | solution.py:36
  35.4 1.3 %backward_kept.1 = f32[768,128]{1,0:T(8,128)S(1)} custom-call(bf16[512,512]{1,0:T(8,128)(2,1)S(1)} %get-tuple-element.69.hid_oh, bf16[512,512]{1,0:T(8,128)(2,1)S(1)} %get-tuple-element.70.hid_ol, bf16[512,512]{1,0:T(8,128)(2,1)S(1)} %get-tuple-element.71.hid_ih, bf16[512,512]{1,0:T(8,128)(2,1)S(1)} %get-tuple-element.72.hid_il, ...), custom_call_target="tpu_custom_call" | custom-call | flops 671088640 | bytes 8654848 | tf_op jit(solution)/shard_map/backward_kept/pallas_call | solution.py:306
  36.7 0.4 collective-permute-done.4
  37.1 0.8 add.3
  37.9 16.3 %all-to-all-start = ((f32[32,24,128]{2,1,0:T(8,128)}), f32[32,24,128]{2,1,0:T(8,128)S(1)}, u32[]{:S(2)}, u32[]{:S(2)}) async-start(f32[32,24,128]{2,1,0:T(8,128)} %bitcast.1), calls=%async_computation | async-start | bytes 786432 | tf_op jit(solution)/shard_map/all_to_all | solution.py:55
  54.2 2.3 %collective-permute-start.6 = (f32[128,512]{1,0:T(8,128)S(1)}, f32[128,512]{1,0:T(8,128)S(1)}, u32[]{:S(2)}, u32[]{:S(2)}) collective-permute-start(f32[128,512]{1,0:T(8,128)S(1)} %get-tuple-element.93.out_i), channel_id=1, source_target_pairs={{0,1},{1,0},{2,3},{3,2},{4,5},{5,4},{6,7},{7,6},{8,9},{9,8},{10,11... | collective-permute-start | bytes 786440 | tf_op jit(solution)/shard_map/ppermute | solution.py:36
  56.6 3.3 %collective-permute-start.5 = (f32[128,512]{1,0:T(8,128)S(1)}, f32[128,512]{1,0:T(8,128)S(1)}, u32[]{:S(2)}, u32[]{:S(2)}) collective-permute-start(f32[128,512]{1,0:T(8,128)S(1)} %get-tuple-element.94.out_e), channel_id=1, source_target_pairs={{1,2},{3,4},{5,6},{7,8},{9,10},{11,12},{13,14},{15,16},{17,18},{19... | collective-permute-start | bytes 786440 | tf_op jit(solution)/shard_map/ppermute | solution.py:41
  59.9 0.7 put_logits.1
  60.6 4.1 %all-to-all-done.received = f32[32,24,128]{2,1,0:T(8,128)S(1)} async-done(((f32[32,24,128]{2,1,0:T(8,128)}), f32[32,24,128]{2,1,0:T(8,128)S(1)}, u32[]{:S(2)}, u32[]{:S(2)}) %all-to-all-start) | async-done | bytes 393248 | tf_op jit(solution)/shard_map/all_to_all | solution.py:55
  64.8 13.1 %all_to_all.15.received = f32[8,24,128]{2,1,0:T(8,128)S(1)} all-to-all(f32[8,24,128]{2,1,0:T(8,128)S(1)} %sum_repeated.3), channel_id=1, replica_groups={{0,16,32,48,64,80,96,112},{2,18,34,50,66,82,98,114},{4,20,36,52,68,84,1..., dimensions={0} | all-to-all | bytes 196608 | tf_op jit(solution)/shard_map/all_to_all | solution.py:55
  77.9 0.0 collective-permute-done.6.refs_1_.ret_i
  77.9 0.0 collective-permute-done.5.refs_0_.ret_e
  77.9 15.6 %all_to_all.16 = f32[32,24,128]{2,1,0:T(8,128)S(1)} all-to-all(f32[32,24,128]{2,1,0:T(8,128)S(1)} %sum_repeated.5), channel_id=1, replica_groups={{0,2,4,6,8,10,12,14,128,130,132,134,136,138,140,142,256,258,260,262,264..., dimensions={0} | all-to-all | bytes 786432 | tf_op jit(solution)/shard_map/all_to_all | solution.py:55
  93.5 5.9 %collective-permute-start.7 = (f32[768,128]{1,0:T(8,128)S(1)}, f32[768,128]{1,0:T(8,128)S(1)}, u32[]{:S(2)}, u32[]{:S(2)}) collective-permute-start(f32[768,128]{1,0:T(8,128)S(1)} %bitcast.4), channel_id=1, source_target_pairs={{0,1},{1,0},{2,3},{3,2},{4,5},{5,4},{6,7},{7,6},{8,9},{9,8},{10,11... | collective-permute-start | bytes 1179656 | tf_op jit(solution)/shard_map/ppermute | solution.py:36
  99.5 1.5 %finish_hidden.1 = f32[512,512]{1,0:T(8,128)} custom-call(f32[128,512]{1,0:T(8,128)S(1)} %get-tuple-element.92.ret_loc, f32[128,512]{1,0:T(8,128)S(1)} %collective-permute-done.5.refs_0_.ret_e, f32[128,512]{1,0:T(8,128)S(1)} %collective-permute-done.6.refs_1_.ret_i, bf16[512,256]{1,0:T(8,128)(2,1)S(1)} %get-tuple-element.84.wout_hh, ...), custom_call_target="tpu_custom_call" | custom-call | flops 268435456 | bytes 1310720 | tf_op jit(solution)/shard_map/finish_hidden/pallas_call | solution.py:306
  101.0 0.0 collective-permute-done.7.other
  101.0 1.0 assemble.1
  (3 shorter events, 0.1 us)
Async XLA Ops:
  0.6 14.1 %collective-permute-start = (f32[512,256]{1,0:T(8,128)}, f32[512,256]{1,0:T(8,128)S(1)}, u32[]{:S(2)}, u32[]{:S(2)}) collective-permute-start(f32[512,256]{1,0:T(8,128)} %features.1), channel_id=1, source_target_pairs={{1,2},{3,4},{5,6},{7,8},{9,10},{11,12},{13,14},{15,16},{17,18},{19... | collective-permute-start | bytes 1572872 | tf_op jit(solution)/shard_map/ppermute | solution.py:41
  9.7 6.5 %collective-permute-start.1 = (f32[512,256]{1,0:T(8,128)S(1)}, f32[512,256]{1,0:T(8,128)S(1)}, u32[]{:S(2)}, u32[]{:S(2)}) collective-permute-start(f32[512,256]{1,0:T(8,128)S(1)} %get-tuple-element.56), channel_id=1, source_target_pairs={{0,1},{1,0},{2,3},{3,2},{4,5},{5,4},{6,7},{7,6},{8,9},{9,8},{10,11... | collective-permute-start | bytes 1572872 | tf_op jit(solution)/shard_map/ppermute | solution.py:36
  16.8 10.6 %collective-permute-start.2 = (f32[520,256]{1,0:T(8,128)S(1)}, f32[520,256]{1,0:T(8,128)S(1)}, u32[]{:S(2)}, u32[]{:S(2)}) collective-permute-start(f32[520,256]{1,0:T(8,128)S(1)} %get-tuple-element.57), channel_id=1, source_target_pairs={{1,2},{3,4},{5,6},{7,8},{9,10},{11,12},{13,14},{15,16},{17,18},{19... | collective-permute-start | bytes 1597448 | tf_op jit(solution)/shard_map/ppermute | solution.py:41
  18.8 5.0 %collective-permute-start.3 = (f32[512,256]{1,0:T(8,128)S(1)}, f32[512,256]{1,0:T(8,128)S(1)}, u32[]{:S(2)}, u32[]{:S(2)}) collective-permute-start(f32[512,256]{1,0:T(8,128)S(1)} %get-tuple-element.61.spread_in), channel_id=1, source_target_pairs={{0,1},{1,0},{2,3},{3,2},{4,5},{5,4},{6,7},{7,6},{8,9},{9,8},{10,11... | collective-permute-start | bytes 1572872 | tf_op jit(solution)/shard_map/ppermute | solution.py:36
  33.5 3.6 %collective-permute-start.4 = (f32[768,128]{1,0:T(8,128)S(1)}, f32[768,128]{1,0:T(8,128)S(1)}, u32[]{:S(2)}, u32[]{:S(2)}) collective-permute-start(f32[768,128]{1,0:T(8,128)S(1)} %get-tuple-element.96), channel_id=1, source_target_pairs={{0,1},{1,0},{2,3},{3,2},{4,5},{5,4},{6,7},{7,6},{8,9},{9,8},{10,11... | collective-permute-start | bytes 1179656 | tf_op jit(solution)/shard_map/ppermute | solution.py:36
  37.9 26.8 %all-to-all-start = ((f32[32,24,128]{2,1,0:T(8,128)}), f32[32,24,128]{2,1,0:T(8,128)S(1)}, u32[]{:S(2)}, u32[]{:S(2)}) async-start(f32[32,24,128]{2,1,0:T(8,128)} %bitcast.1), calls=%async_computation | async-start | bytes 786432 | tf_op jit(solution)/shard_map/all_to_all | solution.py:55
  54.2 23.7 %collective-permute-start.6 = (f32[128,512]{1,0:T(8,128)S(1)}, f32[128,512]{1,0:T(8,128)S(1)}, u32[]{:S(2)}, u32[]{:S(2)}) collective-permute-start(f32[128,512]{1,0:T(8,128)S(1)} %get-tuple-element.93.out_i), channel_id=1, source_target_pairs={{0,1},{1,0},{2,3},{3,2},{4,5},{5,4},{6,7},{7,6},{8,9},{9,8},{10,11... | collective-permute-start | bytes 786440 | tf_op jit(solution)/shard_map/ppermute | solution.py:36
  56.6 21.3 %collective-permute-start.5 = (f32[128,512]{1,0:T(8,128)S(1)}, f32[128,512]{1,0:T(8,128)S(1)}, u32[]{:S(2)}, u32[]{:S(2)}) collective-permute-start(f32[128,512]{1,0:T(8,128)S(1)} %get-tuple-element.94.out_e), channel_id=1, source_target_pairs={{1,2},{3,4},{5,6},{7,8},{9,10},{11,12},{13,14},{15,16},{17,18},{19... | collective-permute-start | bytes 786440 | tf_op jit(solution)/shard_map/ppermute | solution.py:41
  93.5 7.4 %collective-permute-start.7 = (f32[768,128]{1,0:T(8,128)S(1)}, f32[768,128]{1,0:T(8,128)S(1)}, u32[]{:S(2)}, u32[]{:S(2)}) collective-permute-start(f32[768,128]{1,0:T(8,128)S(1)} %bitcast.4), channel_id=1, source_target_pairs={{0,1},{1,0},{2,3},{3,2},{4,5},{5,4},{6,7},{7,6},{8,9},{9,8},{10,11... | collective-permute-start | bytes 1179656 | tf_op jit(solution)/shard_map/ppermute | solution.py:36
